TPU v7x, 32 devices: a whole 2x2x4 slice. The times are simulated.
32 devices in a mesh: dp: 8 (over z, y), tensor: 4 (over x, core).
Axes of the slice: x: 2, y: 2, z: 4, core: 2. Of those that a mesh axis runs over, the one named last changes fastest.
Arguments:
- tokens_in: bfloat16 [16384, 768], P('dp'), may hold values from -6 to 6
- box_coords: int32 [16384, 4], P('dp'), may hold values from 0 to 999
- rel_x: int32 [32, 512, 512], P('dp'), may hold values from 0 to 31
- rel_y: int32 [32, 512, 512], P('dp'), may hold values from 0 to 31
- mask_tokens: int32 [16384], P('dp'), may hold values from 0 to 1, as said below
- cotangent: bfloat16 [16384, 768], P('dp'), may hold values from -14336 to 14336
- layout_weight: bfloat16 [512, 768], replicated, may hold values from -0.25 to 0.25
- qkv_weight: bfloat16 [3, 768, 768], P(None, None, 'tensor'), may hold values from -0.21875 to 0.21875
- qv_bias: float32 [2, 768], P(None, 'tensor'), may hold values from -4 to 4
- bias_table: bfloat16 [64, 12], P(None, 'tensor'), may hold values from -6 to 6
- out_weight: bfloat16 [768, 768], P('tensor'), may hold values from -1.75 to 1.75
- out_bias: float32 [768], replicated, may hold values from -4 to 4
- ln1_gain: float32 [768], replicated, may hold values from 0.1 to 1.9
- ln1_bias: float32 [768], replicated, may hold values from -4 to 4
- ffn_in_weight: bfloat16 [768, 3072], P(None, 'tensor'), may hold values from -0.21875 to 0.21875
- ffn_in_bias: float32 [3072], P('tensor'), may hold values from -4 to 4
- ffn_out_weight: bfloat16 [3072, 768], P('tensor'), may hold values from -0.109375 to 0.109375
- ffn_out_bias: float32 [768], replicated, may hold values from -4 to 4
- ln2_gain: float32 [768], replicated, may hold values from 0.1 to 1.9
- ln2_bias: float32 [768], replicated, may hold values from -4 to 4
- group_rates: float32 [8], replicated, may hold values from 0.005 to 0.05
Outputs:
- block_out: bfloat16 [16384, 768], P('dp')
- input_grad: float32 [16384, 768], P('dp')
- layout_update: float32 [512, 768], replicated
- qkv_update: float32 [3, 768, 768], P(None, None, 'tensor')
- qv_bias_update: float32 [2, 768], P(None, 'tensor')
- table_update: float32 [64, 12], P(None, 'tensor')
- out_update: float32 [768, 768], P('tensor')
- out_bias_update: float32 [768], replicated
- ln1_gain_update: float32 [768], replicated
- ln1_bias_update: float32 [768], replicated
- ffn_in_update: float32 [768, 3072], P(None, 'tensor')
- ffn_in_bias_update: float32 [3072], P('tensor')
- ffn_out_update: float32 [3072, 768], P('tensor')
- ffn_out_bias_update: float32 [768], replicated
- ln2_gain_update: float32 [768], replicated
- ln2_bias_update: float32 [768], replicated
Inputs may be any that keep to these rules, and one draw needn't show every extreme that they name: `mask_tokens`: each window of 512 tokens has at least one masked token.
All inputs are finite; a program needn't handle non-finite values.
Results may differ from a plain program's by a relative error of at most 0.018.
The roundings to bfloat16 on the way count: a program that leaves them out, or rounds other values in their place, can miss the bound.
Values may be sent and summed in bfloat16 or wider, within the bound.
A program may use at most 192 MiB of HBM per device.

v0:
```python
import math

import jax
import jax.numpy as jnp
from jax import lax
from jax.sharding import PartitionSpec as P

HD = 64
LFREQ = 64


EPSILON = 1e-05


def layout_features(box_coords):
    freq_index = jnp.arange(LFREQ).astype(jnp.float32)
    frequency = jnp.exp(freq_index * (-math.log(1000.0) / LFREQ))
    angles = box_coords.astype(jnp.float32)[:, :, None] * frequency[None, None, :]
    waves = jnp.concatenate([jnp.sin(angles), jnp.cos(angles)], axis=2)
    return waves.reshape(box_coords.shape[0], 8 * LFREQ)


def normalize_keep(values_in, gain_vec, shift_vec):
    row_mean = jnp.mean(values_in, axis=-1, keepdims=True)
    centered = values_in - row_mean
    inverse = lax.rsqrt(jnp.mean(centered * centered, axis=-1, keepdims=True) + EPSILON)
    unit_rows = centered * inverse
    return (unit_rows * gain_vec + shift_vec, unit_rows, inverse)


def normalize_back(upstream, unit_rows, inverse, gain_vec):
    scaled = upstream * gain_vec
    mean_one = jnp.mean(scaled, axis=-1, keepdims=True)
    mean_two = jnp.mean(scaled * unit_rows, axis=-1, keepdims=True)
    return (
        (scaled - mean_one - unit_rows * mean_two) * inverse,
        jnp.sum(upstream * unit_rows, axis=0),
        jnp.sum(upstream, axis=0),
    )


def position_bias(rel_x, rel_y, bias_table):
    buckets = bias_table.shape[0] // 2
    levels = jnp.arange(buckets, dtype=jnp.int32)
    onehot_x = (rel_x[:, :, None] == levels[None, None, :]).astype(jnp.bfloat16)
    onehot_y = (rel_y[:, :, None] == levels[None, None, :]).astype(jnp.bfloat16)
    pos_bias = jnp.einsum(
        "ijb,bh->hij", onehot_x, bias_table[:buckets], preferred_element_type=jnp.float32
    ) + jnp.einsum(
        "ijb,bh->hij", onehot_y, bias_table[buckets:], preferred_element_type=jnp.float32
    )
    return (onehot_x, onehot_y, pos_bias)


def window_scores(queries, key_rows, rel_x, rel_y, bias_table, score_scale):
    onehot_x, onehot_y, pos_bias = position_bias(rel_x, rel_y, bias_table)
    scores = (
        jnp.einsum("ihd,jhd->hij", queries, key_rows, preferred_element_type=jnp.float32)
        * score_scale
        + pos_bias
    )
    return (onehot_x, onehot_y, scores)


def attend_window(queries, key_rows, values, rel_x, rel_y, bias_table, score_scale):
    onehot_x, onehot_y, scores = window_scores(
        queries, key_rows, rel_x, rel_y, bias_table, score_scale
    )
    row_max = jnp.max(scores, axis=-1, keepdims=True)
    log_total = jnp.log(jnp.sum(jnp.exp(scores - row_max), axis=-1, keepdims=True)) + row_max
    attn_probs = jnp.exp(scores - log_total)
    attended = jnp.einsum(
        "hij,jhd->ihd", attn_probs.astype(jnp.bfloat16), values, preferred_element_type=jnp.float32
    )
    return (attended.astype(jnp.bfloat16), log_total)


def attend_back(
    queries, key_rows, values, rel_x, rel_y, log_total, dcontext, bias_table, score_scale
):
    onehot_x, onehot_y, scores = window_scores(
        queries, key_rows, rel_x, rel_y, bias_table, score_scale
    )
    attn_probs = jnp.exp(scores - log_total)
    dprobs = jnp.einsum("ihd,jhd->hij", dcontext, values, preferred_element_type=jnp.float32)
    dvalues = jnp.einsum(
        "hij,ihd->jhd",
        attn_probs.astype(jnp.bfloat16),
        dcontext,
        preferred_element_type=jnp.float32,
    )
    row_dot = jnp.sum(attn_probs * dprobs, axis=-1, keepdims=True)
    dscores = (attn_probs * (dprobs - row_dot)).astype(jnp.bfloat16)
    dqueries = (
        jnp.einsum("hij,jhd->ihd", dscores, key_rows, preferred_element_type=jnp.float32)
        * score_scale
    )
    dkey_rows = (
        jnp.einsum("hij,ihd->jhd", dscores, queries, preferred_element_type=jnp.float32)
        * score_scale
    )
    dtable = jnp.concatenate(
        [
            jnp.einsum("ijb,hij->bh", onehot_x, dscores, preferred_element_type=jnp.float32),
            jnp.einsum("ijb,hij->bh", onehot_y, dscores, preferred_element_type=jnp.float32),
        ],
        axis=0,
    )
    return (dqueries, dkey_rows, dvalues, dtable)


def local(
    tokens_in,
    box_coords,
    rel_x,
    rel_y,
    mask_tokens,
    cotangent,
    layout_weight,
    qkv_weight,
    qv_bias,
    bias_table,
    out_weight,
    out_bias,
    ln1_gain,
    ln1_bias,
    ffn_in_weight,
    ffn_in_bias,
    ffn_out_weight,
    ffn_out_bias,
    ln2_gain,
    ln2_bias,
    group_rates,
):
    tok_rows = tokens_in.shape[0]
    windows = rel_x.shape[0]
    win_len = rel_x.shape[1]
    local_heads = bias_table.shape[1]
    score_scale = HD ** (-0.5)
    features = layout_features(box_coords).astype(jnp.bfloat16)
    layer_in = tokens_in.astype(jnp.float32) + jnp.dot(
        features, layout_weight, preferred_element_type=jnp.float32
    )
    layer_low = layer_in.astype(jnp.bfloat16)
    projected = jnp.einsum("td,jdc->jtc", layer_low, qkv_weight, preferred_element_type=jnp.float32)
    queries = (projected[0] + qv_bias[0]).astype(jnp.bfloat16)
    key_rows = projected[1].astype(jnp.bfloat16)
    values = (projected[2] + qv_bias[1]).astype(jnp.bfloat16)
    split_shape = (windows, win_len, local_heads, HD)
    query_blocks = queries.reshape(split_shape)
    key_blocks = key_rows.reshape(split_shape)
    value_blocks = values.reshape(split_shape)

    def forward_window(pieces):
        return attend_window(
            pieces[0], pieces[1], pieces[2], pieces[3], pieces[4], bias_table, score_scale
        )

    attended, log_total = lax.map(
        forward_window, (query_blocks, key_blocks, value_blocks, rel_x, rel_y)
    )
    context = attended.reshape(tok_rows, local_heads * HD)
    attn_part = jnp.dot(context, out_weight, preferred_element_type=jnp.float32)
    residual = layer_in + lax.psum(attn_part, "tensor") + out_bias
    normed, unit_one, inverse_one = normalize_keep(residual, ln1_gain, ln1_bias)
    normed_low = normed.astype(jnp.bfloat16)
    pre_act = jnp.dot(normed_low, ffn_in_weight, preferred_element_type=jnp.float32) + ffn_in_bias
    activated, gelu_back = jax.vjp(jax.nn.gelu, pre_act)
    hidden = activated.astype(jnp.bfloat16)
    ffn_part = jnp.dot(hidden, ffn_out_weight, preferred_element_type=jnp.float32)
    local_count = jnp.sum(mask_tokens.astype(jnp.float32))
    masked_count = lax.psum(local_count, "dp")
    residual_two = normed + lax.psum(ffn_part, "tensor") + ffn_out_bias
    output, unit_two, inverse_two = normalize_keep(residual_two, ln2_gain, ln2_bias)
    output_low = output.astype(jnp.bfloat16)
    selected = mask_tokens.astype(jnp.float32)[:, None] * cotangent.astype(jnp.float32)
    dresid_two, grad_g2, grad_b2 = normalize_back(selected, unit_two, inverse_two, ln2_gain)
    dffn_low = dresid_two.astype(jnp.bfloat16)
    grad_c2 = jnp.sum(dresid_two, axis=0)
    grad_w2 = jnp.einsum("tf,td->fd", hidden, dffn_low, preferred_element_type=jnp.float32)
    dhidden = jnp.einsum("td,fd->tf", dffn_low, ffn_out_weight, preferred_element_type=jnp.float32)
    dpre_act = gelu_back(dhidden)[0].astype(jnp.bfloat16)
    grad_c1 = jnp.sum(dpre_act, axis=0, dtype=jnp.float32)
    grad_w1 = jnp.einsum("td,tf->df", normed_low, dpre_act, preferred_element_type=jnp.float32)
    dnormed_part = jnp.einsum(
        "tf,df->td", dpre_act, ffn_in_weight, preferred_element_type=jnp.float32
    )
    dnormed = dresid_two + lax.psum(dnormed_part, "tensor")
    dresidual, grad_g1, grad_b1 = normalize_back(dnormed, unit_one, inverse_one, ln1_gain)
    grad_ob = jnp.sum(dresidual, axis=0)
    dattn_low = dresidual.astype(jnp.bfloat16)
    grad_ow = jnp.einsum("tc,td->cd", context, dattn_low, preferred_element_type=jnp.float32)
    dcontext = jnp.einsum(
        "td,cd->tc", dattn_low, out_weight, preferred_element_type=jnp.float32
    ).astype(jnp.bfloat16)

    def backward_window(pieces):
        return attend_back(
            pieces[0],
            pieces[1],
            pieces[2],
            pieces[3],
            pieces[4],
            pieces[5],
            pieces[6],
            bias_table,
            score_scale,
        )

    dqueries, dkey_rows, dvalues, tables = lax.map(
        backward_window,
        (
            query_blocks,
            key_blocks,
            value_blocks,
            rel_x,
            rel_y,
            log_total,
            dcontext.reshape(split_shape),
        ),
    )
    grad_table = jnp.sum(tables, axis=0)
    dprojected = jnp.stack(
        [
            dqueries.reshape(tok_rows, local_heads * HD),
            dkey_rows.reshape(tok_rows, local_heads * HD),
            dvalues.reshape(tok_rows, local_heads * HD),
        ]
    ).astype(jnp.bfloat16)
    grad_qkv = jnp.einsum("td,jtc->jdc", layer_low, dprojected, preferred_element_type=jnp.float32)
    grad_qvb = jnp.stack(
        [
            jnp.sum(dprojected[0], axis=0, dtype=jnp.float32),
            jnp.sum(dprojected[2], axis=0, dtype=jnp.float32),
        ]
    )
    dlayer_part = jnp.einsum(
        "jtc,jdc->td", dprojected, qkv_weight, preferred_element_type=jnp.float32
    )
    dlayer = dresidual + lax.psum(dlayer_part, "tensor")
    grad_lay = jnp.einsum(
        "tf,td->fd", features, dlayer.astype(jnp.bfloat16), preferred_element_type=jnp.float32
    )
    summed = lax.psum(
        (
            grad_lay,
            grad_qkv,
            grad_qvb,
            grad_table,
            grad_ow,
            grad_ob,
            grad_g1,
            grad_b1,
            grad_w1,
            grad_c1,
            grad_w2,
            grad_c2,
            grad_g2,
            grad_b2,
        ),
        "dp",
    )
    factor = group_rates / masked_count
    return (
        output_low,
        dlayer / masked_count,
        summed[0] * factor[6],
        summed[1] * factor[0],
        summed[2] * factor[0],
        summed[3] * factor[7],
        summed[4] * factor[1],
        summed[5] * factor[1],
        summed[6] * factor[2],
        summed[7] * factor[2],
        summed[8] * factor[3],
        summed[9] * factor[3],
        summed[10] * factor[4],
        summed[11] * factor[4],
        summed[12] * factor[5],
        summed[13] * factor[5],
    )


def solution(mesh):
    placed = (
        P("dp", None),
        P("dp", None),
        P("dp", None, None),
        P("dp", None, None),
        P("dp"),
        P("dp", None),
        P(),
        P(None, None, "tensor"),
        P(None, "tensor"),
        P(None, "tensor"),
        P("tensor", None),
        P(),
        P(),
        P(),
        P(None, "tensor"),
        P("tensor"),
        P("tensor", None),
        P(),
        P(),
        P(),
        P(),
    )
    return jax.shard_map(
        local,
        mesh=mesh,
        in_specs=placed,
        out_specs=(
            P("dp", None),
            P("dp", None),
            P(),
            P(None, None, "tensor"),
            P(None, "tensor"),
            P(None, "tensor"),
            P("tensor", None),
            P(),
            P(),
            P(),
            P(None, "tensor"),
            P("tensor"),
            P("tensor", None),
            P(),
            P(),
            P(),
        ),
        check_vma=False,
    )
```

profile of v0, /device:TPU:0, one launch (start us, length us, event | category | flops | bytes accessed | tf_op | source)
XLA Modules:
  0.0 1269.4 jit_solution(12648136825752969835)
XLA Ops:
  12.9 7.7 fusion.86
  38.6 125.3 %while.28 = (s32[]{:T(128)}, bf16[4,512,3,64]{1,3,2,0:T(8,128)(2,1)}, f32[4,3,512,1]{2,1,3,0:T(4,128)S(1)}, bf16[4,512,3,64]{1,3,2,0:T(8,128)(2,1)}, bf16[4,512,...) while((s32[]{:T(128)}, ...), condition=%wide.region_3.4_spmd, body=%wide.region_0.3_spmd.sunk | while | flops 325155328 | bytes 41741172 | solution.py:159
  40.5 6.4 fusion.173
  51.8 7.2 fusion.174
  71.8 6.4 fusion.173
  83.0 7.2 fusion.174
  103.1 6.4 fusion.173
  114.3 7.2 fusion.174
  134.3 6.4 fusion.173
  145.6 7.2 fusion.174
  170.2 122.2 %all-reduce.8.cloned.1.call-done = f32[2048,768]{0,1:T(8,128)} async-done(((f32[2048,768]{0,1:T(8,128)}), f32[2048,768]{0,1:T(8,128)}) %all-reduce.8.cloned.1.call-update) | async-done | bytes 6291472 | tf_op jit(solution)/shard_map/psum | solution.py:164
  292.3 7.4 fusion.111
  308.0 5.1 fusion.105
  318.5 114.6 %all-reduce.10.cloned.1.call-done = f32[2048,768]{0,1:T(8,128)} async-done(((f32[2048,768]{0,1:T(8,128)}), f32[2048,768]{0,1:T(8,128)}) %all-reduce.10.cloned.1.call-update) | async-done | bytes 6291472 | tf_op jit(solution)/shard_map/psum | solution.py:173
  433.1 5.6 fusion.110
  445.2 8.5 convert_reduce_fusion
  460.1 119.9 %all-reduce.12.cloned.1.call-done = f32[2048,768]{0,1:T(8,128)} async-done(((f32[2048,768]{0,1:T(8,128)}), f32[2048,768]{0,1:T(8,128)}) %all-reduce.12.cloned.1.call-update) | async-done | bytes 6291472 | tf_op jit(solution)/shard_map/psum | solution.py:188
  580.0 12.2 multiply_reduce_fusion.1
  602.2 224.1 %while.29 = (s32[]{:T(128)}, bf16[4,512,3,64]{1,3,2,0:T(8,128)(2,1)}, bf16[4,512,3,64]{1,3,2,0:T(8,128)(2,1)}, bf16[4,512,3,64]{1,3,2,0:T(8,128)(2,1)}, f32[4,64...) while((s32[]{:T(128)}, ...), condition=%wide.region_17.18_spmd, body=%wide.region_15.17_spmd.sunk | while | flops 746257088 | bytes 93301608 | solution.py:210
  607.1 6.5 fusion.190
  613.5 4.9 copy.151
  618.4 8.1 fusion.191
  646.3 6.6 fusion.196
  652.9 5.2 fusion.195
  662.9 6.5 fusion.190
  669.4 4.9 copy.151
  674.3 8.1 fusion.191
  702.2 6.6 fusion.196
  708.8 5.2 fusion.195
  718.8 6.5 fusion.190
  725.3 4.9 copy.151
  730.2 8.1 fusion.191
  758.1 6.6 fusion.196
  764.6 5.2 fusion.195
  774.7 6.5 fusion.190
  781.2 4.9 copy.151
  786.0 8.1 fusion.191
  814.0 6.6 fusion.196
  820.5 5.2 fusion.195
  835.2 5.8 convolution_bitcast_fusion
  841.4 7.0 fusion.119
  848.5 11.1 fusion.93
  865.8 95.2 %all-reduce.14.cloned.1.call-done = f32[2048,768]{0,1:T(8,128)} async-done(((f32[2048,768]{0,1:T(8,128)}), f32[2048,768]{0,1:T(8,128)}) %all-reduce.14.cloned.1.call-update) | async-done | bytes 6291472 | tf_op jit(solution)/shard_map/psum | solution.py:240
  961.0 7.6 fusion.83
  972.7 40.2 %all-reduce = (f32[]{:T(128)}, f32[2,192]{1,0:T(2,128)S(1)}, f32[64,3]{0,1:T(4,128)S(1)}, f32[768]{0:T(1024)S(1)}, f32[768]{0:T(1024)S(1)}, /*index=5*/f32[768]{...) all-reduce(f32[]{:T(128)} %convert_reduce_fusion.3, ...), channel_id=1, replica_groups=mesh['dp'=8,'tensor'=4] {'dp'}, use_global_device_ids=true, to_apply=%region_20.21 | all-reduce | flops 5953 | bytes 47624 | tf_op jit(solution)/shard_map/psum | solution.py:172
  1028.0 10.0 broadcast_divide_fusion
  1038.0 6.6 copy.124
  1044.5 205.3 %all-reduce.16.cloned.1.call-done = (f32[512,768]{1,0:T(8,128)}, f32[3,768,192]{1,2,0:T(8,128)}, f32[192,768]{1,0:T(8,128)}, f32[768,768]{1,0:T(8,128)}, f32[768,768]{1,0:T(8,128)}) async-done(((f32[512,768]{1,0:T(8,128)}, f32[3,768,192]{1,2,0:T(8,128)}, f32[192,768]{1,0:T(8,128)}, f32[768,768]{1,0:T(8,128)}, f32[768,768]{1,0:T(8,128)}), (f32[512,768]{1,0:T(8,128)}, f32[3,768,192]{1,2,0:T(8,128)}, ...) | async-done | bytes 8650768 | tf_op jit(solution)/shard_map/psum | solution.py:244
  (357 shorter events, 281.9 us)
Async XLA Ops:
  7.2 300.8 %copy-start = (bf16[768,768]{1,0:T(8,128)(2,1)S(1)}, bf16[768,768]{1,0:T(8,128)(2,1)}, u32[]{:S(2)}) copy-start(bf16[768,768]{1,0:T(8,128)(2,1)} %param.41) | copy-start | bytes 3538948
  7.2 285.1 %all-reduce.8.cloned.1.call-start = ((), (), s32[]{:S(2)}) async-start(), calls=%async_computation | async-start | bytes 12582912 | tf_op jit(solution)/shard_map/psum | solution.py:164
  8.1 14.1 %copy-start.28 = (bf16[512,768]{1,0:T(8,128)(2,1)S(1)}, bf16[512,768]{1,0:T(8,128)(2,1)}, u32[]{:S(2)}) copy-start(bf16[512,768]{1,0:T(8,128)(2,1)} %param.31) | copy-start | bytes 2359300
  30.6 8.0 copy-start.66
  31.2 7.4 copy-start.42
  38.6 127.5 %copy-start.26 = (bf16[192,768]{1,0:T(8,128)(2,1)S(1)}, bf16[192,768]{1,0:T(8,128)(2,1)}, u32[]{:S(2)}) copy-start(bf16[192,768]{1,0:T(8,128)(2,1)} %param.35) | copy-start | bytes 884740
  163.9 6.0 copy-start.16
  166.1 126.2 %copy-start.60 = (f32[768]{0:T(1024)S(1)}, f32[768]{0:T(1024)}, u32[]{:S(2)}) copy-start(f32[768]{0:T(1024)} %param.36) | copy-start | bytes 9220
  169.9 263.2 %all-reduce.10.cloned.1.call-start = ((), (), s32[]{:S(2)}) async-start(), calls=%async_computation.1 | async-start | bytes 12582912 | tf_op jit(solution)/shard_map/psum | solution.py:173
  313.2 120.0 %copy-start.61 = (f32[768]{0:T(1024)S(1)}, f32[768]{0:T(1024)}, u32[]{:S(2)}) copy-start(f32[768]{0:T(1024)} %param.42) | copy-start | bytes 9220
  313.2 266.7 %all-reduce.12.cloned.1.call-start = ((), (), s32[]{:S(2)}) async-start(), calls=%async_computation.2 | async-start | bytes 12582912 | tf_op jit(solution)/shard_map/psum | solution.py:188
  313.9 266.0 %copy-start.37 = (f32[2048]{0:T(1024)}, f32[2048]{0:T(1024)S(1)}, u32[]{:S(2)}) copy-start(f32[2048]{0:T(1024)S(1)} %convert_element_type.106) | copy-start | bytes 24580
  438.7 6.4 copy-start.5
  438.8 141.1 %copy-start.35 = (f32[2048]{0:T(1024)}, f32[2048]{0:T(1024)S(1)}, u32[]{:S(2)}) copy-start(f32[2048]{0:T(1024)S(1)} %broadcast_multiply_fusion.9) | copy-start | bytes 24580
  438.8 6.3 slice-start.4
  442.9 137.0 %copy-start.39 = (f32[2048]{0:T(1024)}, f32[2048]{0:T(1024)S(1)}, u32[]{:S(2)}) copy-start(f32[2048]{0:T(1024)S(1)} %add_rsqrt_fusion) | copy-start | bytes 24580
  445.1 134.8 %copy-start.43 = (f32[2048]{0:T(1024)}, f32[2048]{0:T(1024)S(1)}, u32[]{:S(2)}) copy-start(f32[2048]{0:T(1024)S(1)} %broadcast_multiply_fusion.8) | copy-start | bytes 24580
  445.1 134.8 %copy-start.45 = (f32[2048]{0:T(1024)}, f32[2048]{0:T(1024)S(1)}, u32[]{:S(2)}) copy-start(f32[2048]{0:T(1024)S(1)} %broadcast_multiply_fusion.7) | copy-start | bytes 24580
  459.9 120.0 %copy-start.8 = (bf16[2048,768]{0,1:T(8,128)(2,1)S(1)}, bf16[2048,768]{0,1:T(8,128)(2,1)}, u32[]{:S(2)}) copy-start(bf16[2048,768]{0,1:T(8,128)(2,1)} %copy.114) | copy-start | bytes 9437188
  460.0 120.0 %copy-start.58 = (f32[768]{0:T(1024)S(1)}, f32[768]{0:T(1024)}, u32[]{:S(2)}) copy-start(f32[768]{0:T(1024)} %param.44) | copy-start | bytes 9220
  460.0 501.0 %all-reduce.14.cloned.1.call-start = ((), (), s32[]{:S(2)}) async-start(), calls=%async_computation.3 | async-start | bytes 12582912 | tf_op jit(solution)/shard_map/psum | solution.py:240
  646.3 6.6 copy-start.12
  702.2 6.6 copy-start.12
  758.1 6.6 copy-start.12
  814.0 6.6 copy-start.12
  828.6 12.5 copy-start.20
  833.5 7.5 copy-start.21
  841.1 7.3 copy-start.9
  841.1 7.3 copy-start.36
  841.1 7.3 copy-start.38
  841.1 7.3 copy-start.40
  841.1 7.3 copy-start.44
  841.1 7.3 copy-start.46
  841.1 7.3 copy-start.50
  841.2 7.3 copy-start.65
  841.2 408.6 %all-reduce.16.cloned.1.call-start = ((), (), s32[]{:S(2)}) async-start(), calls=%async_computation.4 | async-start | bytes 17301504 | tf_op jit(solution)/shard_map/psum | solution.py:244
  841.4 18.2 %slice-start = ((s8[6291456]{0:T(1024)(128)(4,1)}), s8[4194304]{0:T(1024)(128)(4,1)S(1)}, s32[]{:S(2)}) async-start(s8[6291456]{0:T(1024)(128)(4,1)} %bitcast.225), calls=%async_computation.5 | async-start | bytes 8388608
  841.4 20.2 %slice-start.2 = ((s8[6291456]{0:T(1024)(128)(4,1)}), s8[4194304]{0:T(1024)(128)(4,1)S(1)}, s32[]{:S(2)}) async-start(s8[6291456]{0:T(1024)(128)(4,1)} %bitcast.227), calls=%async_computation.7 | async-start | bytes 8388608
  848.5 11.1 slice-start.1
  848.5 11.1 copy-start.19
  848.5 13.1 %slice-start.3 = ((s8[6291456]{0:T(1024)(128)(4,1)}), s8[2097152]{0:T(1024)(128)(4,1)S(1)}, s32[]{:S(2)}) async-start(s8[6291456]{0:T(1024)(128)(4,1)} %bitcast.227), calls=%async_computation.8 | async-start | bytes 4194304
  862.4 98.6 %copy-start.15 = (bf16[2048,4,128]{0,2,1:T(8,128)(2,1)S(1)}, bf16[2048,4,128]{0,2,1:T(8,128)(2,1)}, u32[]{:S(2)}) copy-start(bf16[2048,4,128]{0,2,1:T(8,128)(2,1)} %copy-done.14) | copy-start | bytes 6291460
  968.7 44.2 %copy-start.17 = (bf16[2048,768]{0,1:T(8,128)(2,1)S(1)}, bf16[2048,768]{0,1:T(8,128)(2,1)}, u32[]{:S(2)}) copy-start(bf16[2048,768]{0,1:T(8,128)(2,1)} %get-tuple-element.346) | copy-start | bytes 9437188
  968.7 47.0 %copy-start.67 = (f32[8]{0:T(128)S(1)}, f32[8]{0:T(128)}, u32[]{:S(2)}) copy-start(f32[8]{0:T(128)} %param.45) | copy-start | bytes 100
  1249.8 6.5 copy-start.24
  1249.8 8.7 copy-start.23
  1252.8 8.0 copy-start.25
  1256.3 6.3 copy-start.1
  (54 other events, 132.3 us)
Sparse Core Ops, SparseCore 0:
  170.0 122.2 all-reduce.7
  313.3 119.7 all-reduce.9
  460.1 119.7 all-reduce.11
  841.2 119.7 all-reduce.13
  968.9 280.8 all-reduce.15
where the time goes:
time: 1280 us; the launch traced here: 1270 us
  waiting for transfers between devices  657 us (51%)
  matrix products  296 us (23%)
  local copies, waits for them, and re-layouts  168 us (13%)
  other arithmetic  90.7 us (7%)
  blocking collectives  40.2 us (3%)
  between operations  14.9 us (1%)
    psum x1, waiting for transfers between devices, local(): lax.psum((grad_lay, grad_qkv, grad_qvb, grad_table, grad_ow, grad_ob, gra...  205 us
    psum x1, waiting for transfers between devices, local(): residual = layer_in + lax.psum(attn_part, 'tensor') + out_bias  122 us
    psum x1, waiting for transfers between devices, local(): dnormed = dresid_two + lax.psum(dnormed_part, 'tensor')  120 us
    psum x1, waiting for transfers between devices, local(): residual_two = normed + lax.psum(ffn_part, 'tensor') + ffn_out_bias  115 us
    psum x1, waiting for transfers between devices, local(): dlayer = dresidual + lax.psum(dlayer_part, 'tensor')  95.2 us
    dot_general x8, matrix products, position_bias(): jnp.einsum('ijb,bh->hij', onehot_y, bias_table[buckets:], preferred_eleme...  61.2 us
    dot_general x8, matrix products, position_bias(): jnp.einsum('ijb,bh->hij', onehot_x, bias_table[:buckets], preferred_eleme...  51.6 us
    psum x1, blocking collectives, local(): masked_count = lax.psum(local_count, 'dp')  40.2 us
  transfers between devices with their start and end apart: 5, of which 5 were waited for; matrix products, arithmetic and copies ran while one was open for 5% of the time, Pallas kernels for 0%

commit v1 on v0

v1 whole, which is shorter than its diff:
```python
import functools
import math

import jax
import jax.numpy as jnp
from jax import lax
from jax.experimental import pallas as pl
from jax.experimental.pallas import tpu as pltpu
from jax.sharding import PartitionSpec as P

HD = 64
LFREQ = 64
BUCKETS = 32
EPSILON = 1e-05
ROWS = 16


def nt(a, b):
    return lax.dot_general(a, b, (((1,), (1,)), ((), ())), preferred_element_type=jnp.float32)


def nn(a, b):
    return jnp.dot(a, b, preferred_element_type=jnp.float32)


def layout_features(box_coords):
    freq_index = jnp.arange(LFREQ).astype(jnp.float32)
    frequency = jnp.exp(freq_index * (-math.log(1000.0) / LFREQ))
    angles = box_coords.astype(jnp.float32)[:, :, None] * frequency[None, None, :]
    waves = jnp.concatenate([jnp.sin(angles), jnp.cos(angles)], axis=2)
    return waves.reshape(box_coords.shape[0], 8 * LFREQ)


def normalize_keep(values_in, gain_vec, shift_vec):
    row_mean = jnp.mean(values_in, axis=-1, keepdims=True)
    centered = values_in - row_mean
    inverse = lax.rsqrt(jnp.mean(centered * centered, axis=-1, keepdims=True) + EPSILON)
    unit_rows = centered * inverse
    return (unit_rows * gain_vec + shift_vec, unit_rows, inverse)


def normalize_back(upstream, unit_rows, inverse, gain_vec):
    scaled = upstream * gain_vec
    mean_one = jnp.mean(scaled, axis=-1, keepdims=True)
    mean_two = jnp.mean(scaled * unit_rows, axis=-1, keepdims=True)
    return (
        (scaled - mean_one - unit_rows * mean_two) * inverse,
        jnp.sum(upstream * unit_rows, axis=0),
        jnp.sum(upstream, axis=0),
    )


def attend_kernel(q_ref, k_ref, v_ref, rx_ref, ry_ref, tab_ref, p_ref, c_ref):
    head = pl.program_id(0)
    win = rx_ref.shape[0]
    q = (q_ref[...].astype(jnp.float32).T * HD ** (-0.5)).astype(jnp.bfloat16)
    s = nn(q, k_ref[...])
    tab = jnp.broadcast_to(tab_ref[pl.ds(head, 1), :], (win, 128))
    parts = []
    for c in range(win // 128):
        sl = slice(128 * c, 128 * c + 128)
        bias_x = jnp.take_along_axis(tab, rx_ref[:, sl], axis=1)
        bias_y = jnp.take_along_axis(tab, ry_ref[:, sl] + BUCKETS, axis=1)
        parts.append(s[:, sl] + (bias_x + bias_y))
    s = jnp.concatenate(parts, axis=1)
    m = jnp.max(s, axis=1, keepdims=True)
    e = jnp.exp(s - m)
    p = e * (1.0 / jnp.sum(e, axis=1, keepdims=True))
    p_ref[0] = p
    c_ref[...] = nt(v_ref[...], p.astype(jnp.bfloat16)).astype(jnp.bfloat16)


def attend(q, k, v, rel_x, rel_y, tab):
    heads, win = tab.shape[0], rel_x.shape[0]
    blk = pl.BlockSpec((HD, win), lambda h: (h, 0))
    full = pl.BlockSpec((win, win), lambda h: (0, 0))
    return pl.pallas_call(
        attend_kernel,
        grid=(heads,),
        in_specs=[blk, blk, blk, full, full, pl.BlockSpec(tab.shape, lambda h: (0, 0))],
        out_specs=[pl.BlockSpec((1, win, win), lambda h: (h, 0, 0)), blk],
        out_shape=[
            jax.ShapeDtypeStruct((heads, win, win), jnp.float32),
            jax.ShapeDtypeStruct((heads * HD, win), jnp.bfloat16),
        ],
        compiler_params=pltpu.CompilerParams(vmem_limit_bytes=48 * 2**20),
        cost_estimate=pl.CostEstimate(
            flops=16 * 10**9, bytes_accessed=20 * 10**6, transcendentals=heads * win * win
        ),
        name="attend",
    )(q, k, v, rel_x, rel_y, tab)


def attend_back_kernel(
    q_ref, k_ref, v_ref, p_ref, dc_ref, rx_ref, ry_ref,
    dq_ref, dk_ref, dv_ref, g_ref, ds_scr, hot_scr, acc,
):
    head = pl.program_id(0)
    heads = pl.num_programs(0)
    win = rx_ref.shape[0]
    dc_t = dc_ref[...]
    dc = dc_t.astype(jnp.float32).T.astype(jnp.bfloat16)
    p = p_ref[0]
    dp = nn(dc, v_ref[...])
    row_dot = jnp.sum(p * dp, axis=1, keepdims=True)
    ds = (p * (dp - row_dot)).astype(jnp.bfloat16)
    dv_ref[...] = nn(dc_t, p.astype(jnp.bfloat16)).astype(jnp.bfloat16)
    dq_ref[...] = (nt(k_ref[...], ds) * HD ** (-0.5)).astype(jnp.bfloat16)
    dk_ref[...] = (nn(q_ref[...], ds) * HD ** (-0.5)).astype(jnp.bfloat16)
    ds_scr[head] = ds

    @pl.when(head == heads - 1)
    def _():
        acc[...] = jnp.zeros_like(acc)
        one, zero = jnp.bfloat16(1), jnp.bfloat16(0)
        half = BUCKETS * ROWS

        def step(g, carry):
            rows = pl.ds(pl.multiple_of(g * ROWS, ROWS), ROWS)
            x = rx_ref[rows, :].astype(jnp.float32).astype(jnp.bfloat16)
            y = ry_ref[rows, :].astype(jnp.float32).astype(jnp.bfloat16)
            for b in range(BUCKETS):
                hot_scr[b * ROWS : (b + 1) * ROWS, :] = jnp.where(x == jnp.bfloat16(b), one, zero)
                hot_scr[half + b * ROWS : half + (b + 1) * ROWS, :] = jnp.where(
                    y == jnp.bfloat16(b), one, zero
                )
            left = ds_scr[:, rows, :].reshape(ds_scr.shape[0] * ROWS, win)
            acc[...] += nt(left, hot_scr[...])
            return carry

        lax.fori_loop(0, win // ROWS, step, 0)
        row = lax.broadcasted_iota(jnp.int32, (ROWS, 2 * half), 0)
        col = lax.broadcasted_iota(jnp.int32, (ROWS, 2 * half), 1) % ROWS
        for h in range(ds_scr.shape[0]):
            part = jnp.where(row == col, acc[h * ROWS : (h + 1) * ROWS, :], 0.0)
            g_ref[h : h + 1, :] = jnp.sum(part, axis=0, keepdims=True)


def attend_back(q, k, v, p, dc, rel_x, rel_y):
    heads, win = p.shape[0], rel_x.shape[0]
    hots = 2 * BUCKETS * ROWS
    blk = pl.BlockSpec((HD, win), lambda h: (h, 0))
    full = pl.BlockSpec((win, win), lambda h: (0, 0))
    dq, dk, dv, g = pl.pallas_call(
        attend_back_kernel,
        grid=(heads,),
        in_specs=[blk, blk, blk, pl.BlockSpec((1, win, win), lambda h: (h, 0, 0)), blk, full, full],
        out_specs=[blk, blk, blk, pl.BlockSpec((heads, hots), lambda h: (0, 0))],
        out_shape=[jax.ShapeDtypeStruct((heads * HD, win), jnp.bfloat16)] * 3
        + [jax.ShapeDtypeStruct((heads, hots), jnp.float32)],
        scratch_shapes=[
            pltpu.VMEM((heads, win, win), jnp.bfloat16),
            pltpu.VMEM((hots, win), jnp.bfloat16),
            pltpu.VMEM((heads * ROWS, hots), jnp.float32),
        ],
        compiler_params=pltpu.CompilerParams(vmem_limit_bytes=56 * 2**20),
        cost_estimate=pl.CostEstimate(
            flops=20 * 10**9, bytes_accessed=20 * 10**6, transcendentals=0
        ),
        name="attend_back",
    )(q, k, v, p, dc, rel_x, rel_y)
    return dq, dk, dv, jnp.sum(g.reshape(heads, 2 * BUCKETS, ROWS), axis=2).T


def bits_of(size):
    return [1 << b for b in range(size.bit_length() - 1)]


def swap(value, axis, size, bit):
    return lax.ppermute(value, axis, [(i, i ^ bit) for i in range(size)])


def gather_pieces(own, axis, size):
    pieces = {0: own}
    for bit in reversed(bits_of(size)):
        for r in list(pieces):
            pieces[r | bit] = swap(pieces[r], axis, size, bit)
    return [pieces[r] for r in range(size)]


def scatter_pieces(pieces, axis, size):
    pieces = dict(enumerate(pieces))
    for bit in bits_of(size):
        for r in [r for r in pieces if r & bit]:
            got = swap(pieces.pop(r).astype(jnp.bfloat16), axis, size, bit)
            pieces[r ^ bit] = pieces[r ^ bit].astype(jnp.float32) + got.astype(jnp.float32)
    return pieces[0]


def reduce_rows(total, axis, size):
    me = lax.axis_index(axis)
    held = total
    for bit in bits_of(size):
        half = held.shape[0] // 2
        side = (me // bit) % 2
        mine = lax.dynamic_slice_in_dim(held, side * half, half)
        other = lax.dynamic_slice_in_dim(held, (1 - side) * half, half)
        got = swap(other.astype(jnp.bfloat16), axis, size, bit)
        held = mine.astype(jnp.float32) + got.astype(jnp.float32)
    held = held.astype(jnp.bfloat16)
    for bit in reversed(bits_of(size)):
        got = swap(held, axis, size, bit)
        side = (me // bit) % 2
        held = jnp.where(
            side == 0, jnp.concatenate([held, got]), jnp.concatenate([got, held])
        )
    return held


def sum_small(value, axis, size):
    for bit in bits_of(size):
        value = value + swap(value, axis, size, bit)
    return value


def place_pieces(pieces, me):
    size, rows = len(pieces), pieces[0].shape[0]
    whole = jnp.zeros((size * rows,) + pieces[0].shape[1:], pieces[0].dtype)
    for r, piece in enumerate(pieces):
        whole = lax.dynamic_update_slice_in_dim(whole, piece, (me ^ r) * rows, 0)
    return whole


def local(
    n_dp, n_t,
    tokens_in, box_coords, rel_x, rel_y, mask_tokens, cotangent, layout_weight, qkv_weight, qv_bias,
    bias_table, out_weight, out_bias, ln1_gain, ln1_bias, ffn_in_weight, ffn_in_bias, ffn_out_weight,
    ffn_out_bias, ln2_gain, ln2_bias, group_rates,
):
    me = lax.axis_index("tensor")
    win = rel_x.shape[1]
    model = tokens_in.shape[1]
    heads_t = bias_table.shape[1]
    cols_t = heads_t * HD
    hid_t = ffn_in_weight.shape[1]
    tok_rows = tokens_in.shape[0] // n_t

    def mine(whole):
        return lax.dynamic_slice_in_dim(whole, me * (whole.shape[0] // n_t), whole.shape[0] // n_t)

    qkv_rows = jnp.transpose(qkv_weight, (0, 2, 1))
    small_own = jnp.concatenate(
        [qv_bias.reshape(-1), ffn_in_bias, bias_table.T.astype(jnp.float32).reshape(-1)]
    )
    small_all = gather_pieces(small_own, "tensor", n_t)
    qkv_all = gather_pieces(qkv_rows, "tensor", n_t)
    rest_all = gather_pieces(
        jnp.concatenate([out_weight, ffn_in_weight.T, ffn_out_weight], axis=0), "tensor", n_t
    )
    wqkv = [jnp.concatenate([piece[n] for piece in qkv_all], axis=0) for n in range(3)]
    wo = jnp.concatenate([piece[:cols_t] for piece in rest_all], axis=0)
    w1 = jnp.concatenate([piece[cols_t : cols_t + hid_t] for piece in rest_all], axis=0)
    w2 = jnp.concatenate([piece[cols_t + hid_t :] for piece in rest_all], axis=0)
    bq = jnp.concatenate([piece[:cols_t] for piece in small_all])
    bv = jnp.concatenate([piece[cols_t : 2 * cols_t] for piece in small_all])
    b1 = jnp.concatenate([piece[2 * cols_t : 2 * cols_t + hid_t] for piece in small_all])
    table = jnp.concatenate(
        [piece[2 * cols_t + hid_t :].reshape(heads_t, 2 * BUCKETS) for piece in small_all]
    )
    table = jnp.pad(table, ((0, 0), (0, 128 - 2 * BUCKETS)))

    count = sum_small(jnp.sum(mask_tokens.astype(jnp.float32)).reshape(1), "dp", n_dp)[0]

    features = layout_features(mine(box_coords)).astype(jnp.bfloat16)
    layer_in = mine(tokens_in).astype(jnp.float32) + nn(features, layout_weight)
    layer_low = layer_in.astype(jnp.bfloat16)
    queries = (nt(wqkv[0], layer_low) + bq[:, None]).astype(jnp.bfloat16)
    key_rows = nt(wqkv[1], layer_low).astype(jnp.bfloat16)
    values = (nt(wqkv[2], layer_low) + bv[:, None]).astype(jnp.bfloat16)
    relx, rely = mine(rel_x)[0], mine(rel_y)[0]
    probs, context_t = attend(queries, key_rows, values, relx, rely, table)
    context = context_t.T
    residual = layer_in + nn(context, wo) + out_bias
    normed, unit_one, inverse_one = normalize_keep(residual, ln1_gain, ln1_bias)
    normed_low = normed.astype(jnp.bfloat16)
    pre_act = nt(normed_low, w1) + b1
    activated, gelu_back = jax.vjp(jax.nn.gelu, pre_act)
    hidden = activated.astype(jnp.bfloat16)
    residual_two = normed + nn(hidden, w2) + ffn_out_bias
    output, unit_two, inverse_two = normalize_keep(residual_two, ln2_gain, ln2_bias)
    block_out = lax.all_gather(output.astype(jnp.bfloat16), "tensor", axis=0, tiled=True)

    selected = mine(mask_tokens).astype(jnp.float32)[:, None] * mine(cotangent).astype(jnp.float32)
    dresid_two, grad_g2, grad_b2 = normalize_back(selected, unit_two, inverse_two, ln2_gain)
    dffn_low = dresid_two.astype(jnp.bfloat16)
    grad_c2 = jnp.sum(dresid_two, axis=0)
    grad_w2 = nn(hidden.T, dffn_low)
    dpre_act = gelu_back(nt(dffn_low, w2))[0].astype(jnp.bfloat16)
    grad_c1 = jnp.sum(dpre_act, axis=0, dtype=jnp.float32)
    grad_w1 = nn(dpre_act.T, normed_low)
    dnormed = dresid_two + nn(dpre_act, w1)
    dresidual, grad_g1, grad_b1 = normalize_back(dnormed, unit_one, inverse_one, ln1_gain)

    def reduced(parts):
        pieces = [
            jnp.concatenate([part[r * rows : (r + 1) * rows] for part, rows in parts], axis=0)
            for r in range(n_t)
        ]
        return reduce_rows(scatter_pieces(pieces, "tensor", n_t), "dp", n_dp)

    w2_sum = reduced([(grad_w2, hid_t)])
    w1_sum = reduced([(grad_w1, hid_t)])

    grad_ob = jnp.sum(dresidual, axis=0)
    dattn_low = dresidual.astype(jnp.bfloat16)
    grad_ow = nn(context_t, dattn_low)
    dcontext = nt(wo, dattn_low).astype(jnp.bfloat16)
    dq, dk, dv, grad_table = attend_back(
        queries, key_rows, values, probs, dcontext, relx, rely
    )
    grad_qkv = [nn(d, layer_low) for d in (dq, dk, dv)]
    grad_bq = jnp.sum(dq, axis=1, dtype=jnp.float32)
    grad_bv = jnp.sum(dv, axis=1, dtype=jnp.float32)
    dlayer = dresidual + sum(nn(d.T, w) for d, w in zip((dq, dk, dv), wqkv))
    grad_lay = nn(features.T, dlayer.astype(jnp.bfloat16))
    lay_rows = grad_lay.shape[0] // n_t
    lay_pieces = [
        lax.dynamic_slice_in_dim(grad_lay, (me ^ r) * lay_rows, lay_rows) for r in range(n_t)
    ]
    rest_sum = reduced(
        [(g, cols_t) for g in grad_qkv]
        + [(grad_ow, cols_t), (jnp.concatenate(lay_pieces, axis=0), lay_rows)]
    )
    din = (dlayer / count).astype(jnp.bfloat16)
    input_grad = place_pieces(gather_pieces(din, "tensor", n_t), me).astype(jnp.float32)
    lay_sum = place_pieces(gather_pieces(rest_sum[4 * cols_t :], "tensor", n_t), me)

    def pieces_of(vec, size):
        return vec.reshape(n_t, size)

    split = jnp.concatenate(
        [
            pieces_of(grad_bq, cols_t),
            pieces_of(grad_bv, cols_t),
            pieces_of(grad_c1, hid_t),
            pieces_of(grad_table.T, heads_t * 2 * BUCKETS),
        ],
        axis=1,
    )
    common = jnp.concatenate([grad_ob, grad_g1, grad_b1, grad_c2, grad_g2, grad_b2])
    whole = jnp.zeros_like(split)
    for r in range(n_t):
        whole = lax.dynamic_update_slice_in_dim(whole, split[r : r + 1], me ^ r, 0)
    flat = jnp.concatenate([whole.reshape(-1), common])
    flat = sum_small(sum_small(flat, "tensor", n_t), "dp", n_dp)
    width = split.shape[1]
    own = lax.dynamic_slice_in_dim(flat, me * width, width)
    common = flat[n_t * width :].reshape(6, model)

    factor = group_rates / count
    f32 = jnp.float32
    qkv_sum = rest_sum[: 3 * cols_t].reshape(3, cols_t, model)
    return (
        block_out,
        input_grad,
        lay_sum.astype(f32) * factor[6],
        jnp.transpose(qkv_sum, (0, 2, 1)).astype(f32) * factor[0],
        own[: 2 * cols_t].reshape(2, cols_t) * factor[0],
        own[2 * cols_t + hid_t :].reshape(heads_t, 2 * BUCKETS).T * factor[7],
        rest_sum[3 * cols_t : 4 * cols_t].astype(f32) * factor[1],
        common[0] * factor[1],
        common[1] * factor[2],
        common[2] * factor[2],
        w1_sum.T.astype(f32) * factor[3],
        own[2 * cols_t : 2 * cols_t + hid_t] * factor[3],
        w2_sum.astype(f32) * factor[4],
        common[3] * factor[4],
        common[4] * factor[5],
        common[5] * factor[5],
    )


def solution(mesh):
    placed = (
        P("dp", None), P("dp", None), P("dp", None, None), P("dp", None, None), P("dp"), P("dp", None),
        P(), P(None, None, "tensor"), P(None, "tensor"), P(None, "tensor"), P("tensor", None),
        P(), P(), P(), P(None, "tensor"), P("tensor"), P("tensor", None), P(), P(), P(), P(),
    )
    return jax.shard_map(
        functools.partial(local, mesh.shape["dp"], mesh.shape["tensor"]),
        mesh=mesh,
        in_specs=placed,
        out_specs=(
            P("dp", None), P("dp", None), P(), P(None, None, "tensor"), P(None, "tensor"),
            P(None, "tensor"), P("tensor", None), P(), P(), P(), P(None, "tensor"), P("tensor"),
            P("tensor", None), P(), P(), P(),
        ),
        check_vma=False,
    )
```

time: 1280 us -> 488 us (0.38)
  waiting for transfers between devices: 657 us -> 193 us
  matrix products: 296 us -> 71 us
  local copies, waits for them, and re-layouts: 168 us -> 42.3 us
  Pallas kernels: 0 us -> 59.7 us
  starting transfers between devices: 1.06 us -> 50 us
  other arithmetic: 90.7 us -> 47 us
  blocking collectives: 40.2 us -> 0 us
    psum x5 -> x0, waiting for transfers between devices: 657 us -> none  [the longest x1 205 us: local(): lax.psum((grad_lay, grad_qkv, grad_qvb, grad_table, grad_ow, grad_ob, gra...]
    dot_general x65 -> x20, matrix products: 294 us -> 71 us  [the longest x14 44.9 us: nn(): return jnp.dot(a, b, preferred_element_type=jnp.float32)]
    ppermute x0 -> x50, waiting for transfers between devices: none -> 193 us  [swap(): return lax.ppermute(value, axis, [(i, i ^ bit) for i in range(size)])]
    dot_general x16 -> x0, local copies, waits for them, and re-layouts: 77.7 us -> none  [the longest x8 38.9 us: position_bias(): jnp.einsum('ijb,bh->hij', onehot_y, bias_table[buckets:], preferred_eleme...]
    pallas_call x0 -> x2, Pallas kernels: none -> 59.7 us  [the longest x1 32 us: attend_back(): pl.pallas_call(attend_back_kernel, grid=(heads,), in_specs=[blk, blk, blk...]
    ppermute x0 -> x50, starting transfers between devices: none -> 50 us  [swap(): return lax.ppermute(value, axis, [(i, i ^ bit) for i in range(size)])]
    psum x1 -> x0, blocking collectives: 40.2 us -> none  [local(): masked_count = lax.psum(local_count, 'dp')]
    unnamed x145 -> x195, local copies, waits for them, and re-layouts: 35.7 us -> 17.3 us
  transfers between devices with their start and end apart: 5 -> 51, of which waited for: 5 -> 25; matrix products, arithmetic and copies ran while one was open for 5% -> 17% of each run, Pallas kernels for 0% -> 6%
where the time goes in v1:
time: 488 us; the launch traced here: 481 us
  waiting for transfers between devices  193 us (40%)
  matrix products  71 us (15%)
  Pallas kernels  59.7 us (12%)
  starting transfers between devices  50 us (10%)
  other arithmetic  47 us (10%)
  local copies, waits for them, and re-layouts  42.3 us (9%)
  between operations  18.1 us (4%)
    ppermute x50, waiting for transfers between devices, swap(): return lax.ppermute(value, axis, [(i, i ^ bit) for i in range(size)])  193 us
    ppermute x50, starting transfers between devices, swap(): return lax.ppermute(value, axis, [(i, i ^ bit) for i in range(size)])  50 us
    dot_general x14, matrix products, nn(): return jnp.dot(a, b, preferred_element_type=jnp.float32)  44.9 us
    pallas_call x1, Pallas kernels, attend_back(): pl.pallas_call(attend_back_kernel, grid=(heads,), in_specs=[blk, blk, blk...  32 us
    pallas_call x1, Pallas kernels, attend(): pl.pallas_call(attend_kernel, grid=(heads,), in_specs=[blk, blk, blk, ful...  27.7 us
    dot_general x6, matrix products, nt(): lax.dot_general(a, b, (((1,), (1,)), ((), ())), preferred_element_type=jn...  26.1 us
    unnamed x195, local copies, waits for them, and re-layouts  17.3 us
  transfers between devices with their start and end apart: 51, of which 25 were waited for; matrix products, arithmetic and copies ran while one was open for 17% of the time, Pallas kernels for 6%

profile of v1, /device:TPU:0, one launch (start us, length us, event | category | flops | bytes accessed | tf_op | source)
XLA Modules:
  0.0 480.7 jit_solution(2136943945589563939)
XLA Ops:
  9.7 3.0 collective-permute-start.4
  25.9 3.1 fusion.61
  32.8 2.9 collective-permute-start.10
  37.1 4.0 collective-permute-start.11
  44.4 3.6 collective-permute-done.5
  53.5 41.0 %collective-permute-done.7 = bf16[1728,768]{1,0:T(8,128)(2,1)} collective-permute-done((bf16[1728,768]{1,0:T(8,128)(2,1)}, bf16[1728,768]{1,0:T(8,128)(2,1)}, u32[]{:S(2)}, u32[]{:S(2)}) %collective-permute-start.7) | collective-permute-done | bytes 2654240 | tf_op jit(solution)/shard_map/ppermute | solution.py:170
  96.3 27.7 %attend.1 = (f32[12,512,512]{2,1,0:T(8,128)}, bf16[768,512]{1,0:T(8,128)(2,1)S(1)}) custom-call(bf16[768,512]{1,0:T(8,128)(2,1)S(1)} %add_convert_fusion.3.q_ref, bf16[768,512]{1,0:T(8,128)(2,1)S(1)} %convolution_convert_fusion.1.k_ref, bf16[768,512]{1,0:T(8,128)(2,1)S(1)} %add_convert_fusion.2.v_ref, s32[512,512]{1,0:T(8,128)S(1)} %get-tuple-element.192.rx_ref, ...), custom_call_target="tpu_custom_call" | custom-call | flops 16000000000 | bytes 20000000 | tf_op jit(solution)/shard_map/attend/pallas_call | solution.py:77
  132.5 5.4 %fusion.16 = f32[512,3072]{1,0:T(8,128)} fusion(bf16[768,768]{1,0:T(8,128)(2,1)S(1)} %get-tuple-element.98, bf16[768,768]{1,0:T(8,128)(2,1)S(1)} %get-tuple-element.96, bf16[768,768]{1,0:T(8,128)(2,1)S(1)} %get-tuple-element.94, bf16[768,768]{1,0:T(8,128)(2,1)S(1)} %bitcast.74, f32[512,768]{1,0:T(8,128)S(1)} %get-tuple-element.170, f32[768]{0:T(1024)S(1)} %copy-done.77, ...), kind=kOutput, calls=%fused_computation.74 | convolution fusion | flops 2436759552 | bytes 12593152 | tf_op jit(solution)/shard_map/dot_general | solution.py:19
  137.9 7.1 %fusion.63 = (f32[512]{0:T(512)S(1)}, f32[512,768]{1,0:T(8,128)S(1)}) fusion(f32[768]{0:T(1024)S(1)} %copy-done.82, bf16[768,768]{1,0:T(8,128)(2,1)S(1)} %get-tuple-element.99, bf16[768,768]{1,0:T(8,128)(2,1)S(1)} %get-tuple-element.97, bf16[768,768]{1,0:T(8,128)(2,1)S(1)} %get-tuple-element.95, bf16[768,768]{1,0:T(8,128)(2,1)S(1)} %copy-done.37, ...), kind=kOutput, calls=%fused_computation.221 | convolution fusion | flops 2453274112 | bytes 14183424 | tf_op jit(solution)/shard_map/dot_general | solution.py:23
  148.2 16.6 %convert_reduce_fusion = (f32[3072]{0:T(1024)S(1)}, bf16[512,3072]{1,0:T(8,128)(2,1)S(1)}) fusion(f32[512,3072]{1,0:T(8,128)} %fusion.16, f32[3072]{0:T(1024)S(1)} %pad_maximum_fusion.22, bf16[768,768]{1,0:T(8,128)(2,1)S(1)} %get-tuple-element.99, bf16[768,768]{1,0:T(8,128)(2,1)S(1)} %get-tuple-element.97, bf16[768,768]{1,0:T(8,128)(2,1)S(1)} %get-tuple-element.95, ...), kind=kOutput, calls=%fused_computation.9 | convolution fusion | flops 2471359488 | bytes 15753216 | tf_op jit(solution)/shard_map/dot_general | solution.py:19
  164.8 3.6 multiply_reduce_fusion.1
  170.6 32.0 %attend_back.1 = (bf16[768,512]{1,0:T(8,128)(2,1)}, bf16[768,512]{1,0:T(8,128)(2,1)}, bf16[768,512]{1,0:T(8,128)(2,1)}, f32[12,1024]{1,0:T(8,128)}) custom-call(bf16[768,512]{1,0:T(8,128)(2,1)} %copy-done.6, bf16[768,512]{1,0:T(8,128)(2,1)} %copy-done.4, bf16[768,512]{1,0:T(8,128)(2,1)} %copy-done.5, f32[12,512,512]{2,1,0:T(8,128)} %get-tuple-element.23.p_ref, ...), custom_call_target="tpu_custom_call" | custom-call | flops 20000000000 | bytes 20000000 | tf_op jit(solution)/shard_map/attend_back/pallas_call | solution.py:144
  204.0 3.1 fusion.28
  207.1 2.6 fusion.67
  209.9 2.6 fusion.66
  212.5 2.6 fusion.64
  217.2 2.6 fusion.65
  219.8 7.1 %fusion.69 = (bf16[3072,768]{1,0:T(8,128)(2,1)}, f32[3072,768]{1,0:T(8,128)}) fusion(f32[512,768]{1,0:T(8,128)S(1)} %copy-done.33, f32[512,3072]{1,0:T(8,128)S(1)} %bitcast.83, f32[3072]{0:T(1024)S(1)} %pad_maximum_fusion.22), kind=kOutput, calls=%fused_computation.227 | convolution fusion | flops 2434400256 | bytes 22032384 | tf_op jit(solution)/shard_map/dot_general | solution.py:23
  230.4 4.1 constant_dynamic-update-slice_fusion.10
  243.0 2.9 fusion.68
  249.4 2.9 collective-permute-done.28
  252.8 2.2 fusion.7
  258.0 2.4 collective-permute-done.30
  260.4 2.7 collective-permute-start.31
  263.2 2.1 collective-permute-done.31
  269.4 14.5 %collective-permute-done.43 = bf16[768,768]{1,0:T(8,128)(2,1)S(1)} collective-permute-done((bf16[768,768]{1,0:T(8,128)(2,1)S(1)}, bf16[768,768]{1,0:T(8,128)(2,1)S(1)}, u32[]{:S(2)}, u32[]{:S(2)}) %collective-permute-start.43) | collective-permute-done | bytes 1179680 | tf_op jit(solution)/shard_map/ppermute | solution.py:170
  286.3 3.6 slice_multiply_fusion
  289.9 2.6 fusion.8
  292.6 8.3 %collective-permute-done.13 = bf16[512,768]{1,0:T(8,128)(2,1)} collective-permute-done((bf16[512,768]{1,0:T(8,128)(2,1)}, bf16[512,768]{1,0:T(8,128)(2,1)}, u32[]{:S(2)}, u32[]{:S(2)}) %collective-permute-start.13) | collective-permute-done | bytes 786464 | tf_op jit(solution)/shard_map/ppermute | solution.py:170
  301.4 24.8 %collective-permute-done.34 = bf16[768,768]{1,0:T(8,128)(2,1)} collective-permute-done((bf16[768,768]{1,0:T(8,128)(2,1)}, bf16[768,768]{1,0:T(8,128)(2,1)}, u32[]{:S(2)}, u32[]{:S(2)}) %collective-permute-start.34) | collective-permute-done | bytes 1179680 | tf_op jit(solution)/shard_map/ppermute | solution.py:170
  327.7 2.8 fusion.10
  331.2 22.9 %collective-permute-done.17 = bf16[896,768]{1,0:T(8,128)(2,1)} collective-permute-done((bf16[896,768]{1,0:T(8,128)(2,1)S(1)}, bf16[896,768]{1,0:T(8,128)(2,1)}, u32[]{:S(2)}, u32[]{:S(2)}) %collective-permute-start.17) | collective-permute-done | bytes 1376288 | tf_op jit(solution)/shard_map/ppermute | solution.py:170
  360.0 9.3 %collective-permute-done.45 = bf16[192,768]{1,0:T(8,128)(2,1)S(1)} collective-permute-done((bf16[192,768]{1,0:T(8,128)(2,1)S(1)}, bf16[192,768]{1,0:T(8,128)(2,1)S(1)}, u32[]{:S(2)}, u32[]{:S(2)}) %collective-permute-start.45) | collective-permute-done | bytes 294944 | tf_op jit(solution)/shard_map/ppermute | solution.py:170
  373.1 2.2 collective-permute-start.19
  379.1 9.2 %collective-permute-done.19 = bf16[224,768]{1,0:T(8,128)(2,1)S(1)} collective-permute-done((bf16[224,768]{1,0:T(8,128)(2,1)S(1)}, bf16[224,768]{1,0:T(8,128)(2,1)S(1)}, u32[]{:S(2)}, u32[]{:S(2)}) %collective-permute-start.19) | collective-permute-done | bytes 344096 | tf_op jit(solution)/shard_map/ppermute | solution.py:170
  389.0 2.6 collective-permute-start.38
  391.6 9.2 %collective-permute-done.20 = bf16[112,768]{1,0:T(8,128)(2,1)S(1)} collective-permute-done((bf16[112,768]{1,0:T(8,128)(2,1)S(1)}, bf16[112,768]{1,0:T(8,128)(2,1)S(1)}, u32[]{:S(2)}, u32[]{:S(2)}) %collective-permute-start.20) | collective-permute-done | bytes 172064 | tf_op jit(solution)/shard_map/ppermute | solution.py:170
  400.9 4.9 %collective-permute-done.38 = bf16[96,768]{1,0:T(8,128)(2,1)S(1)} collective-permute-done((bf16[96,768]{1,0:T(8,128)(2,1)S(1)}, bf16[96,768]{1,0:T(8,128)(2,1)S(1)}, u32[]{:S(2)}, u32[]{:S(2)}) %collective-permute-start.38) | collective-permute-done | bytes 147488 | tf_op jit(solution)/shard_map/ppermute | solution.py:170
  405.9 2.9 collective-permute-start.39
  409.0 2.4 collective-permute-done.21
  413.5 4.2 collective-permute-done.39
  419.0 5.0 %collective-permute-done.48 = bf16[192,768]{1,0:T(8,128)(2,1)S(1)} collective-permute-done((bf16[192,768]{1,0:T(8,128)(2,1)S(1)}, bf16[192,768]{1,0:T(8,128)(2,1)S(1)}, u32[]{:S(2)}, u32[]{:S(2)}) %collective-permute-start.48) | collective-permute-done | bytes 294944 | tf_op jit(solution)/shard_map/ppermute | solution.py:170
  426.2 4.1 collective-permute-done.22
  436.0 3.2 convert_element_type.229
  442.1 4.9 %collective-permute-done.49 = bf16[384,768]{1,0:T(8,128)(2,1)} collective-permute-done((bf16[384,768]{1,0:T(8,128)(2,1)}, bf16[384,768]{1,0:T(8,128)(2,1)}, u32[]{:S(2)}, u32[]{:S(2)}) %collective-permute-start.49) | collective-permute-done | bytes 589856 | tf_op jit(solution)/shard_map/ppermute | solution.py:170
  447.0 4.0 convert_multiply_fusion
  450.9 8.5 %collective-permute-done.23 = bf16[448,768]{1,0:T(8,128)(2,1)} collective-permute-done((bf16[448,768]{1,0:T(8,128)(2,1)S(1)}, bf16[448,768]{1,0:T(8,128)(2,1)}, u32[]{:S(2)}, u32[]{:S(2)}) %collective-permute-start.23) | collective-permute-done | bytes 688160 | tf_op jit(solution)/shard_map/ppermute | solution.py:170
  465.7 3.0 collective-permute-done.25
  (403 shorter events, 113.7 us)
Async XLA Ops:
  7.2 443.7 %all-gather.2.cloned.1.call-start = ((), (), s32[]{:S(2)}) async-start(), calls=%async_computation | async-start | bytes 3932160 | tf_op jit(solution)/shard_map/all_gather | solution.py:281
  9.7 33.3 %collective-permute-start.4 = (f32[1344]{0:T(1024)S(1)}, f32[1344]{0:T(1024)S(1)}, u32[]{:S(2)}, u32[]{:S(2)}) collective-permute-start(f32[1344]{0:T(1024)S(1)} %constant_dynamic-update-slice_fusion.17), channel_id=1, source_target_pairs={{0,2},{1,3},{2,0},{3,1},{4,6},{5,7},{6,4},{7,5},{8,10},{9,11},{10,... | collective-permute-start | bytes 16136 | tf_op jit(solution)/shard_map/ppermute | solution.py:170
  12.7 30.9 %collective-permute-start.3 = (f32[1344]{0:T(1024)S(1)}, f32[1344]{0:T(1024)S(1)}, u32[]{:S(2)}, u32[]{:S(2)}) collective-permute-start(f32[1344]{0:T(1024)S(1)} %constant_dynamic-update-slice_fusion.17), channel_id=1, source_target_pairs={{0,1},{1,0},{2,3},{3,2},{4,5},{5,4},{6,7},{7,6},{8,9},{9,8},{10,11... | collective-permute-start | bytes 16136 | tf_op jit(solution)/shard_map/ppermute | solution.py:170
  14.0 17.6 %collective-permute-start.9 = (f32[1]{0:T(128)}, f32[1]{0:T(128)}, u32[]{:S(2)}, u32[]{:S(2)}) collective-permute-start(f32[1]{0:T(128)} %bitcast.20), channel_id=1, source_target_pairs={{0,4},{4,0},{8,12},{12,8},{16,20},{20,16},{24,28},{28,24},{1,5},{5... | collective-permute-start | bytes 20 | tf_op jit(solution)/shard_map/ppermute | solution.py:170
  15.5 28.4 %collective-permute-start.1 = (bf16[3,192,768]{2,1,0:T(8,128)(2,1)}, bf16[3,192,768]{2,1,0:T(8,128)(2,1)}, u32[]{:S(2)}, u32[]{:S(2)}) collective-permute-start(bf16[3,192,768]{2,1,0:T(8,128)(2,1)} %bitcast.1), channel_id=1, source_target_pairs={{0,2},{1,3},{2,0},{3,1},{4,6},{5,7},{6,4},{7,5},{8,10},{9,11},{10,... | collective-permute-start | bytes 2654216 | tf_op jit(solution)/shard_map/ppermute | solution.py:170
  19.5 75.0 %collective-permute-start.7 = (bf16[1728,768]{1,0:T(8,128)(2,1)}, bf16[1728,768]{1,0:T(8,128)(2,1)}, u32[]{:S(2)}, u32[]{:S(2)}) collective-permute-start(bf16[1728,768]{1,0:T(8,128)(2,1)} %pad_maximum_fusion.2), channel_id=1, source_target_pairs={{0,2},{1,3},{2,0},{3,1},{4,6},{5,7},{6,4},{7,5},{8,10},{9,11},{10,... | collective-permute-start | bytes 7962632 | tf_op jit(solution)/shard_map/ppermute | solution.py:170
  37.1 4.6 collective-permute-start.11
  41.7 7.8 %collective-permute-start = (bf16[3,192,768]{2,1,0:T(8,128)(2,1)}, bf16[3,192,768]{2,1,0:T(8,128)(2,1)}, u32[]{:S(2)}, u32[]{:S(2)}) collective-permute-start(bf16[3,192,768]{2,1,0:T(8,128)(2,1)} %bitcast.1), channel_id=1, source_target_pairs={{0,1},{1,0},{2,3},{3,2},{4,5},{5,4},{6,7},{7,6},{8,9},{9,8},{10,11... | collective-permute-start | bytes 2654216 | tf_op jit(solution)/shard_map/ppermute | solution.py:170
  42.9 82.0 %collective-permute-start.6 = (bf16[1728,768]{1,0:T(8,128)(2,1)}, bf16[1728,768]{1,0:T(8,128)(2,1)}, u32[]{:S(2)}, u32[]{:S(2)}) collective-permute-start(bf16[1728,768]{1,0:T(8,128)(2,1)} %pad_maximum_fusion.2), channel_id=1, source_target_pairs={{0,1},{1,0},{2,3},{3,2},{4,5},{5,4},{6,7},{7,6},{8,9},{9,8},{10,11... | collective-permute-start | bytes 7962632 | tf_op jit(solution)/shard_map/ppermute | solution.py:170
  43.6 4.4 collective-permute-start.5
  43.9 7.2 %collective-permute-start.2 = (bf16[3,192,768]{2,1,0:T(8,128)(2,1)}, bf16[3,192,768]{2,1,0:T(8,128)(2,1)}, u32[]{:S(2)}, u32[]{:S(2)}) collective-permute-start(bf16[3,192,768]{2,1,0:T(8,128)(2,1)} %collective-permute-done.1), channel_id=1, source_target_pairs={{0,1},{1,0},{2,3},{3,2},{4,5},{5,4},{6,7},{7,6},{8,9},{9,8},{10,11... | collective-permute-start | bytes 2654216 | tf_op jit(solution)/shard_map/ppermute | solution.py:170
  94.5 35.2 %collective-permute-start.8 = (bf16[1728,768]{1,0:T(8,128)(2,1)}, bf16[1728,768]{1,0:T(8,128)(2,1)S(1)}, u32[]{:S(2)}, u32[]{:S(2)}) collective-permute-start(bf16[1728,768]{1,0:T(8,128)(2,1)} %collective-permute-done.7), channel_id=1, source_target_pairs={{0,1},{1,0},{2,3},{3,2},{4,5},{5,4},{6,7},{7,6},{8,9},{9,8},{10,11... | collective-permute-start | bytes 7962632 | tf_op jit(solution)/shard_map/ppermute | solution.py:170
  228.7 18.4 %collective-permute-start.27 = (f32[9984]{0:T(1024)S(1)}, f32[9984]{0:T(1024)S(1)}, u32[]{:S(2)}, u32[]{:S(2)}) collective-permute-start(f32[9984]{0:T(1024)S(1)} %constant_dynamic-update-slice_fusion.11), channel_id=1, source_target_pairs={{0,1},{1,0},{2,3},{3,2},{4,5},{5,4},{6,7},{7,6},{8,9},{9,8},{10,11... | collective-permute-start | bytes 119816 | tf_op jit(solution)/shard_map/ppermute | solution.py:170
  240.5 27.1 %collective-permute-start.16 = (bf16[896,768]{1,0:T(8,128)(2,1)S(1)}, bf16[896,768]{1,0:T(8,128)(2,1)S(1)}, u32[]{:S(2)}, u32[]{:S(2)}) collective-permute-start(bf16[896,768]{1,0:T(8,128)(2,1)S(1)} %get-tuple-element.110), channel_id=1, source_target_pairs={{0,1},{1,0},{2,3},{3,2},{4,5},{5,4},{6,7},{7,6},{8,9},{9,8},{10,11... | collective-permute-start | bytes 4128776 | tf_op jit(solution)/shard_map/ppermute | solution.py:170
  241.3 27.8 %collective-permute-start.41 = (bf16[768,768]{1,0:T(8,128)(2,1)S(1)}, bf16[768,768]{1,0:T(8,128)(2,1)S(1)}, u32[]{:S(2)}, u32[]{:S(2)}) collective-permute-start(bf16[768,768]{1,0:T(8,128)(2,1)S(1)} %get-tuple-element.90), channel_id=1, source_target_pairs={{0,1},{1,0},{2,3},{3,2},{4,5},{5,4},{6,7},{7,6},{8,9},{9,8},{10,11... | collective-permute-start | bytes 3538952 | tf_op jit(solution)/shard_map/ppermute | solution.py:170
  241.4 11.4 %collective-permute-start.42 = (bf16[768,768]{1,0:T(8,128)(2,1)S(1)}, bf16[768,768]{1,0:T(8,128)(2,1)S(1)}, u32[]{:S(2)}, u32[]{:S(2)}) collective-permute-start(bf16[768,768]{1,0:T(8,128)(2,1)S(1)} %get-tuple-element.91), channel_id=1, source_target_pairs={{0,1},{1,0},{2,3},{3,2},{4,5},{5,4},{6,7},{7,6},{8,9},{9,8},{10,11... | collective-permute-start | bytes 3538952 | tf_op jit(solution)/shard_map/ppermute | solution.py:170
  247.1 19.0 %collective-permute-start.33 = (bf16[768,768]{1,0:T(8,128)(2,1)S(1)}, bf16[768,768]{1,0:T(8,128)(2,1)S(1)}, u32[]{:S(2)}, u32[]{:S(2)}) collective-permute-start(bf16[768,768]{1,0:T(8,128)(2,1)S(1)} %get-tuple-element.93), channel_id=1, source_target_pairs={{0,1},{1,0},{2,3},{3,2},{4,5},{5,4},{6,7},{7,6},{8,9},{9,8},{10,11... | collective-permute-start | bytes 3538952 | tf_op jit(solution)/shard_map/ppermute | solution.py:170
  247.2 5.2 %collective-permute-start.28 = (f32[9984]{0:T(1024)S(1)}, f32[9984]{0:T(1024)S(1)}, u32[]{:S(2)}, u32[]{:S(2)}) collective-permute-start(f32[9984]{0:T(1024)S(1)} %add.354), channel_id=1, source_target_pairs={{0,2},{1,3},{2,0},{3,1},{4,6},{5,7},{6,4},{7,5},{8,10},{9,11},{10,... | collective-permute-start | bytes 119816 | tf_op jit(solution)/shard_map/ppermute | solution.py:170
  252.3 4.0 collective-permute-start.29
  255.0 29.0 %collective-permute-start.43 = (bf16[768,768]{1,0:T(8,128)(2,1)S(1)}, bf16[768,768]{1,0:T(8,128)(2,1)S(1)}, u32[]{:S(2)}, u32[]{:S(2)}) collective-permute-start(bf16[768,768]{1,0:T(8,128)(2,1)S(1)} %fusion.7), channel_id=1, source_target_pairs={{0,2},{1,3},{2,0},{3,1},{4,6},{5,7},{6,4},{7,5},{8,10},{9,11},{10,... | collective-permute-start | bytes 3538952 | tf_op jit(solution)/shard_map/ppermute | solution.py:170
  260.4 4.9 %collective-permute-start.31 = (f32[9984]{0:T(1024)S(1)}, f32[9984]{0:T(1024)S(1)}, u32[]{:S(2)}, u32[]{:S(2)}) collective-permute-start(f32[9984]{0:T(1024)S(1)} %add.357), channel_id=1, source_target_pairs={{0,16},{4,20},{8,24},{12,28},{16,0},{20,4},{24,8},{28,12},{1,17},{... | collective-permute-start | bytes 119816 | tf_op jit(solution)/shard_map/ppermute | solution.py:170
  265.3 35.6 %collective-permute-start.13 = (bf16[512,768]{1,0:T(8,128)(2,1)}, bf16[512,768]{1,0:T(8,128)(2,1)}, u32[]{:S(2)}, u32[]{:S(2)}) collective-permute-start(bf16[512,768]{1,0:T(8,128)(2,1)} %get-tuple-element.89), channel_id=1, source_target_pairs={{0,2},{1,3},{2,0},{3,1},{4,6},{5,7},{6,4},{7,5},{8,10},{9,11},{10,... | collective-permute-start | bytes 2359304 | tf_op jit(solution)/shard_map/ppermute | solution.py:170
  266.2 34.7 %collective-permute-start.32 = (bf16[768,768]{1,0:T(8,128)(2,1)}, bf16[768,768]{1,0:T(8,128)(2,1)}, u32[]{:S(2)}, u32[]{:S(2)}) collective-permute-start(bf16[768,768]{1,0:T(8,128)(2,1)} %get-tuple-element.92), channel_id=1, source_target_pairs={{0,1},{1,0},{2,3},{3,2},{4,5},{5,4},{6,7},{7,6},{8,9},{9,8},{10,11... | collective-permute-start | bytes 3538952 | tf_op jit(solution)/shard_map/ppermute | solution.py:170
  267.6 58.6 %collective-permute-start.34 = (bf16[768,768]{1,0:T(8,128)(2,1)}, bf16[768,768]{1,0:T(8,128)(2,1)}, u32[]{:S(2)}, u32[]{:S(2)}) collective-permute-start(bf16[768,768]{1,0:T(8,128)(2,1)} %fusion.9), channel_id=1, source_target_pairs={{0,2},{1,3},{2,0},{3,1},{4,6},{5,7},{6,4},{7,5},{8,10},{9,11},{10,... | collective-permute-start | bytes 3538952 | tf_op jit(solution)/shard_map/ppermute | solution.py:170
  269.1 61.5 %collective-permute-start.15 = (bf16[896,768]{1,0:T(8,128)(2,1)}, bf16[896,768]{1,0:T(8,128)(2,1)S(1)}, u32[]{:S(2)}, u32[]{:S(2)}) collective-permute-start(bf16[896,768]{1,0:T(8,128)(2,1)} %get-tuple-element.109), channel_id=1, source_target_pairs={{0,1},{1,0},{2,3},{3,2},{4,5},{5,4},{6,7},{7,6},{8,9},{9,8},{10,11... | collective-permute-start | bytes 4128776 | tf_op jit(solution)/shard_map/ppermute | solution.py:170
  283.9 70.1 %collective-permute-start.17 = (bf16[896,768]{1,0:T(8,128)(2,1)S(1)}, bf16[896,768]{1,0:T(8,128)(2,1)}, u32[]{:S(2)}, u32[]{:S(2)}) collective-permute-start(bf16[896,768]{1,0:T(8,128)(2,1)S(1)} %add_convert_fusion), channel_id=1, source_target_pairs={{0,2},{1,3},{2,0},{3,1},{4,6},{5,7},{6,4},{7,5},{8,10},{9,11},{10,... | collective-permute-start | bytes 4128776 | tf_op jit(solution)/shard_map/ppermute | solution.py:170
  300.9 131.5 %collective-permute-start.12 = (bf16[512,768]{1,0:T(8,128)(2,1)}, bf16[512,768]{1,0:T(8,128)(2,1)}, u32[]{:S(2)}, u32[]{:S(2)}) collective-permute-start(bf16[512,768]{1,0:T(8,128)(2,1)} %get-tuple-element.89), channel_id=1, source_target_pairs={{0,1},{1,0},{2,3},{3,2},{4,5},{5,4},{6,7},{7,6},{8,9},{9,8},{10,11... | collective-permute-start | bytes 2359304 | tf_op jit(solution)/shard_map/ppermute | solution.py:170
  300.9 133.9 %collective-permute-start.14 = (bf16[512,768]{1,0:T(8,128)(2,1)}, bf16[512,768]{1,0:T(8,128)(2,1)}, u32[]{:S(2)}, u32[]{:S(2)}) collective-permute-start(bf16[512,768]{1,0:T(8,128)(2,1)} %collective-permute-done.13), channel_id=1, source_target_pairs={{0,1},{1,0},{2,3},{3,2},{4,5},{5,4},{6,7},{7,6},{8,9},{9,8},{10,11... | collective-permute-start | bytes 2359304 | tf_op jit(solution)/shard_map/ppermute | solution.py:170
  326.2 31.4 %collective-permute-start.44 = (bf16[384,768]{1,0:T(8,128)(2,1)S(1)}, bf16[384,768]{1,0:T(8,128)(2,1)S(1)}, u32[]{:S(2)}, u32[]{:S(2)}) collective-permute-start(bf16[384,768]{1,0:T(8,128)(2,1)S(1)} %dynamic-slice_convert_fusion.1), channel_id=1, source_target_pairs={{0,4},{4,0},{8,12},{12,8},{16,20},{20,16},{24,28},{28,24},{1,5},{5... | collective-permute-start | bytes 1769480 | tf_op jit(solution)/shard_map/ppermute | solution.py:170
  330.6 28.7 %collective-permute-start.35 = (bf16[384,768]{1,0:T(8,128)(2,1)S(1)}, bf16[384,768]{1,0:T(8,128)(2,1)S(1)}, u32[]{:S(2)}, u32[]{:S(2)}) collective-permute-start(bf16[384,768]{1,0:T(8,128)(2,1)S(1)} %dynamic-slice_convert_fusion.2), channel_id=1, source_target_pairs={{0,4},{4,0},{8,12},{12,8},{16,20},{20,16},{24,28},{28,24},{1,5},{5... | collective-permute-start | bytes 1769480 | tf_op jit(solution)/shard_map/ppermute | solution.py:170
  355.9 17.0 %collective-permute-start.18 = (bf16[448,768]{1,0:T(8,128)(2,1)S(1)}, bf16[448,768]{1,0:T(8,128)(2,1)S(1)}, u32[]{:S(2)}, u32[]{:S(2)}) collective-permute-start(bf16[448,768]{1,0:T(8,128)(2,1)S(1)} %dynamic-slice_convert_fusion), channel_id=1, source_target_pairs={{0,4},{4,0},{8,12},{12,8},{16,20},{20,16},{24,28},{28,24},{1,5},{5... | collective-permute-start | bytes 2064392 | tf_op jit(solution)/shard_map/ppermute | solution.py:170
  357.7 11.6 %collective-permute-start.45 = (bf16[192,768]{1,0:T(8,128)(2,1)S(1)}, bf16[192,768]{1,0:T(8,128)(2,1)S(1)}, u32[]{:S(2)}, u32[]{:S(2)}) collective-permute-start(bf16[192,768]{1,0:T(8,128)(2,1)S(1)} %dynamic-slice_convert_fusion.4), channel_id=1, source_target_pairs={{0,8},{4,12},{8,0},{12,4},{16,24},{20,28},{24,16},{28,20},{1,9},{5... | collective-permute-start | bytes 884744 | tf_op jit(solution)/shard_map/ppermute | solution.py:170
  359.5 13.3 %collective-permute-start.36 = (bf16[192,768]{1,0:T(8,128)(2,1)S(1)}, bf16[192,768]{1,0:T(8,128)(2,1)S(1)}, u32[]{:S(2)}, u32[]{:S(2)}) collective-permute-start(bf16[192,768]{1,0:T(8,128)(2,1)S(1)} %dynamic-slice_convert_fusion.5), channel_id=1, source_target_pairs={{0,8},{4,12},{8,0},{12,4},{16,24},{20,28},{24,16},{28,20},{1,9},{5... | collective-permute-start | bytes 884744 | tf_op jit(solution)/shard_map/ppermute | solution.py:170
  369.4 8.1 %collective-permute-start.46 = (bf16[96,768]{1,0:T(8,128)(2,1)S(1)}, bf16[96,768]{1,0:T(8,128)(2,1)S(1)}, u32[]{:S(2)}, u32[]{:S(2)}) collective-permute-start(bf16[96,768]{1,0:T(8,128)(2,1)S(1)} %dynamic-slice_convert_fusion.9), channel_id=1, source_target_pairs={{0,16},{4,20},{8,24},{12,28},{16,0},{20,4},{24,8},{28,12},{1,17},{... | collective-permute-start | bytes 442376 | tf_op jit(solution)/shard_map/ppermute | solution.py:170
  373.1 15.3 %collective-permute-start.19 = (bf16[224,768]{1,0:T(8,128)(2,1)S(1)}, bf16[224,768]{1,0:T(8,128)(2,1)S(1)}, u32[]{:S(2)}, u32[]{:S(2)}) collective-permute-start(bf16[224,768]{1,0:T(8,128)(2,1)S(1)} %dynamic-slice_convert_fusion.3), channel_id=1, source_target_pairs={{0,8},{4,12},{8,0},{12,4},{16,24},{20,28},{24,16},{28,20},{1,9},{5... | collective-permute-start | bytes 1032200 | tf_op jit(solution)/shard_map/ppermute | solution.py:170
  375.3 13.6 %collective-permute-start.37 = (bf16[96,768]{1,0:T(8,128)(2,1)S(1)}, bf16[96,768]{1,0:T(8,128)(2,1)S(1)}, u32[]{:S(2)}, u32[]{:S(2)}) collective-permute-start(bf16[96,768]{1,0:T(8,128)(2,1)S(1)} %dynamic-slice_convert_fusion.10), channel_id=1, source_target_pairs={{0,16},{4,20},{8,24},{12,28},{16,0},{20,4},{24,8},{28,12},{1,17},{... | collective-permute-start | bytes 442376 | tf_op jit(solution)/shard_map/ppermute | solution.py:170
  377.5 31.3 %collective-permute-start.47 = (bf16[96,768]{1,0:T(8,128)(2,1)S(1)}, bf16[96,768]{1,0:T(8,128)(2,1)S(1)}, u32[]{:S(2)}, u32[]{:S(2)}) collective-permute-start(bf16[96,768]{1,0:T(8,128)(2,1)S(1)} %add_convert_fusion.5), channel_id=1, source_target_pairs={{0,16},{4,20},{8,24},{12,28},{16,0},{20,4},{24,8},{28,12},{1,17},{... | collective-permute-start | bytes 442376 | tf_op jit(solution)/shard_map/ppermute | solution.py:170
  388.5 12.3 %collective-permute-start.20 = (bf16[112,768]{1,0:T(8,128)(2,1)S(1)}, bf16[112,768]{1,0:T(8,128)(2,1)S(1)}, u32[]{:S(2)}, u32[]{:S(2)}) collective-permute-start(bf16[112,768]{1,0:T(8,128)(2,1)S(1)} %dynamic-slice_convert_fusion.8), channel_id=1, source_target_pairs={{0,16},{4,20},{8,24},{12,28},{16,0},{20,4},{24,8},{28,12},{1,17},{... | collective-permute-start | bytes 516104 | tf_op jit(solution)/shard_map/ppermute | solution.py:170
  389.0 16.9 %collective-permute-start.38 = (bf16[96,768]{1,0:T(8,128)(2,1)S(1)}, bf16[96,768]{1,0:T(8,128)(2,1)S(1)}, u32[]{:S(2)}, u32[]{:S(2)}) collective-permute-start(bf16[96,768]{1,0:T(8,128)(2,1)S(1)} %add_convert_fusion.6), channel_id=1, source_target_pairs={{0,16},{4,20},{8,24},{12,28},{16,0},{20,4},{24,8},{28,12},{1,17},{... | collective-permute-start | bytes 442376 | tf_op jit(solution)/shard_map/ppermute | solution.py:170
  400.9 10.5 %collective-permute-start.21 = (bf16[112,768]{1,0:T(8,128)(2,1)S(1)}, bf16[112,768]{1,0:T(8,128)(2,1)S(1)}, u32[]{:S(2)}, u32[]{:S(2)}) collective-permute-start(bf16[112,768]{1,0:T(8,128)(2,1)S(1)} %add_convert_fusion.4), channel_id=1, source_target_pairs={{0,16},{4,20},{8,24},{12,28},{16,0},{20,4},{24,8},{28,12},{1,17},{... | collective-permute-start | bytes 516104 | tf_op jit(solution)/shard_map/ppermute | solution.py:170
  405.9 11.8 %collective-permute-start.39 = (bf16[192,768]{1,0:T(8,128)(2,1)S(1)}, bf16[192,768]{1,0:T(8,128)(2,1)S(1)}, u32[]{:S(2)}, u32[]{:S(2)}) collective-permute-start(bf16[192,768]{1,0:T(8,128)(2,1)S(1)} %maximum_select_fusion.7), channel_id=1, source_target_pairs={{0,8},{4,12},{8,0},{12,4},{16,24},{20,28},{24,16},{28,20},{1,9},{5... | collective-permute-start | bytes 884744 | tf_op jit(solution)/shard_map/ppermute | solution.py:170
  408.9 15.1 %collective-permute-start.48 = (bf16[192,768]{1,0:T(8,128)(2,1)S(1)}, bf16[192,768]{1,0:T(8,128)(2,1)S(1)}, u32[]{:S(2)}, u32[]{:S(2)}) collective-permute-start(bf16[192,768]{1,0:T(8,128)(2,1)S(1)} %maximum_select_fusion.8), channel_id=1, source_target_pairs={{0,8},{4,12},{8,0},{12,4},{16,24},{20,28},{24,16},{28,20},{1,9},{5... | collective-permute-start | bytes 884744 | tf_op jit(solution)/shard_map/ppermute | solution.py:170
  411.4 18.9 %collective-permute-start.22 = (bf16[224,768]{1,0:T(8,128)(2,1)S(1)}, bf16[224,768]{1,0:T(8,128)(2,1)S(1)}, u32[]{:S(2)}, u32[]{:S(2)}) collective-permute-start(bf16[224,768]{1,0:T(8,128)(2,1)S(1)} %maximum_select_fusion.6), channel_id=1, source_target_pairs={{0,8},{4,12},{8,0},{12,4},{16,24},{20,28},{24,16},{28,20},{1,9},{5... | collective-permute-start | bytes 1032200 | tf_op jit(solution)/shard_map/ppermute | solution.py:170
  417.9 21.3 %collective-permute-start.40 = (bf16[384,768]{1,0:T(8,128)(2,1)S(1)}, bf16[384,768]{1,0:T(8,128)(2,1)S(1)}, u32[]{:S(2)}, u32[]{:S(2)}) collective-permute-start(bf16[384,768]{1,0:T(8,128)(2,1)S(1)} %maximum_select_fusion.4), channel_id=1, source_target_pairs={{0,4},{4,0},{8,12},{12,8},{16,20},{20,16},{24,28},{28,24},{1,5},{5... | collective-permute-start | bytes 1769480 | tf_op jit(solution)/shard_map/ppermute | solution.py:170
  425.2 21.8 %collective-permute-start.49 = (bf16[384,768]{1,0:T(8,128)(2,1)}, bf16[384,768]{1,0:T(8,128)(2,1)}, u32[]{:S(2)}, u32[]{:S(2)}) collective-permute-start(bf16[384,768]{1,0:T(8,128)(2,1)} %maximum_select_fusion.5), channel_id=1, source_target_pairs={{0,4},{4,0},{8,12},{12,8},{16,20},{20,16},{24,28},{28,24},{1,5},{5... | collective-permute-start | bytes 1769480 | tf_op jit(solution)/shard_map/ppermute | solution.py:170
  430.6 28.9 %collective-permute-start.23 = (bf16[448,768]{1,0:T(8,128)(2,1)S(1)}, bf16[448,768]{1,0:T(8,128)(2,1)}, u32[]{:S(2)}, u32[]{:S(2)}) collective-permute-start(bf16[448,768]{1,0:T(8,128)(2,1)S(1)} %maximum_select_fusion.3), channel_id=1, source_target_pairs={{0,4},{4,0},{8,12},{12,8},{16,20},{20,16},{24,28},{28,24},{1,5},{5... | collective-permute-start | bytes 2064392 | tf_op jit(solution)/shard_map/ppermute | solution.py:170
  461.3 7.4 %collective-permute-start.24 = (bf16[128,768]{1,0:T(8,128)(2,1)S(1)}, bf16[128,768]{1,0:T(8,128)(2,1)S(1)}, u32[]{:S(2)}, u32[]{:S(2)}) collective-permute-start(bf16[128,768]{1,0:T(8,128)(2,1)S(1)} %get-tuple-element.113), channel_id=1, source_target_pairs={{0,1},{1,0},{2,3},{3,2},{4,5},{5,4},{6,7},{7,6},{8,9},{9,8},{10,11... | collective-permute-start | bytes 589832 | tf_op jit(solution)/shard_map/ppermute | solution.py:170
  461.4 7.3 %collective-permute-start.25 = (bf16[128,768]{1,0:T(8,128)(2,1)S(1)}, bf16[128,768]{1,0:T(8,128)(2,1)S(1)}, u32[]{:S(2)}, u32[]{:S(2)}) collective-permute-start(bf16[128,768]{1,0:T(8,128)(2,1)S(1)} %get-tuple-element.113), channel_id=1, source_target_pairs={{0,2},{1,3},{2,0},{3,1},{4,6},{5,7},{6,4},{7,5},{8,10},{9,11},{10,... | collective-permute-start | bytes 589832 | tf_op jit(solution)/shard_map/ppermute | solution.py:170
  (91 other events, 1136.7 us)
Sparse Core Ops, SparseCore 0:
  227.1 28.9 all-gather.1

commit v2 on v1

--- a/solution.py
+++ b/solution.py
@@ -13,6 +13,8 @@
 BUCKETS = 32
 EPSILON = 1e-05
 ROWS = 16
+HEADS_T = 3
+MESH = pl.DeviceIdType.MESH
 
 
 def nt(a, b):
@@ -50,45 +52,395 @@
     )
 
 
-def attend_kernel(q_ref, k_ref, v_ref, rx_ref, ry_ref, tab_ref, p_ref, c_ref):
-    head = pl.program_id(0)
-    win = rx_ref.shape[0]
-    q = (q_ref[...].astype(jnp.float32).T * HD ** (-0.5)).astype(jnp.bfloat16)
-    s = nn(q, k_ref[...])
-    tab = jnp.broadcast_to(tab_ref[pl.ds(head, 1), :], (win, 128))
-    parts = []
-    for c in range(win // 128):
-        sl = slice(128 * c, 128 * c + 128)
-        bias_x = jnp.take_along_axis(tab, rx_ref[:, sl], axis=1)
-        bias_y = jnp.take_along_axis(tab, ry_ref[:, sl] + BUCKETS, axis=1)
-        parts.append(s[:, sl] + (bias_x + bias_y))
-    s = jnp.concatenate(parts, axis=1)
-    m = jnp.max(s, axis=1, keepdims=True)
-    e = jnp.exp(s - m)
-    p = e * (1.0 / jnp.sum(e, axis=1, keepdims=True))
-    p_ref[0] = p
-    c_ref[...] = nt(v_ref[...], p.astype(jnp.bfloat16)).astype(jnp.bfloat16)
-
-
-def attend(q, k, v, rel_x, rel_y, tab):
-    heads, win = tab.shape[0], rel_x.shape[0]
-    blk = pl.BlockSpec((HD, win), lambda h: (h, 0))
-    full = pl.BlockSpec((win, win), lambda h: (0, 0))
+def xor_index(index, bit):
+    return index + bit - 2 * bit * ((index // bit) % 2)
+
+
+def signal_peers(peers):
+    barrier = pltpu.get_barrier_semaphore()
+    for peer in peers:
+        pl.semaphore_signal(barrier, inc=1, device_id=peer, device_id_type=MESH)
+    pl.semaphore_wait(barrier, len(peers))
+
+
+def remote(src, dst, send, recv, peer):
+    return pltpu.make_async_remote_copy(
+        src_ref=src, dst_ref=dst, send_sem=send, recv_sem=recv, device_id=peer, device_id_type=MESH
+    )
+
+
+class Gather:
+    def __init__(self, own, place, rows, split, sems, slot, peers):
+        self.own, self.place, self.rows, self.split = own, place, rows, split
+        self.send, self.recv, self.here = sems
+        self.slot = slot
+        self.mate, self.across, self.beside, self.side = peers
+
+    def copy(self, name):
+        s = self.slot
+        half = self.rows // 2 if self.split else self.rows
+        mine = pl.ds(pl.multiple_of(self.side * half, half), half) if self.split else pl.ds(0, half)
+        yours = pl.ds(pl.multiple_of((1 - self.side) * half, half), half)
+        whole = pl.ds(0, self.rows)
+        if name == "here":
+            return pltpu.make_async_copy(self.own(whole), self.place(0, whole), self.here.at[s])
+        src, dst, peer, k = {
+            "mate": lambda: (self.own(whole), self.place(1, whole), self.mate, 0),
+            "across": lambda: (self.own(mine), self.place(2, mine), self.across, 1),
+            "pass": lambda: (self.place(2, mine), self.place(3, mine), self.mate, 2),
+            "beside": lambda: (self.place(2, mine), self.place(2, mine), self.beside, 3),
+            "pass_two": lambda: (self.place(2, yours), self.place(3, yours), self.mate, 4),
+        }[name]()
+        return remote(src, dst, self.send.at[s, k], self.recv.at[s, k], peer)
+
+    def start(self):
+        self.copy("across").start()
+        self.copy("mate").start()
+        self.copy("here").start()
+
+    def forward(self):
+        self.copy("across").wait_recv()
+        if self.split:
+            self.copy("beside").start()
+        self.copy("pass").start()
+
+    def forward_two(self):
+        if self.split:
+            self.copy("beside").wait_recv()
+            self.copy("pass_two").start()
+
+    def arrive_near(self):
+        self.copy("here").wait()
+        self.copy("mate").wait_recv()
+
+    def arrive_far(self):
+        self.copy("pass").wait_recv()
+        if self.split:
+            self.copy("pass_two").wait_recv()
+
+    def arrive(self):
+        self.arrive_near()
+        self.arrive_far()
+
+    def finish(self):
+        for name in ("mate", "across", "pass") + (("beside", "pass_two") if self.split else ()):
+            self.copy(name).wait_send()
+
+
+def waves(column, frequency, quarter):
+    angle = column * frequency
+    turns = jnp.floor(angle * (2.0 / math.pi) + 0.5)
+    rest = ((angle - turns * 1.5703125) - turns * 4.837512969970703125e-4) - turns * 7.549789948768648e-8
+    quadrant = turns.astype(jnp.int32) + quarter
+    z = rest * rest
+    sine = ((-1.9515295891e-4 * z + 8.3321608736e-3) * z - 1.6666654611e-1) * z * rest + rest
+    cosine = ((2.443315711809948e-5 * z - 1.388731625493765e-3) * z + 4.166664568298827e-2) * z * z - 0.5 * z + 1.0
+    value = jnp.where(quadrant % 2 == 1, cosine, sine)
+    return jnp.where((quadrant // 2) % 2 == 1, -value, value)
+
+
+def gelu(v):
+    return 0.5 * v * (1.0 + jnp.tanh(math.sqrt(2.0 / math.pi) * (v + 0.044715 * (v * v * v))))
+
+
+def forward_kernel(
+    tok_ref, box_ref, rx_ref, ry_ref, mask_ref, cot_ref, freq_ref, lay_ref, vec_ref,
+    cols_own, rows_own, qkv_own, wo_own, w1_own, w2_own,
+    probs_out, qkvt_out, ctxt_out, low_out, feat_out, unit_out, inv_out, nlow_out, pre_out, hid_out,
+    block_out, dres_out, sums_out, wqkv_out, wo_out, w1_out, w2_out,
+    wqkv, wo, w1, w2, cols, rows, tabs, layer_in, qkvt, pbuf, ctxt, ctx, normed, pre, hid, acc,
+    send, recv, here, out_sem, p_sem,
+):
+    t, d = lax.axis_index("tensor"), lax.axis_index("dp")
+    mate, across = {"tensor": xor_index(t, 1)}, {"tensor": xor_index(t, 2)}
+    beside = {"dp": xor_index(d, 1)}
+    peers = (mate, across, beside, d % 2)
+    win, model = tok_ref.shape
+    heads = 4 * HEADS_T
+    cols_t = HEADS_T * HD
+    sems = (send, recv, here)
+    f32, bf16 = jnp.float32, jnp.bfloat16
+
+    def chunk(slot, own, place, count, split=True):
+        return Gather(own, place, count, split, sems, slot, peers)
+
+    g_cols = chunk(0, lambda s: cols_own.at[s], lambda r, s: cols.at[r, s], cols_t, False)
+    g_rows = chunk(1, lambda s: rows_own.at[s], lambda r, s: rows.at[r, s], 8, False)
+
+    def piece_rows(r, s, count):
+        return pl.ds(pl.multiple_of(r * count + s.start, 16), s.size)
+
+    g_qkv = [
+        chunk(
+            2 + n,
+            lambda s, n=n: qkv_own.at[n, s],
+            lambda r, s, n=n: wqkv.at[n, piece_rows(r, s, cols_t)],
+            cols_t,
+        )
+        for n in range(3)
+    ]
+    g_wo = chunk(5, lambda s: wo_own.at[s], lambda r, s: wo.at[piece_rows(r, s, cols_t)], cols_t)
+
+    def part(slot, own, whole, half):
+        count = own.shape[0] // 2
+
+        def moved(s):
+            return pl.ds(pl.multiple_of(s.start + half * count, 16), s.size)
+
+        return chunk(slot, lambda s: own.at[moved(s)], lambda r, s: whole.at[r, moved(s)], count)
+
+    g_w1 = [part(6 + h, w1_own, w1, h) for h in range(2)]
+    g_w2 = [part(8 + h, w2_own, w2, h) for h in range(2)]
+    everything = [g_cols, g_rows] + g_qkv + [g_wo] + g_w1 + g_w2
+
+    signal_peers((mate, across, beside))
+    for g in [g_cols, g_rows] + g_qkv:
+        g.start()
+
+    lane = lax.broadcasted_iota(jnp.int32, (1, 128), 1)
+    quarter = jnp.where(lane >= LFREQ, 1, 0)
+    block = 128
+
+    @pl.loop(0, win // block)
+    def _(i):
+        sl = pl.ds(pl.multiple_of(i * block, block), block)
+        box = box_ref[sl, :].astype(f32)
+        for m in range(4):
+            feat_out[sl, 2 * LFREQ * m : 2 * LFREQ * (m + 1)] = waves(
+                box[:, m : m + 1], freq_ref[0:1, :], quarter
+            ).astype(bf16)
+        value = tok_ref[sl, :].astype(f32) + nn(feat_out[sl, :], lay_ref[...])
+        layer_in[sl, :] = value
+        low_out[sl, :] = value.astype(bf16)
+
+    for g in [g_cols, g_rows] + g_qkv:
+        g.forward()
+    g_wo.start()
+    g_w1[0].start()
+    for g in g_qkv:
+        g.forward_two()
+    g_cols.arrive()
+    g_rows.arrive()
+    for r in range(4):
+        tabs[HEADS_T * r : HEADS_T * (r + 1), :] = rows[r, 1 : 1 + HEADS_T, 0:128]
+
+    for n in range(3):
+        g_qkv[n].arrive()
+
+        @pl.loop(0, 4)
+        def _(r, n=n):
+            sl = pl.ds(pl.multiple_of(r * cols_t, 16), cols_t)
+            value = nt(wqkv[n, sl, :], low_out[...])
+            qkvt[n, sl, :] = (value + cols[r, :, n : n + 1]).astype(bf16)
+
+    def table_row(h):
+        return (tabs[pl.ds(h, 1), :] * 2048.0 + 32768.5).astype(jnp.int32) - 32768
+
+    def p_copy(i, slot):
+        return pltpu.make_async_copy(pbuf.at[slot], probs_out.at[pl.ds(2 * i, 2)], p_sem.at[slot])
+
+    @pl.loop(0, heads // 2)
+    def _(i):
+        slot = i % 2
+        sl = pl.ds(pl.multiple_of(i * 2 * HD, 2 * HD), 2 * HD)
+        q = (qkvt[0, sl, :].astype(f32).T * HD ** (-0.5)).astype(bf16)
+        tab = jnp.broadcast_to((table_row(2 * i) << 16) + table_row(2 * i + 1), (win, 128))
+        bias = ([], [])
+        for c in range(win // 128):
+            at = slice(128 * c, 128 * c + 128)
+            word = jnp.take_along_axis(tab, rx_ref[:, at], axis=1) + jnp.take_along_axis(
+                tab, ry_ref[:, at] + BUCKETS, axis=1
+            )
+            second = word << 16
+            bias[0].append((word - (second >> 16)).astype(f32) * 2.0**-27)
+            bias[1].append(second.astype(f32) * 2.0**-27)
+
+        @pl.when(i >= 2)
+        def _():
+            p_copy(i - 2, slot).wait()
+
+        for u in range(2):
+            rows_u = pl.ds(pl.multiple_of(i * 2 * HD + u * HD, HD), HD)
+            s = nn(q[:, u * HD : (u + 1) * HD], qkvt[1, rows_u, :]) + jnp.concatenate(bias[u], axis=1)
+            m = jnp.max(s, axis=1, keepdims=True)
+            e = jnp.exp(s - m)
+            p = e * (1.0 / jnp.sum(e, axis=1, keepdims=True))
+            pbuf[slot, u] = p
+            ctxt[rows_u, :] = nt(qkvt[2, rows_u, :], p.astype(bf16)).astype(bf16)
+        p_copy(i, slot).start()
+
+        @pl.when(i == 0)
+        def _():
+            g_wo.forward()
+            g_w1[1].start()
+
+        @pl.when(i == 1)
+        def _():
+            g_w1[0].forward()
+            g_wo.forward_two()
+            g_w2[0].start()
+
+        @pl.when(i == 2)
+        def _():
+            g_w2[1].start()
+
+        @pl.when(i == 3)
+        def _():
+            g_w1[1].forward()
+            g_w1[0].forward_two()
+
+        @pl.when(i == 5)
+        def _():
+            g_w2[0].forward()
+            g_w1[1].forward_two()
+
+    last = heads // 2
+    outs = [
+        (qkvt, qkvt_out), (ctxt, ctxt_out), (wqkv, wqkv_out),
+    ]
+    done = []
+
+    def leave(src, dst):
+        c = pltpu.make_async_copy(src, dst, out_sem.at[len(done)])
+        c.start()
+        done.append(c)
+
+    for src, dst in outs:
+        leave(src, dst)
+    g_wo.arrive()
+    leave(wo, wo_out)
+
+    ctx[...] = ctxt[...].astype(f32).T.astype(bf16)
+
+    @pl.loop(0, win // block)
+    def _(i):
+        sl = pl.ds(pl.multiple_of(i * block, block), block)
+        value = layer_in[sl, :] + nn(ctx[sl, :], wo[...]) + vec_ref[0:1, :]
+        mean = jnp.mean(value, axis=1, keepdims=True)
+        centered = value - mean
+        inverse = lax.rsqrt(jnp.mean(centered * centered, axis=1, keepdims=True) + EPSILON)
+        unit = centered * inverse
+        unit_out[sl, :] = unit
+        inv_out[sl, :] = inverse
+        value = unit * vec_ref[1:2, :] + vec_ref[2:3, :]
+        normed[sl, :] = value
+        nlow_out[sl, :] = value.astype(bf16)
+
+    g_w2[0].forward_two()
+    g_w2[1].forward()
+    for r in range(4):
+        if r == 0:
+            for g in g_w1 + g_w2:
+                g.arrive_near()
+        if r == 2:
+            g_w2[1].forward_two()
+            for g in g_w1 + g_w2:
+                g.arrive_far()
+            leave(w1, w1_out)
+            leave(w2, w2_out)
+
+        @pl.loop(0, win // 256)
+        def _(i, r=r):
+            sl = pl.ds(pl.multiple_of(i * 256, 256), 256)
+            value = nn(nlow_out[sl, :], w1[r]) + rows[r, 0:1, :]
+            pre[r, sl, :] = value
+            low_hid = gelu(value).astype(bf16)
+            hid[r, sl, :] = low_hid
+            more = nn(low_hid, w2[r])
+            acc[sl, :] = more if r == 0 else acc[sl, :] + more
+
+        leave(pre.at[r], pre_out.at[r])
+        leave(hid.at[r], hid_out.at[r])
+
+    sums_out[...] = jnp.zeros_like(sums_out)
+
+    @pl.loop(0, win // block)
+    def _(i):
+        sl = pl.ds(pl.multiple_of(i * block, block), block)
+        value = normed[sl, :] + acc[sl, :] + vec_ref[3:4, :]
+        mean = jnp.mean(value, axis=1, keepdims=True)
+        centered = value - mean
+        inverse = lax.rsqrt(jnp.mean(centered * centered, axis=1, keepdims=True) + EPSILON)
+        unit = centered * inverse
+        block_out[sl, :] = (unit * vec_ref[4:5, :] + vec_ref[5:6, :]).astype(bf16)
+        selected = mask_ref[sl, :].astype(f32) * cot_ref[sl, :].astype(f32)
+        scaled = selected * vec_ref[4:5, :]
+        mean_one = jnp.mean(scaled, axis=1, keepdims=True)
+        mean_two = jnp.mean(scaled * unit, axis=1, keepdims=True)
+        dres = (scaled - mean_one - unit * mean_two) * inverse
+        dres_out[sl, :] = dres
+        sums_out[0:1, :] += jnp.sum(selected * unit, axis=0, keepdims=True)
+        sums_out[1:2, :] += jnp.sum(selected, axis=0, keepdims=True)
+        sums_out[2:3, :] += jnp.sum(dres, axis=0, keepdims=True)
+
+    for i in (last - 2, last - 1):
+        p_copy(i, i % 2).wait()
+    for c in done:
+        c.wait()
+    for g in everything:
+        g.finish()
+
+
+def forward_window(n_dp, tok, box, rx, ry, mask, cot, freq, lay, vec, cols_own, rows_own, qkv_own, wo_own, w1_own, w2_own):
+    win, model = tok.shape
+    cols_t, hid_t = wo_own.shape[0], w1_own.shape[1]
+    heads = 4 * HEADS_T
+    f32, bf16 = jnp.float32, jnp.bfloat16
+    shape = jax.ShapeDtypeStruct
+    here = pl.BlockSpec(memory_space=pltpu.VMEM)
+    away = pl.BlockSpec(memory_space=pl.ANY)
+    outs = [
+        (shape((heads, win, win), f32), away),
+        (shape((3, model, win), bf16), away),
+        (shape((model, win), bf16), away),
+        (shape((win, model), bf16), here),
+        (shape((win, 8 * LFREQ), bf16), here),
+        (shape((win, model), f32), here),
+        (shape((win, 1), f32), here),
+        (shape((win, model), bf16), here),
+        (shape((4, win, hid_t), f32), away),
+        (shape((4, win, hid_t), bf16), away),
+        (shape((win, model), bf16), here),
+        (shape((win, model), f32), here),
+        (shape((8, model), f32), here),
+        (shape((3, model, model), bf16), away),
+        (shape((model, model), bf16), away),
+        (shape((4, model, hid_t), bf16), away),
+        (shape((4, hid_t, model), bf16), away),
+    ]
     return pl.pallas_call(
-        attend_kernel,
-        grid=(heads,),
-        in_specs=[blk, blk, blk, full, full, pl.BlockSpec(tab.shape, lambda h: (0, 0))],
-        out_specs=[pl.BlockSpec((1, win, win), lambda h: (h, 0, 0)), blk],
-        out_shape=[
-            jax.ShapeDtypeStruct((heads, win, win), jnp.float32),
-            jax.ShapeDtypeStruct((heads * HD, win), jnp.bfloat16),
+        forward_kernel,
+        in_specs=[here] * 9 + [away] * 6,
+        out_specs=[spec for _, spec in outs],
+        out_shape=[s for s, _ in outs],
+        scratch_shapes=[
+            pltpu.VMEM((3, model, model), bf16),
+            pltpu.VMEM((model, model), bf16),
+            pltpu.VMEM((4, model, hid_t), bf16),
+            pltpu.VMEM((4, hid_t, model), bf16),
+            pltpu.VMEM((4, cols_t, 128), f32),
+            pltpu.VMEM((4, 8, model), f32),
+            pltpu.VMEM((heads, 128), f32),
+            pltpu.VMEM((win, model), f32),
+            pltpu.VMEM((3, model, win), bf16),
+            pltpu.VMEM((2, 2, win, win), f32),
+            pltpu.VMEM((model, win), bf16),
+            pltpu.VMEM((win, model), bf16),
+            pltpu.VMEM((win, model), f32),
+            pltpu.VMEM((4, win, hid_t), f32),
+            pltpu.VMEM((4, win, hid_t), bf16),
+            pltpu.VMEM((win, model), f32),
+            pltpu.SemaphoreType.DMA((10, 5)),
+            pltpu.SemaphoreType.DMA((10, 5)),
+            pltpu.SemaphoreType.DMA((10,)),
+            pltpu.SemaphoreType.DMA((16,)),
+            pltpu.SemaphoreType.DMA((2,)),
         ],
-        compiler_params=pltpu.CompilerParams(vmem_limit_bytes=48 * 2**20),
-        cost_estimate=pl.CostEstimate(
-            flops=16 * 10**9, bytes_accessed=20 * 10**6, transcendentals=heads * win * win
+        compiler_params=pltpu.CompilerParams(
+            vmem_limit_bytes=60 * 2**20, collective_id=0, has_side_effects=True
         ),
-        name="attend",
-    )(q, k, v, rel_x, rel_y, tab)
+        name="forward_window",
+    )(tok, box, rx, ry, mask, cot, freq, lay, vec, cols_own, rows_own, qkv_own, wo_own, w1_own, w2_own)
 
 
 def attend_back_kernel(
@@ -238,57 +590,46 @@
     def mine(whole):
         return lax.dynamic_slice_in_dim(whole, me * (whole.shape[0] // n_t), whole.shape[0] // n_t)
 
-    qkv_rows = jnp.transpose(qkv_weight, (0, 2, 1))
-    small_own = jnp.concatenate(
-        [qv_bias.reshape(-1), ffn_in_bias, bias_table.T.astype(jnp.float32).reshape(-1)]
-    )
-    small_all = gather_pieces(small_own, "tensor", n_t)
-    qkv_all = gather_pieces(qkv_rows, "tensor", n_t)
-    rest_all = gather_pieces(
-        jnp.concatenate([out_weight, ffn_in_weight.T, ffn_out_weight], axis=0), "tensor", n_t
-    )
-    wqkv = [jnp.concatenate([piece[n] for piece in qkv_all], axis=0) for n in range(3)]
-    wo = jnp.concatenate([piece[:cols_t] for piece in rest_all], axis=0)
-    w1 = jnp.concatenate([piece[cols_t : cols_t + hid_t] for piece in rest_all], axis=0)
-    w2 = jnp.concatenate([piece[cols_t + hid_t :] for piece in rest_all], axis=0)
-    bq = jnp.concatenate([piece[:cols_t] for piece in small_all])
-    bv = jnp.concatenate([piece[cols_t : 2 * cols_t] for piece in small_all])
-    b1 = jnp.concatenate([piece[2 * cols_t : 2 * cols_t + hid_t] for piece in small_all])
-    table = jnp.concatenate(
-        [piece[2 * cols_t + hid_t :].reshape(heads_t, 2 * BUCKETS) for piece in small_all]
-    )
-    table = jnp.pad(table, ((0, 0), (0, 128 - 2 * BUCKETS)))
-
+    zeros = jnp.zeros((cols_t,), jnp.float32)
+    cols_own = jnp.pad(jnp.stack([qv_bias[0], zeros, qv_bias[1]], axis=1), ((0, 0), (0, 125)))
+    rows_own = jnp.concatenate(
+        [
+            ffn_in_bias[None, :],
+            jnp.pad(bias_table.T.astype(jnp.float32), ((0, 0), (0, hid_t - 2 * BUCKETS))),
+            jnp.zeros((8 - 1 - heads_t, hid_t), jnp.float32),
+        ],
+        axis=0,
+    )
+    freq_index = jnp.arange(LFREQ).astype(jnp.float32)
+    freq = jnp.exp(freq_index * (-math.log(1000.0) / LFREQ))
+    freq = jnp.broadcast_to(jnp.concatenate([freq, freq])[None, :], (8, 2 * LFREQ))
+    zero = jnp.zeros_like(out_bias)
+    vec = jnp.stack([out_bias, ln1_gain, ln1_bias, ffn_out_bias, ln2_gain, ln2_bias, zero, zero])
+    relx, rely = mine(rel_x)[0], mine(rel_y)[0]
     count = sum_small(jnp.sum(mask_tokens.astype(jnp.float32)).reshape(1), "dp", n_dp)[0]
 
-    features = layout_features(mine(box_coords)).astype(jnp.bfloat16)
-    layer_in = mine(tokens_in).astype(jnp.float32) + nn(features, layout_weight)
-    layer_low = layer_in.astype(jnp.bfloat16)
-    queries = (nt(wqkv[0], layer_low) + bq[:, None]).astype(jnp.bfloat16)
-    key_rows = nt(wqkv[1], layer_low).astype(jnp.bfloat16)
-    values = (nt(wqkv[2], layer_low) + bv[:, None]).astype(jnp.bfloat16)
-    relx, rely = mine(rel_x)[0], mine(rel_y)[0]
-    probs, context_t = attend(queries, key_rows, values, relx, rely, table)
-    context = context_t.T
-    residual = layer_in + nn(context, wo) + out_bias
-    normed, unit_one, inverse_one = normalize_keep(residual, ln1_gain, ln1_bias)
-    normed_low = normed.astype(jnp.bfloat16)
-    pre_act = nt(normed_low, w1) + b1
-    activated, gelu_back = jax.vjp(jax.nn.gelu, pre_act)
-    hidden = activated.astype(jnp.bfloat16)
-    residual_two = normed + nn(hidden, w2) + ffn_out_bias
-    output, unit_two, inverse_two = normalize_keep(residual_two, ln2_gain, ln2_bias)
-    block_out = lax.all_gather(output.astype(jnp.bfloat16), "tensor", axis=0, tiled=True)
-
-    selected = mine(mask_tokens).astype(jnp.float32)[:, None] * mine(cotangent).astype(jnp.float32)
-    dresid_two, grad_g2, grad_b2 = normalize_back(selected, unit_two, inverse_two, ln2_gain)
+    (
+        probs, qkvt, context_t, layer_low, features, unit_one, inverse_one, normed_low, pre_all, hid_all,
+        block_own, dresid_two, sums, wqkv, wo, w1, w2,
+    ) = forward_window(
+        n_dp, mine(tokens_in), mine(box_coords), relx, rely, mine(mask_tokens)[:, None], mine(cotangent), freq,
+        layout_weight, vec, cols_own, rows_own, jnp.transpose(qkv_weight, (0, 2, 1)), out_weight, ffn_in_weight, ffn_out_weight,
+    )
+    queries, key_rows, values = qkvt[0], qkvt[1], qkvt[2]
+    block_out = lax.all_gather(block_own, "tensor", axis=0, tiled=True)
+    grad_g2, grad_b2, grad_c2 = sums[0], sums[1], sums[2]
     dffn_low = dresid_two.astype(jnp.bfloat16)
-    grad_c2 = jnp.sum(dresid_two, axis=0)
-    grad_w2 = nn(hidden.T, dffn_low)
-    dpre_act = gelu_back(nt(dffn_low, w2))[0].astype(jnp.bfloat16)
-    grad_c1 = jnp.sum(dpre_act, axis=0, dtype=jnp.float32)
-    grad_w1 = nn(dpre_act.T, normed_low)
-    dnormed = dresid_two + nn(dpre_act, w1)
+    grad_w2, grad_w1, grad_c1, dnormed = [], [], [], dresid_two
+    for r in range(n_t):
+        grad_w2.append(nn(hid_all[r].T, dffn_low))
+        gelu_back = jax.vjp(jax.nn.gelu, pre_all[r])[1]
+        dpre = gelu_back(nt(dffn_low, w2[r]))[0].astype(jnp.bfloat16)
+        grad_c1.append(jnp.sum(dpre, axis=0, dtype=jnp.float32))
+        grad_w1.append(nn(normed_low.T, dpre))
+        dnormed = dnormed + nt(dpre, w1[r])
+    grad_w2 = jnp.concatenate(grad_w2, axis=0)
+    grad_w1 = jnp.concatenate(grad_w1, axis=0)
+    grad_c1 = jnp.concatenate(grad_c1)
     dresidual, grad_g1, grad_b1 = normalize_back(dnormed, unit_one, inverse_one, ln1_gain)
 
     def reduced(parts):
@@ -361,7 +702,7 @@
         common[0] * factor[1],
         common[1] * factor[2],
         common[2] * factor[2],
-        w1_sum.T.astype(f32) * factor[3],
+        w1_sum.astype(f32) * factor[3],
         own[2 * cols_t : 2 * cols_t + hid_t] * factor[3],
         w2_sum.astype(f32) * factor[4],
         common[3] * factor[4],

time: 488 us -> 457 us (0.936)
  waiting for transfers between devices: 193 us -> 140 us
  Pallas kernels: 59.7 us -> 104 us
  matrix products: 71 us -> 59.5 us
  other arithmetic: 47 us -> 37.7 us
  starting transfers between devices: 50 us -> 44.2 us
    ppermute x50 -> x41, waiting for transfers between devices: 193 us -> 140 us  [swap(): return lax.ppermute(value, axis, [(i, i ^ bit) for i in range(size)])]
    pallas_call x1, Pallas kernels: 27.7 us -> 71.9 us  [forward_window(): pl.pallas_call(forward_kernel, in_specs=[here] * 9 + [away] * 6, out_spec...]
    dot_general x6 -> x9, matrix products: 26.1 us -> 18.9 us  [nt(): lax.dot_general(a, b, (((1,), (1,)), ((), ())), preferred_element_type=jn...]
    slice x15 -> x1, local copies, waits for them, and re-layouts: 7.38 us -> 0.88 us  [local(): grad_g2, grad_b2, grad_c2 = (sums[0], sums[1], sums[2])]
    ppermute x50 -> x41, starting transfers between devices: 50 us -> 44.2 us  [swap(): return lax.ppermute(value, axis, [(i, i ^ bit) for i in range(size)])]
    another operation x0 -> x11, local copies, waits for them, and re-layouts: none -> 5.73 us  [the longest x8 4.77 us: local(): jnp.stack([out_bias, ln1_gain, ln1_bias, ffn_out_bias, ln2_gain, ln2_bias...]
    dot_general x14 -> x16, matrix products: 44.9 us -> 40.6 us  [nn(): return jnp.dot(a, b, preferred_element_type=jnp.float32)]
    unnamed x195 -> x110, local copies, waits for them, and re-layouts: 17.3 us -> 19 us
  transfers between devices with their start and end apart: 51 -> 42, of which waited for: 25 -> 21; matrix products, arithmetic and copies ran while one was open for 17% -> 25% of each run, Pallas kernels for 6% -> 7%
where the time goes in v2:
time: 457 us; the launch traced here: 449 us
  waiting for transfers between devices  140 us (31%)
  Pallas kernels  104 us (23%)
  matrix products  59.5 us (13%)
  local copies, waits for them, and re-layouts  46.3 us (10%)
  starting transfers between devices  44.2 us (10%)
  other arithmetic  37.7 us (8%)
  between operations  18 us (4%)
    ppermute x41, waiting for transfers between devices, swap(): return lax.ppermute(value, axis, [(i, i ^ bit) for i in range(size)])  140 us
    pallas_call x1, Pallas kernels, forward_window(): pl.pallas_call(forward_kernel, in_specs=[here] * 9 + [away] * 6, out_spec...  71.9 us
    ppermute x41, starting transfers between devices, swap(): return lax.ppermute(value, axis, [(i, i ^ bit) for i in range(size)])  44.2 us
    dot_general x16, matrix products, nn(): return jnp.dot(a, b, preferred_element_type=jnp.float32)  40.6 us
    pallas_call x1, Pallas kernels, attend_back(): pl.pallas_call(attend_back_kernel, grid=(heads,), in_specs=[blk, blk, blk...  31.9 us
    unnamed x110, local copies, waits for them, and re-layouts  19 us
    dot_general x9, matrix products, nt(): lax.dot_general(a, b, (((1,), (1,)), ((), ())), preferred_element_type=jn...  18.9 us
  transfers between devices with their start and end apart: 42, of which 21 were waited for; matrix products, arithmetic and copies ran while one was open for 25% of the time, Pallas kernels for 7%

profile of v2, /device:TPU:0, one launch (start us, length us, event | category | flops | bytes accessed | tf_op | source)
XLA Modules:
  0.0 449.2 jit_solution(8090445679414913558)
XLA Ops:
  17.8 2.6 constant_dynamic-slice_fusion
  20.4 3.0 dynamic-slice_bitcast_fusion
  25.3 71.9 %forward_window.1 = (f32[12,512,512]{2,1,0:T(8,128)}, bf16[3,768,512]{2,1,0:T(8,128)(2,1)}, bf16[768,512]{1,0:T(8,128)(2,1)}, bf16[512,768]{1,0:T(8,128)(2,1)}, ...) custom-call(bf16[512,768]{1,0:T(8,128)(2,1)} %get-tuple-element.134., ...), custom_call_target="tpu_custom_call" | custom-call | tf_op jit(solution)/shard_map/forward_window/pallas_call | solution.py:411
  98.7 3.3 convolution_convert_fusion
  103.6 3.2 convolution_convert_fusion.1
  108.6 3.0 convert_reduce_fusion
  118.5 2.3 fusion.58
  120.8 2.2 fusion.52
  123.0 2.2 fusion.46
  125.3 2.8 multiply_reduce_fusion
  132.8 31.9 %attend_back.1 = (bf16[768,512]{1,0:T(8,128)(2,1)}, bf16[768,512]{1,0:T(8,128)(2,1)}, bf16[768,512]{1,0:T(8,128)(2,1)}, f32[12,1024]{1,0:T(8,128)}) custom-call(bf16[768,512]{1,0:T(8,128)(2,1)} %get-tuple-element.79.q_ref, bf16[768,512]{1,0:T(8,128)(2,1)} %get-tuple-element.78.k_ref, bf16[768,512]{1,0:T(8,128)(2,1)} %get-tuple-element.77.v_ref, ...), custom_call_target="tpu_custom_call" | custom-call | flops 20000000000 | bytes 20000000 | tf_op jit(solution)/shard_map/attend_back/pallas_call | solution.py:496
  169.7 3.5 fusion.81
  176.2 2.6 fusion.98
  178.8 2.6 fusion.100
  181.3 2.6 fusion.99
  190.0 4.2 fusion.101
  195.3 2.1 slice_dynamic-update-slice_fusion.14
  197.4 2.1 slice_dynamic-update-slice_fusion.13
  204.5 2.9 collective-permute-start.1
  208.7 3.9 collective-permute-start.2
  215.6 3.2 constant_dynamic-update-slice_fusion.8
  222.0 3.3 add_convert_fusion.1
  228.6 3.2 collective-permute-done.20
  235.8 2.6 collective-permute-start.22
  241.3 3.1 add_convert_fusion.2
  245.2 3.5 add_convert_fusion
  249.9 4.6 %collective-permute-done.34 = bf16[768,768]{1,0:T(8,128)(2,1)} collective-permute-done((bf16[768,768]{1,0:T(8,128)(2,1)}, bf16[768,768]{1,0:T(8,128)(2,1)}, u32[]{:S(2)}, u32[]{:S(2)}) %collective-permute-start.34) | collective-permute-done | bytes 1179680 | tf_op jit(solution)/shard_map/ppermute | solution.py:522
  257.2 3.8 slice_multiply_fusion
  260.9 2.9 convert_add_fusion.1
  263.9 32.6 %collective-permute-done.4 = bf16[512,768]{1,0:T(8,128)(2,1)S(1)} collective-permute-done((bf16[512,768]{1,0:T(8,128)(2,1)}, bf16[512,768]{1,0:T(8,128)(2,1)S(1)}, u32[]{:S(2)}, u32[]{:S(2)}) %collective-permute-start.4) | collective-permute-done | bytes 786464 | tf_op jit(solution)/shard_map/ppermute | solution.py:522
  301.2 23.8 %collective-permute-done.8 = bf16[896,768]{1,0:T(8,128)(2,1)} collective-permute-done((bf16[896,768]{1,0:T(8,128)(2,1)}, bf16[896,768]{1,0:T(8,128)(2,1)}, u32[]{:S(2)}, u32[]{:S(2)}) %collective-permute-start.8) | collective-permute-done | bytes 1376288 | tf_op jit(solution)/shard_map/ppermute | solution.py:522
  325.0 2.9 convert_add_fusion
  331.7 9.3 %collective-permute-done.36 = bf16[192,768]{1,0:T(8,128)(2,1)S(1)} collective-permute-done((bf16[192,768]{1,0:T(8,128)(2,1)S(1)}, bf16[192,768]{1,0:T(8,128)(2,1)S(1)}, u32[]{:S(2)}, u32[]{:S(2)}) %collective-permute-start.36) | collective-permute-done | bytes 294944 | tf_op jit(solution)/shard_map/ppermute | solution.py:522
  346.8 2.6 collective-permute-start.28
  350.1 10.6 %collective-permute-done.10 = bf16[224,768]{1,0:T(8,128)(2,1)S(1)} collective-permute-done((bf16[224,768]{1,0:T(8,128)(2,1)S(1)}, bf16[224,768]{1,0:T(8,128)(2,1)S(1)}, u32[]{:S(2)}, u32[]{:S(2)}) %collective-permute-start.10) | collective-permute-done | bytes 344096 | tf_op jit(solution)/shard_map/ppermute | solution.py:522
  363.9 10.3 %collective-permute-done.11 = bf16[112,768]{1,0:T(8,128)(2,1)S(1)} collective-permute-done((bf16[112,768]{1,0:T(8,128)(2,1)S(1)}, bf16[112,768]{1,0:T(8,128)(2,1)S(1)}, u32[]{:S(2)}, u32[]{:S(2)}) %collective-permute-start.11) | collective-permute-done | bytes 172064 | tf_op jit(solution)/shard_map/ppermute | solution.py:522
  374.4 2.2 collective-permute-start.39
  376.5 3.2 collective-permute-done.29
  379.9 4.2 collective-permute-done.12
  385.5 2.4 collective-permute-done.39
  389.3 4.9 %collective-permute-done.30 = bf16[192,768]{1,0:T(8,128)(2,1)S(1)} collective-permute-done((bf16[192,768]{1,0:T(8,128)(2,1)S(1)}, bf16[192,768]{1,0:T(8,128)(2,1)S(1)}, u32[]{:S(2)}, u32[]{:S(2)}) %collective-permute-start.30) | collective-permute-done | bytes 294944 | tf_op jit(solution)/shard_map/ppermute | solution.py:522
  395.6 4.9 %collective-permute-done.13 = bf16[224,768]{1,0:T(8,128)(2,1)S(1)} collective-permute-done((bf16[224,768]{1,0:T(8,128)(2,1)S(1)}, bf16[224,768]{1,0:T(8,128)(2,1)S(1)}, u32[]{:S(2)}, u32[]{:S(2)}) %collective-permute-start.13) | collective-permute-done | bytes 344096 | tf_op jit(solution)/shard_map/ppermute | solution.py:522
  404.5 3.2 convert_element_type.205
  407.7 2.3 convert_multiply_fusion
  410.1 7.0 %collective-permute-done.31 = bf16[384,768]{1,0:T(8,128)(2,1)S(1)} collective-permute-done((bf16[384,768]{1,0:T(8,128)(2,1)S(1)}, bf16[384,768]{1,0:T(8,128)(2,1)S(1)}, u32[]{:S(2)}, u32[]{:S(2)}) %collective-permute-start.31) | collective-permute-done | bytes 589856 | tf_op jit(solution)/shard_map/ppermute | solution.py:522
  417.1 2.3 convert_multiply_fusion.1
  419.3 9.5 %collective-permute-done.14 = bf16[448,768]{1,0:T(8,128)(2,1)S(1)} collective-permute-done((bf16[448,768]{1,0:T(8,128)(2,1)S(1)}, bf16[448,768]{1,0:T(8,128)(2,1)S(1)}, u32[]{:S(2)}, u32[]{:S(2)}) %collective-permute-start.14) | collective-permute-done | bytes 688160 | tf_op jit(solution)/shard_map/ppermute | solution.py:522
  434.3 2.6 collective-permute-done.16
  (286 shorter events, 105.5 us)
Async XLA Ops:
  7.2 412.1 %all-gather.2.cloned.1.call-start = ((), (), s32[]{:S(2)}) async-start(), calls=%async_computation | async-start | bytes 3932160 | tf_op jit(solution)/shard_map/all_gather | solution.py:619
  98.7 18.1 %copy-start.17 = (bf16[512,768]{1,0:T(8,128)(2,1)}, bf16[512,768]{1,0:T(8,128)(2,1)S(1)}, u32[]{:S(2)}) copy-start(bf16[512,768]{1,0:T(8,128)(2,1)S(1)} %convert_element_type.196) | copy-start | bytes 2359300
  102.0 120.0 %collective-permute-start.33 = (bf16[768,768]{1,0:T(8,128)(2,1)}, bf16[768,768]{1,0:T(8,128)(2,1)}, u32[]{:S(2)}, u32[]{:S(2)}) collective-permute-start(bf16[768,768]{1,0:T(8,128)(2,1)} %convolution_convert_fusion), channel_id=1, source_target_pairs={{0,1},{1,0},{2,3},{3,2},{4,5},{5,4},{6,7},{7,6},{8,9},{9,8},{10,11... | collective-permute-start | bytes 3538952 | tf_op jit(solution)/shard_map/ppermute | solution.py:522
  103.6 10.0 %slice-start = ((s8[4718592]{0:T(1024)(128)(4,1)}), s8[4194304]{0:T(1024)(128)(4,1)S(1)}, s32[]{:S(2)}) async-start(s8[4718592]{0:T(1024)(128)(4,1)} %bitcast.185), calls=%async_computation.1 | async-start | bytes 8388608
  106.7 142.0 %collective-permute-start.32 = (bf16[768,768]{1,0:T(8,128)(2,1)}, bf16[768,768]{1,0:T(8,128)(2,1)}, u32[]{:S(2)}, u32[]{:S(2)}) collective-permute-start(bf16[768,768]{1,0:T(8,128)(2,1)} %convolution_convert_fusion.1), channel_id=1, source_target_pairs={{0,1},{1,0},{2,3},{3,2},{4,5},{5,4},{6,7},{7,6},{8,9},{9,8},{10,11... | collective-permute-start | bytes 3538952 | tf_op jit(solution)/shard_map/ppermute | solution.py:522
  107.4 95.8 %collective-permute-start = (f32[1]{0:T(128)}, f32[1]{0:T(128)}, u32[]{:S(2)}, u32[]{:S(2)}) collective-permute-start(f32[1]{0:T(128)} %bitcast.25), channel_id=1, source_target_pairs={{0,4},{4,0},{8,12},{12,8},{16,20},{20,16},{24,28},{28,24},{1,5},{5... | collective-permute-start | bytes 20 | tf_op jit(solution)/shard_map/ppermute | solution.py:522
  113.4 127.3 %collective-permute-start.24 = (bf16[768,768]{1,0:T(8,128)(2,1)}, bf16[768,768]{1,0:T(8,128)(2,1)}, u32[]{:S(2)}, u32[]{:S(2)}) collective-permute-start(bf16[768,768]{1,0:T(8,128)(2,1)} %convolution_convert_fusion.2), channel_id=1, source_target_pairs={{0,1},{1,0},{2,3},{3,2},{4,5},{5,4},{6,7},{7,6},{8,9},{9,8},{10,11... | collective-permute-start | bytes 3538952 | tf_op jit(solution)/shard_map/ppermute | solution.py:522
  169.3 51.3 %collective-permute-start.18 = (f32[9984]{0:T(1024)S(1)}, f32[9984]{0:T(1024)S(1)}, u32[]{:S(2)}, u32[]{:S(2)}) collective-permute-start(f32[9984]{0:T(1024)S(1)} %constant_dynamic-update-slice_fusion.9), channel_id=1, source_target_pairs={{0,1},{1,0},{2,3},{3,2},{4,5},{5,4},{6,7},{7,6},{8,9},{9,8},{10,11... | collective-permute-start | bytes 119816 | tf_op jit(solution)/shard_map/ppermute | solution.py:522
  200.6 13.4 %copy-start.44 = (f32[512,768]{1,0:T(8,128)S(1)}, f32[512,768]{1,0:T(8,128)}, u32[]{:S(2)}) copy-start(f32[512,768]{1,0:T(8,128)} %fusion.39) | copy-start | bytes 4718596
  204.5 3.6 collective-permute-start.1
  208.7 4.5 collective-permute-start.2
  220.6 23.8 %collective-permute-start.7 = (bf16[896,768]{1,0:T(8,128)(2,1)}, bf16[896,768]{1,0:T(8,128)(2,1)}, u32[]{:S(2)}, u32[]{:S(2)}) collective-permute-start(bf16[896,768]{1,0:T(8,128)(2,1)} %get-tuple-element.81), channel_id=1, source_target_pairs={{0,1},{1,0},{2,3},{3,2},{4,5},{5,4},{6,7},{7,6},{8,9},{9,8},{10,11... | collective-permute-start | bytes 4128776 | tf_op jit(solution)/shard_map/ppermute | solution.py:522
  221.1 6.5 %collective-permute-start.19 = (f32[9984]{0:T(1024)S(1)}, f32[9984]{0:T(1024)S(1)}, u32[]{:S(2)}, u32[]{:S(2)}) collective-permute-start(f32[9984]{0:T(1024)S(1)} %add.295), channel_id=1, source_target_pairs={{0,2},{1,3},{2,0},{3,1},{4,6},{5,7},{6,4},{7,5},{8,10},{9,11},{10,... | collective-permute-start | bytes 119816 | tf_op jit(solution)/shard_map/ppermute | solution.py:522
  225.3 29.2 %collective-permute-start.34 = (bf16[768,768]{1,0:T(8,128)(2,1)}, bf16[768,768]{1,0:T(8,128)(2,1)}, u32[]{:S(2)}, u32[]{:S(2)}) collective-permute-start(bf16[768,768]{1,0:T(8,128)(2,1)} %add_convert_fusion.1), channel_id=1, source_target_pairs={{0,2},{1,3},{2,0},{3,1},{4,6},{5,7},{6,4},{7,5},{8,10},{9,11},{10,... | collective-permute-start | bytes 3538952 | tf_op jit(solution)/shard_map/ppermute | solution.py:522
  227.7 13.6 %copy-start.24 = (bf16[512,768]{1,0:T(8,128)(2,1)S(1)}, bf16[512,768]{1,0:T(8,128)(2,1)}, u32[]{:S(2)}) copy-start(bf16[512,768]{1,0:T(8,128)(2,1)} %get-tuple-element.56) | copy-start | bytes 2359300
  227.7 13.6 %copy-start.40 = (bf16[512,768]{1,0:T(8,128)(2,1)S(1)}, bf16[512,768]{1,0:T(8,128)(2,1)}, u32[]{:S(2)}) copy-start(bf16[512,768]{1,0:T(8,128)(2,1)} %copy-done.39) | copy-start | bytes 2359300
  227.7 4.1 collective-permute-start.20
  231.8 4.0 collective-permute-start.21
  235.8 4.9 %collective-permute-start.22 = (f32[9984]{0:T(1024)S(1)}, f32[9984]{0:T(1024)S(1)}, u32[]{:S(2)}, u32[]{:S(2)}) collective-permute-start(f32[9984]{0:T(1024)S(1)} %add.298), channel_id=1, source_target_pairs={{0,16},{4,20},{8,24},{12,28},{16,0},{20,4},{24,8},{28,12},{1,17},{... | collective-permute-start | bytes 119816 | tf_op jit(solution)/shard_map/ppermute | solution.py:522
  240.7 55.9 %collective-permute-start.23 = (bf16[768,768]{1,0:T(8,128)(2,1)}, bf16[768,768]{1,0:T(8,128)(2,1)}, u32[]{:S(2)}, u32[]{:S(2)}) collective-permute-start(bf16[768,768]{1,0:T(8,128)(2,1)} %convolution_convert_fusion.3), channel_id=1, source_target_pairs={{0,1},{1,0},{2,3},{3,2},{4,5},{5,4},{6,7},{7,6},{8,9},{9,8},{10,11... | collective-permute-start | bytes 3538952 | tf_op jit(solution)/shard_map/ppermute | solution.py:522
  240.7 59.7 %collective-permute-start.6 = (bf16[896,768]{1,0:T(8,128)(2,1)}, bf16[896,768]{1,0:T(8,128)(2,1)}, u32[]{:S(2)}, u32[]{:S(2)}) collective-permute-start(bf16[896,768]{1,0:T(8,128)(2,1)} %get-tuple-element.80), channel_id=1, source_target_pairs={{0,1},{1,0},{2,3},{3,2},{4,5},{5,4},{6,7},{7,6},{8,9},{9,8},{10,11... | collective-permute-start | bytes 4128776 | tf_op jit(solution)/shard_map/ppermute | solution.py:522
  244.4 52.7 %collective-permute-start.25 = (bf16[768,768]{1,0:T(8,128)(2,1)}, bf16[768,768]{1,0:T(8,128)(2,1)}, u32[]{:S(2)}, u32[]{:S(2)}) collective-permute-start(bf16[768,768]{1,0:T(8,128)(2,1)} %add_convert_fusion.2), channel_id=1, source_target_pairs={{0,2},{1,3},{2,0},{3,1},{4,6},{5,7},{6,4},{7,5},{8,10},{9,11},{10,... | collective-permute-start | bytes 3538952 | tf_op jit(solution)/shard_map/ppermute | solution.py:522
  248.7 47.8 %collective-permute-start.4 = (bf16[512,768]{1,0:T(8,128)(2,1)}, bf16[512,768]{1,0:T(8,128)(2,1)S(1)}, u32[]{:S(2)}, u32[]{:S(2)}) collective-permute-start(bf16[512,768]{1,0:T(8,128)(2,1)} %get-tuple-element.68), channel_id=1, source_target_pairs={{0,2},{1,3},{2,0},{3,1},{4,6},{5,7},{6,4},{7,5},{8,10},{9,11},{10,... | collective-permute-start | bytes 2359304 | tf_op jit(solution)/shard_map/ppermute | solution.py:522
  254.5 70.5 %collective-permute-start.8 = (bf16[896,768]{1,0:T(8,128)(2,1)}, bf16[896,768]{1,0:T(8,128)(2,1)}, u32[]{:S(2)}, u32[]{:S(2)}) collective-permute-start(bf16[896,768]{1,0:T(8,128)(2,1)} %add_convert_fusion), channel_id=1, source_target_pairs={{0,2},{1,3},{2,0},{3,1},{4,6},{5,7},{6,4},{7,5},{8,10},{9,11},{10,... | collective-permute-start | bytes 4128776 | tf_op jit(solution)/shard_map/ppermute | solution.py:522
  296.5 105.5 %collective-permute-start.3 = (bf16[512,768]{1,0:T(8,128)(2,1)}, bf16[512,768]{1,0:T(8,128)(2,1)}, u32[]{:S(2)}, u32[]{:S(2)}) collective-permute-start(bf16[512,768]{1,0:T(8,128)(2,1)} %get-tuple-element.68), channel_id=1, source_target_pairs={{0,1},{1,0},{2,3},{3,2},{4,5},{5,4},{6,7},{7,6},{8,9},{9,8},{10,11... | collective-permute-start | bytes 2359304 | tf_op jit(solution)/shard_map/ppermute | solution.py:522
  296.6 106.7 %collective-permute-start.5 = (bf16[512,768]{1,0:T(8,128)(2,1)S(1)}, bf16[512,768]{1,0:T(8,128)(2,1)}, u32[]{:S(2)}, u32[]{:S(2)}) collective-permute-start(bf16[512,768]{1,0:T(8,128)(2,1)S(1)} %collective-permute-done.4), channel_id=1, source_target_pairs={{0,1},{1,0},{2,3},{3,2},{4,5},{5,4},{6,7},{7,6},{8,9},{9,8},{10,11... | collective-permute-start | bytes 2359304 | tf_op jit(solution)/shard_map/ppermute | solution.py:522
  297.1 32.2 %collective-permute-start.35 = (bf16[384,768]{1,0:T(8,128)(2,1)S(1)}, bf16[384,768]{1,0:T(8,128)(2,1)S(1)}, u32[]{:S(2)}, u32[]{:S(2)}) collective-permute-start(bf16[384,768]{1,0:T(8,128)(2,1)S(1)} %dynamic-slice_convert_fusion.1), channel_id=1, source_target_pairs={{0,4},{4,0},{8,12},{12,8},{16,20},{20,16},{24,28},{28,24},{1,5},{5... | collective-permute-start | bytes 1769480 | tf_op jit(solution)/shard_map/ppermute | solution.py:522
  300.4 30.7 %collective-permute-start.26 = (bf16[384,768]{1,0:T(8,128)(2,1)S(1)}, bf16[384,768]{1,0:T(8,128)(2,1)S(1)}, u32[]{:S(2)}, u32[]{:S(2)}) collective-permute-start(bf16[384,768]{1,0:T(8,128)(2,1)S(1)} %dynamic-slice_convert_fusion.2), channel_id=1, source_target_pairs={{0,4},{4,0},{8,12},{12,8},{16,20},{20,16},{24,28},{28,24},{1,5},{5... | collective-permute-start | bytes 1769480 | tf_op jit(solution)/shard_map/ppermute | solution.py:522
  328.0 16.9 %collective-permute-start.9 = (bf16[448,768]{1,0:T(8,128)(2,1)S(1)}, bf16[448,768]{1,0:T(8,128)(2,1)S(1)}, u32[]{:S(2)}, u32[]{:S(2)}) collective-permute-start(bf16[448,768]{1,0:T(8,128)(2,1)S(1)} %dynamic-slice_convert_fusion), channel_id=1, source_target_pairs={{0,4},{4,0},{8,12},{12,8},{16,20},{20,16},{24,28},{28,24},{1,5},{5... | collective-permute-start | bytes 2064392 | tf_op jit(solution)/shard_map/ppermute | solution.py:522
  329.4 11.6 %collective-permute-start.36 = (bf16[192,768]{1,0:T(8,128)(2,1)S(1)}, bf16[192,768]{1,0:T(8,128)(2,1)S(1)}, u32[]{:S(2)}, u32[]{:S(2)}) collective-permute-start(bf16[192,768]{1,0:T(8,128)(2,1)S(1)} %dynamic-slice_convert_fusion.4), channel_id=1, source_target_pairs={{0,8},{4,12},{8,0},{12,4},{16,24},{20,28},{24,16},{28,20},{1,9},{5... | collective-permute-start | bytes 884744 | tf_op jit(solution)/shard_map/ppermute | solution.py:522
  331.2 13.6 %collective-permute-start.27 = (bf16[192,768]{1,0:T(8,128)(2,1)S(1)}, bf16[192,768]{1,0:T(8,128)(2,1)S(1)}, u32[]{:S(2)}, u32[]{:S(2)}) collective-permute-start(bf16[192,768]{1,0:T(8,128)(2,1)S(1)} %dynamic-slice_convert_fusion.5), channel_id=1, source_target_pairs={{0,8},{4,12},{8,0},{12,4},{16,24},{20,28},{24,16},{28,20},{1,9},{5... | collective-permute-start | bytes 884744 | tf_op jit(solution)/shard_map/ppermute | solution.py:522
  341.1 8.3 %collective-permute-start.37 = (bf16[96,768]{1,0:T(8,128)(2,1)S(1)}, bf16[96,768]{1,0:T(8,128)(2,1)S(1)}, u32[]{:S(2)}, u32[]{:S(2)}) collective-permute-start(bf16[96,768]{1,0:T(8,128)(2,1)S(1)} %dynamic-slice_convert_fusion.9), channel_id=1, source_target_pairs={{0,16},{4,20},{8,24},{12,28},{16,0},{20,4},{24,8},{28,12},{1,17},{... | collective-permute-start | bytes 442376 | tf_op jit(solution)/shard_map/ppermute | solution.py:522
  345.1 15.6 %collective-permute-start.10 = (bf16[224,768]{1,0:T(8,128)(2,1)S(1)}, bf16[224,768]{1,0:T(8,128)(2,1)S(1)}, u32[]{:S(2)}, u32[]{:S(2)}) collective-permute-start(bf16[224,768]{1,0:T(8,128)(2,1)S(1)} %dynamic-slice_convert_fusion.3), channel_id=1, source_target_pairs={{0,8},{4,12},{8,0},{12,4},{16,24},{20,28},{24,16},{28,20},{1,9},{5... | collective-permute-start | bytes 1032200 | tf_op jit(solution)/shard_map/ppermute | solution.py:522
  346.8 15.0 %collective-permute-start.28 = (bf16[96,768]{1,0:T(8,128)(2,1)S(1)}, bf16[96,768]{1,0:T(8,128)(2,1)S(1)}, u32[]{:S(2)}, u32[]{:S(2)}) collective-permute-start(bf16[96,768]{1,0:T(8,128)(2,1)S(1)} %dynamic-slice_convert_fusion.10), channel_id=1, source_target_pairs={{0,16},{4,20},{8,24},{12,28},{16,0},{20,4},{24,8},{28,12},{1,17},{... | collective-permute-start | bytes 442376 | tf_op jit(solution)/shard_map/ppermute | solution.py:522
  349.4 24.9 %collective-permute-start.38 = (bf16[96,768]{1,0:T(8,128)(2,1)S(1)}, bf16[96,768]{1,0:T(8,128)(2,1)S(1)}, u32[]{:S(2)}, u32[]{:S(2)}) collective-permute-start(bf16[96,768]{1,0:T(8,128)(2,1)S(1)} %add_convert_fusion.4), channel_id=1, source_target_pairs={{0,16},{4,20},{8,24},{12,28},{16,0},{20,4},{24,8},{28,12},{1,17},{... | collective-permute-start | bytes 442376 | tf_op jit(solution)/shard_map/ppermute | solution.py:522
  360.8 13.4 %collective-permute-start.11 = (bf16[112,768]{1,0:T(8,128)(2,1)S(1)}, bf16[112,768]{1,0:T(8,128)(2,1)S(1)}, u32[]{:S(2)}, u32[]{:S(2)}) collective-permute-start(bf16[112,768]{1,0:T(8,128)(2,1)S(1)} %dynamic-slice_convert_fusion.8), channel_id=1, source_target_pairs={{0,16},{4,20},{8,24},{12,28},{16,0},{20,4},{24,8},{28,12},{1,17},{... | collective-permute-start | bytes 516104 | tf_op jit(solution)/shard_map/ppermute | solution.py:522
  361.9 17.9 %collective-permute-start.29 = (bf16[96,768]{1,0:T(8,128)(2,1)S(1)}, bf16[96,768]{1,0:T(8,128)(2,1)S(1)}, u32[]{:S(2)}, u32[]{:S(2)}) collective-permute-start(bf16[96,768]{1,0:T(8,128)(2,1)S(1)} %add_convert_fusion.5), channel_id=1, source_target_pairs={{0,16},{4,20},{8,24},{12,28},{16,0},{20,4},{24,8},{28,12},{1,17},{... | collective-permute-start | bytes 442376 | tf_op jit(solution)/shard_map/ppermute | solution.py:522
  374.2 9.8 %collective-permute-start.12 = (bf16[112,768]{1,0:T(8,128)(2,1)S(1)}, bf16[112,768]{1,0:T(8,128)(2,1)S(1)}, u32[]{:S(2)}, u32[]{:S(2)}) collective-permute-start(bf16[112,768]{1,0:T(8,128)(2,1)S(1)} %add_convert_fusion.3), channel_id=1, source_target_pairs={{0,16},{4,20},{8,24},{12,28},{16,0},{20,4},{24,8},{28,12},{1,17},{... | collective-permute-start | bytes 516104 | tf_op jit(solution)/shard_map/ppermute | solution.py:522
  374.4 13.5 %collective-permute-start.39 = (bf16[192,768]{1,0:T(8,128)(2,1)S(1)}, bf16[192,768]{1,0:T(8,128)(2,1)S(1)}, u32[]{:S(2)}, u32[]{:S(2)}) collective-permute-start(bf16[192,768]{1,0:T(8,128)(2,1)S(1)} %maximum_select_fusion.8), channel_id=1, source_target_pairs={{0,8},{4,12},{8,0},{12,4},{16,24},{20,28},{24,16},{28,20},{1,9},{5... | collective-permute-start | bytes 884744 | tf_op jit(solution)/shard_map/ppermute | solution.py:522
  379.8 14.4 %collective-permute-start.30 = (bf16[192,768]{1,0:T(8,128)(2,1)S(1)}, bf16[192,768]{1,0:T(8,128)(2,1)S(1)}, u32[]{:S(2)}, u32[]{:S(2)}) collective-permute-start(bf16[192,768]{1,0:T(8,128)(2,1)S(1)} %maximum_select_fusion.7), channel_id=1, source_target_pairs={{0,8},{4,12},{8,0},{12,4},{16,24},{20,28},{24,16},{28,20},{1,9},{5... | collective-permute-start | bytes 884744 | tf_op jit(solution)/shard_map/ppermute | solution.py:522
  384.1 16.5 %collective-permute-start.13 = (bf16[224,768]{1,0:T(8,128)(2,1)S(1)}, bf16[224,768]{1,0:T(8,128)(2,1)S(1)}, u32[]{:S(2)}, u32[]{:S(2)}) collective-permute-start(bf16[224,768]{1,0:T(8,128)(2,1)S(1)} %maximum_select_fusion.6), channel_id=1, source_target_pairs={{0,8},{4,12},{8,0},{12,4},{16,24},{20,28},{24,16},{28,20},{1,9},{5... | collective-permute-start | bytes 1032200 | tf_op jit(solution)/shard_map/ppermute | solution.py:522
  387.9 14.1 %copy-start.3 = (bf16[2048,768]{1,0:T(8,128)(2,1)S(1)}, bf16[2048,768]{1,0:T(8,128)(2,1)}, u32[]{:S(2)}) copy-start(bf16[2048,768]{1,0:T(8,128)(2,1)} %copy-done.2) | copy-start | bytes 9437188
  388.1 19.6 %collective-permute-start.40 = (bf16[384,768]{1,0:T(8,128)(2,1)S(1)}, bf16[384,768]{1,0:T(8,128)(2,1)S(1)}, u32[]{:S(2)}, u32[]{:S(2)}) collective-permute-start(bf16[384,768]{1,0:T(8,128)(2,1)S(1)} %maximum_select_fusion.5), channel_id=1, source_target_pairs={{0,4},{4,0},{8,12},{12,8},{16,20},{20,16},{24,28},{28,24},{1,5},{5... | collective-permute-start | bytes 1769480 | tf_op jit(solution)/shard_map/ppermute | solution.py:522
  394.4 22.7 %collective-permute-start.31 = (bf16[384,768]{1,0:T(8,128)(2,1)S(1)}, bf16[384,768]{1,0:T(8,128)(2,1)S(1)}, u32[]{:S(2)}, u32[]{:S(2)}) collective-permute-start(bf16[384,768]{1,0:T(8,128)(2,1)S(1)} %maximum_select_fusion.4), channel_id=1, source_target_pairs={{0,4},{4,0},{8,12},{12,8},{16,20},{20,16},{24,28},{28,24},{1,5},{5... | collective-permute-start | bytes 1769480 | tf_op jit(solution)/shard_map/ppermute | solution.py:522
  400.8 28.0 %collective-permute-start.14 = (bf16[448,768]{1,0:T(8,128)(2,1)S(1)}, bf16[448,768]{1,0:T(8,128)(2,1)S(1)}, u32[]{:S(2)}, u32[]{:S(2)}) collective-permute-start(bf16[448,768]{1,0:T(8,128)(2,1)S(1)} %maximum_select_fusion.3), channel_id=1, source_target_pairs={{0,4},{4,0},{8,12},{12,8},{16,20},{20,16},{24,28},{28,24},{1,5},{5... | collective-permute-start | bytes 2064392 | tf_op jit(solution)/shard_map/ppermute | solution.py:522
  429.5 7.4 %collective-permute-start.15 = (bf16[128,768]{1,0:T(8,128)(2,1)S(1)}, bf16[128,768]{1,0:T(8,128)(2,1)S(1)}, u32[]{:S(2)}, u32[]{:S(2)}) collective-permute-start(bf16[128,768]{1,0:T(8,128)(2,1)S(1)} %get-tuple-element.84), channel_id=1, source_target_pairs={{0,1},{1,0},{2,3},{3,2},{4,5},{5,4},{6,7},{7,6},{8,9},{9,8},{10,11... | collective-permute-start | bytes 589832 | tf_op jit(solution)/shard_map/ppermute | solution.py:522
  429.6 7.3 %collective-permute-start.16 = (bf16[128,768]{1,0:T(8,128)(2,1)S(1)}, bf16[128,768]{1,0:T(8,128)(2,1)S(1)}, u32[]{:S(2)}, u32[]{:S(2)}) collective-permute-start(bf16[128,768]{1,0:T(8,128)(2,1)S(1)} %get-tuple-element.84), channel_id=1, source_target_pairs={{0,2},{1,3},{2,0},{3,1},{4,6},{5,7},{6,4},{7,5},{8,10},{9,11},{10,... | collective-permute-start | bytes 589832 | tf_op jit(solution)/shard_map/ppermute | solution.py:522
  436.9 1.4 collective-permute-start.17
  (41 other events, 122.2 us)
Sparse Core Ops, SparseCore 0:
  169.8 28.8 all-gather.1

commit v3 on v2

--- a/solution.py
+++ b/solution.py
@@ -23,33 +23,6 @@
 
 def nn(a, b):
     return jnp.dot(a, b, preferred_element_type=jnp.float32)
-
-
-def layout_features(box_coords):
-    freq_index = jnp.arange(LFREQ).astype(jnp.float32)
-    frequency = jnp.exp(freq_index * (-math.log(1000.0) / LFREQ))
-    angles = box_coords.astype(jnp.float32)[:, :, None] * frequency[None, None, :]
-    waves = jnp.concatenate([jnp.sin(angles), jnp.cos(angles)], axis=2)
-    return waves.reshape(box_coords.shape[0], 8 * LFREQ)
-
-
-def normalize_keep(values_in, gain_vec, shift_vec):
-    row_mean = jnp.mean(values_in, axis=-1, keepdims=True)
-    centered = values_in - row_mean
-    inverse = lax.rsqrt(jnp.mean(centered * centered, axis=-1, keepdims=True) + EPSILON)
-    unit_rows = centered * inverse
-    return (unit_rows * gain_vec + shift_vec, unit_rows, inverse)
-
-
-def normalize_back(upstream, unit_rows, inverse, gain_vec):
-    scaled = upstream * gain_vec
-    mean_one = jnp.mean(scaled, axis=-1, keepdims=True)
-    mean_two = jnp.mean(scaled * unit_rows, axis=-1, keepdims=True)
-    return (
-        (scaled - mean_one - unit_rows * mean_two) * inverse,
-        jnp.sum(upstream * unit_rows, axis=0),
-        jnp.sum(upstream, axis=0),
-    )
 
 
 def xor_index(index, bit):
@@ -372,6 +345,7 @@
         sums_out[0:1, :] += jnp.sum(selected * unit, axis=0, keepdims=True)
         sums_out[1:2, :] += jnp.sum(selected, axis=0, keepdims=True)
         sums_out[2:3, :] += jnp.sum(dres, axis=0, keepdims=True)
+        sums_out[3:4, :] += jnp.sum(mask_ref[sl, :].astype(f32), axis=0, keepdims=True)
 
     for i in (last - 2, last - 1):
         p_copy(i, i % 2).wait()
@@ -443,134 +417,598 @@
     )(tok, box, rx, ry, mask, cot, freq, lay, vec, cols_own, rows_own, qkv_own, wo_own, w1_own, w2_own)
 
 
-def attend_back_kernel(
-    q_ref, k_ref, v_ref, p_ref, dc_ref, rx_ref, ry_ref,
-    dq_ref, dk_ref, dv_ref, g_ref, ds_scr, hot_scr, acc,
-):
-    head = pl.program_id(0)
-    heads = pl.num_programs(0)
-    win = rx_ref.shape[0]
-    dc_t = dc_ref[...]
-    dc = dc_t.astype(jnp.float32).T.astype(jnp.bfloat16)
-    p = p_ref[0]
-    dp = nn(dc, v_ref[...])
-    row_dot = jnp.sum(p * dp, axis=1, keepdims=True)
-    ds = (p * (dp - row_dot)).astype(jnp.bfloat16)
-    dv_ref[...] = nn(dc_t, p.astype(jnp.bfloat16)).astype(jnp.bfloat16)
-    dq_ref[...] = (nt(k_ref[...], ds) * HD ** (-0.5)).astype(jnp.bfloat16)
-    dk_ref[...] = (nn(q_ref[...], ds) * HD ** (-0.5)).astype(jnp.bfloat16)
-    ds_scr[head] = ds
-
-    @pl.when(head == heads - 1)
-    def _():
-        acc[...] = jnp.zeros_like(acc)
-        one, zero = jnp.bfloat16(1), jnp.bfloat16(0)
-        half = BUCKETS * ROWS
-
-        def step(g, carry):
-            rows = pl.ds(pl.multiple_of(g * ROWS, ROWS), ROWS)
-            x = rx_ref[rows, :].astype(jnp.float32).astype(jnp.bfloat16)
-            y = ry_ref[rows, :].astype(jnp.float32).astype(jnp.bfloat16)
-            for b in range(BUCKETS):
-                hot_scr[b * ROWS : (b + 1) * ROWS, :] = jnp.where(x == jnp.bfloat16(b), one, zero)
-                hot_scr[half + b * ROWS : half + (b + 1) * ROWS, :] = jnp.where(
-                    y == jnp.bfloat16(b), one, zero
-                )
-            left = ds_scr[:, rows, :].reshape(ds_scr.shape[0] * ROWS, win)
-            acc[...] += nt(left, hot_scr[...])
-            return carry
-
-        lax.fori_loop(0, win // ROWS, step, 0)
-        row = lax.broadcasted_iota(jnp.int32, (ROWS, 2 * half), 0)
-        col = lax.broadcasted_iota(jnp.int32, (ROWS, 2 * half), 1) % ROWS
-        for h in range(ds_scr.shape[0]):
-            part = jnp.where(row == col, acc[h * ROWS : (h + 1) * ROWS, :], 0.0)
-            g_ref[h : h + 1, :] = jnp.sum(part, axis=0, keepdims=True)
-
-
-def attend_back(q, k, v, p, dc, rel_x, rel_y):
-    heads, win = p.shape[0], rel_x.shape[0]
-    hots = 2 * BUCKETS * ROWS
-    blk = pl.BlockSpec((HD, win), lambda h: (h, 0))
-    full = pl.BlockSpec((win, win), lambda h: (0, 0))
-    dq, dk, dv, g = pl.pallas_call(
-        attend_back_kernel,
-        grid=(heads,),
-        in_specs=[blk, blk, blk, pl.BlockSpec((1, win, win), lambda h: (h, 0, 0)), blk, full, full],
-        out_specs=[blk, blk, blk, pl.BlockSpec((heads, hots), lambda h: (0, 0))],
-        out_shape=[jax.ShapeDtypeStruct((heads * HD, win), jnp.bfloat16)] * 3
-        + [jax.ShapeDtypeStruct((heads, hots), jnp.float32)],
-        scratch_shapes=[
-            pltpu.VMEM((heads, win, win), jnp.bfloat16),
-            pltpu.VMEM((hots, win), jnp.bfloat16),
-            pltpu.VMEM((heads * ROWS, hots), jnp.float32),
-        ],
-        compiler_params=pltpu.CompilerParams(vmem_limit_bytes=56 * 2**20),
-        cost_estimate=pl.CostEstimate(
-            flops=20 * 10**9, bytes_accessed=20 * 10**6, transcendentals=0
-        ),
-        name="attend_back",
-    )(q, k, v, p, dc, rel_x, rel_y)
-    return dq, dk, dv, jnp.sum(g.reshape(heads, 2 * BUCKETS, ROWS), axis=2).T
-
-
 def bits_of(size):
     return [1 << b for b in range(size.bit_length() - 1)]
 
 
-def swap(value, axis, size, bit):
-    return lax.ppermute(value, axis, [(i, i ^ bit) for i in range(size)])
-
-
-def gather_pieces(own, axis, size):
-    pieces = {0: own}
-    for bit in reversed(bits_of(size)):
-        for r in list(pieces):
-            pieces[r | bit] = swap(pieces[r], axis, size, bit)
-    return [pieces[r] for r in range(size)]
-
-
-def scatter_pieces(pieces, axis, size):
-    pieces = dict(enumerate(pieces))
-    for bit in bits_of(size):
-        for r in [r for r in pieces if r & bit]:
-            got = swap(pieces.pop(r).astype(jnp.bfloat16), axis, size, bit)
-            pieces[r ^ bit] = pieces[r ^ bit].astype(jnp.float32) + got.astype(jnp.float32)
-    return pieces[0]
-
-
-def reduce_rows(total, axis, size):
-    me = lax.axis_index(axis)
-    held = total
-    for bit in bits_of(size):
-        half = held.shape[0] // 2
-        side = (me // bit) % 2
-        mine = lax.dynamic_slice_in_dim(held, side * half, half)
-        other = lax.dynamic_slice_in_dim(held, (1 - side) * half, half)
-        got = swap(other.astype(jnp.bfloat16), axis, size, bit)
-        held = mine.astype(jnp.float32) + got.astype(jnp.float32)
-    held = held.astype(jnp.bfloat16)
-    for bit in reversed(bits_of(size)):
-        got = swap(held, axis, size, bit)
-        side = (me // bit) % 2
-        held = jnp.where(
-            side == 0, jnp.concatenate([held, got]), jnp.concatenate([got, held])
+def tn(a, b):
+    return lax.dot_general(a, b, (((0,), (0,)), ((), ())), preferred_element_type=jnp.float32)
+
+
+def add_into(dst, more):
+    rows = dst.shape[0]
+    step = 64 if rows % 64 == 0 else 16
+
+    @pl.loop(0, rows // step)
+    def _(i):
+        sl = pl.ds(pl.multiple_of(i * step, step), step)
+        total = dst[sl, :].astype(jnp.float32)
+        for ref in more:
+            total = total + ref[sl, :].astype(jnp.float32)
+        dst[sl, :] = total.astype(jnp.bfloat16)
+
+
+class Reduce:
+    def __init__(self, slot, rows, x_first, part, core, first, second, quarters, final, extra, result, sems, peers):
+        self.slot, self.rows, self.x_first, self.part = slot, rows, x_first, part
+        self.core, self.first, self.second, self.quarters, self.final = core, first, second, quarters, final
+        self.extra, self.result = extra, result
+        self.send, self.recv, self.here = sems
+        self.mate, self.across, self.beside, self.along, self.further, self.side, self.level = peers
+
+    def move(self, k, src, dst, peer):
+        return remote(src, dst, self.send.at[self.slot, k], self.recv.at[self.slot, k], peer)
+
+    def half(self, mine):
+        h = self.rows // 2
+        side = self.side if mine else 1 - self.side
+        return pl.ds(pl.multiple_of(side * h, h), h)
+
+    def quarter(self, level):
+        q = self.rows // 8
+        return pl.ds(pl.multiple_of(self.side * (self.rows // 2) + level * q, q), q)
+
+    def moves(self, stage):
+        if stage == 0:
+            return [self.move(k, self.part(2 * k + 1), self.core.at[k], self.mate) for k in range(2)]
+        if stage == 1 and self.x_first:
+            return [self.move(2, self.core.at[1], self.first, self.across)]
+        if stage == 1:
+            h = self.rows // 2
+            return [
+                self.move(2 + k, self.core.at[k, self.half(False)], self.first.at[pl.ds(k * h, h)], self.beside)
+                for k in range(2)
+            ]
+        if stage == 2 and self.x_first:
+            return [self.move(4, self.core.at[0, self.half(False)], self.second, self.beside)]
+        if stage == 2:
+            return [self.move(4, self.core.at[1, self.half(True)], self.second, self.across)]
+        if stage == 3:
+            return [
+                self.move(
+                    4 + k, self.core.at[0, self.quarter(xor_level(self.level, k))], self.quarters.at[k - 1], self.along[k]
+                )
+                for k in range(1, 4)
+            ]
+        if stage == 4:
+            rows = self.quarter(self.level)
+            return [self.move(7 + k, self.final, self.result.at[rows], self.along[k]) for k in range(1, 4)]
+        rows = self.half(True)
+        return [self.move(11, self.result.at[rows], self.result.at[rows], self.beside)]
+
+    def own_copy(self):
+        return pltpu.make_async_copy(self.final, self.result.at[self.quarter(self.level)], self.here.at[self.slot])
+
+    def more(self, k):
+        return self.move(12 + k, self.final_of(k), self.extra.at[k], self.further[k])
+
+    def final_of(self, k):
+        return self.final if k == 0 else self.extra.at[len(self.further) + k]
+
+    def take(self, stage):
+        for m in self.moves(stage):
+            m.wait_recv()
+        h = self.rows // 2
+        if stage == 0:
+            for k in range(2):
+                add_into(self.core.at[k], [self.part(2 * k)])
+        if stage == 1 and self.x_first:
+            add_into(self.core.at[0], [self.first])
+        if stage == 1 and not self.x_first:
+            for k in range(2):
+                add_into(self.core.at[k, self.half(True)], [self.first.at[pl.ds(k * h, h)]])
+        if stage == 2:
+            add_into(self.core.at[0, self.half(True)], [self.second])
+        if stage == 3:
+            self.final[...] = self.core[0, self.quarter(self.level), :]
+            add_into(self.final, [self.quarters.at[k] for k in range(3)])
+            for k in range(len(self.further)):
+                self.more(k).start()
+                self.more(k).wait()
+                total = self.final_of(k)[...].astype(jnp.float32) + self.extra[k].astype(jnp.float32)
+                self.final_of(k + 1)[...] = total.astype(jnp.bfloat16)
+            if self.further:
+                self.final[...] = self.final_of(len(self.further))[...]
+            self.own_copy().start()
+        if stage == 4:
+            self.own_copy().wait()
+
+    def go(self, stage):
+        for m in self.moves(stage):
+            m.start()
+
+    def next(self, stage):
+        self.take(stage)
+        if stage < 5:
+            self.go(stage + 1)
+
+    def sent(self, stage):
+        for m in self.moves(stage):
+            m.wait_send()
+
+
+def xor_level(level, k):
+    for bit in (1, 2):
+        if k & bit:
+            level = xor_index(level, bit)
+    return level
+
+
+def gelu_slope(v):
+    k = math.sqrt(2.0 / math.pi)
+    square = v * v
+    t = jnp.tanh(k * v * (1.0 + 0.044715 * square))
+    return 0.5 * (1.0 + t) + (0.5 * k) * v * (1.0 - t * t) * (1.0 + 3 * 0.044715 * square)
+
+
+SMALL = 16
+
+
+def backward_kernel(
+    n_dp, inv_ref, vec_ref, sums_ref, dres_in, hid_in, pre_in, unit_in, nlow_in, low_in, feat_in, qkvt_in, ctxt_in,
+    probs_in, rx_in, ry_in, w1_in, w2_in, wo_in, wqkv_in, block_in,
+    block_all, in_all, red1, red2, red3, lay_all, small_out,
+    arena, hidb, preb, dres, unit, nlow, nlow_t, dn, low_rows, qkvb, ctxtb, dctx, lowb, featb, wob, rxb, ryb, hot, acc,
+    part1, part2, part3, core1, core2, core3, first1, first2, first3, second1, second2, second3,
+    quarters1, quarters2, quarters3, final1, final2, final3, extra1, extra2, extra3, small, small_in, short,
+    load_sem, send, recv, here, share_send, share_recv, small_send, small_recv, p_sem,
+):
+    t, d = lax.axis_index("tensor"), lax.axis_index("dp")
+    mate, across = {"tensor": xor_index(t, 1)}, {"tensor": xor_index(t, 2)}
+    beside = {"dp": xor_index(d, 1)}
+    along = [None] + [{"dp": d + 2 * (xor_level((d // 2) % 4, k) - (d // 2) % 4)} for k in range(1, 4)]
+    further = [{"dp": xor_index(d, bit)} for bit in bits_of(n_dp) if bit >= 8]
+    peers = (mate, across, beside, along, further, d % 2, (d // 2) % 4)
+    sems = (send, recv, here)
+    f32, bf16 = jnp.float32, jnp.bfloat16
+    win, model = dres.shape
+    heads = 4 * HEADS_T
+    cols_t = HEADS_T * HD
+    hid_t = model
+    block = 128
+
+    def load(k, src, dst):
+        return pltpu.make_async_copy(src, dst, load_sem.at[k])
+
+    def w_rows(r):
+        return pl.ds(r * hid_t, hid_t)
+
+    def h_rows(r):
+        return pl.ds(r * win, win)
+
+    order = (1, 3, 2, 0)
+    ld_dres = load(0, dres_in, dres)
+    ld_hid = {r: load(1 + r, hid_in.at[r], hidb.at[h_rows(r)]) for r in order}
+    ld_w2 = {r: load(5 + r, w2_in.at[r], arena.at[w_rows(r)]) for r in order}
+    ld_w1 = {r: load(9 + r, w1_in.at[r], arena.at[w_rows(4 + r)]) for r in order}
+    ld_pre = {r: load(13 + r, pre_in.at[r], preb.at[i % 2]) for i, r in enumerate(order)}
+    ld_rest = [
+        load(17 + k, src, dst)
+        for k, (src, dst) in enumerate(
+            [
+                (nlow_in, nlow), (unit_in, unit), (ctxt_in, ctxtb), (wo_in, wob), (qkvt_in, qkvb), (low_in, lowb),
+                (feat_in, featb), (rx_in, rxb), (ry_in, ryb),
+            ]
         )
-    return held
-
-
-def sum_small(value, axis, size):
-    for bit in bits_of(size):
-        value = value + swap(value, axis, size, bit)
-    return value
-
-
-def place_pieces(pieces, me):
-    size, rows = len(pieces), pieces[0].shape[0]
-    whole = jnp.zeros((size * rows,) + pieces[0].shape[1:], pieces[0].dtype)
-    for r, piece in enumerate(pieces):
-        whole = lax.dynamic_update_slice_in_dim(whole, piece, (me ^ r) * rows, 0)
-    return whole
+    ]
+    ld_wqkv = [load(26 + n, wqkv_in.at[n], hidb.at[pl.ds(n * model, model)]) for n in range(3)]
+    ld_dres.start()
+    for r in order:
+        ld_hid[r].start()
+    for r in order[:2]:
+        ld_pre[r].start()
+    for r in order:
+        ld_w2[r].start()
+    ld_rest[0].start()
+    for r in order:
+        ld_w1[r].start()
+    for c in ld_rest[1:]:
+        c.start()
+
+    def reduce_of(slot, rows, at, x_first, part, core, first, second, quarters, final, extra, result):
+        h, q = rows // 2, rows // 8
+        return Reduce(
+            slot, rows, x_first, part, core.at[:, pl.ds(at, rows)], first.at[pl.ds(at, rows)],
+            second.at[pl.ds(at // 2, h)], quarters.at[:, pl.ds(at // 8, q)], final.at[pl.ds(at // 8, q)],
+            extra.at[:, pl.ds(at // 8, q)], result.at[pl.ds(at, rows)], sems, peers,
+        )
+
+    def chunks(slot, sizes, x_first, parts, *buffers):
+        out, at = [], 0
+        for k, (rows, part) in enumerate(zip(sizes, parts)):
+            out.append(reduce_of(slot + k, rows, at, x_first, part, *buffers))
+            at += rows
+        return out
+
+    third = hid_t // 3
+    sizes = [third] * 3
+
+    def thirds(ref):
+        return [lambda r, k=k: ref.at[r, pl.ds(k * third, third)] for k in range(3)]
+
+    s2 = chunks(0, sizes, True, thirds(part2), core2, first2, second2, quarters2, final2, extra2, red2)
+    s1 = chunks(3, sizes, False, thirds(part1), core1, first1, second1, quarters1, final1, extra1, red1)
+    lay_t = lay_all.shape[0] // 4
+    s3 = chunks(
+        6, [2 * cols_t, 2 * cols_t, lay_t], True,
+        [
+            lambda r: part2.at[r, pl.ds(0, 2 * cols_t)],
+            lambda r: part2.at[r, pl.ds(2 * cols_t, 2 * cols_t)],
+            lambda r: part3.at[r],
+        ],
+        core3, first3, second3, quarters3, final3, extra3, red3,
+    )
+
+    def share(k, src, whole, rows):
+        def at(index):
+            return whole.at[pl.ds(pl.multiple_of(index * rows, rows), rows)]
+
+        def moved(j, from_ref, index, peer):
+            return remote(from_ref, at(index), share_send.at[k, j], share_recv.at[k, j], peer)
+
+        far = xor_index(t, 2)
+        return {
+            "here": pltpu.make_async_copy(src, at(t), share_send.at[k, 3]),
+            "across": moved(0, src, t, across),
+            "mate": moved(1, src, t, mate),
+            "pass": moved(2, at(far), far, mate),
+        }
+
+    def share_start(c):
+        for name in ("across", "mate", "here"):
+            c[name].start()
+
+    def share_pass(c):
+        c["across"].wait_recv()
+        c["pass"].start()
+
+    def share_end(c):
+        c["here"].wait()
+        c["mate"].wait_recv()
+        c["pass"].wait_recv()
+        for name in ("across", "mate", "pass"):
+            c[name].wait_send()
+
+    sh_block = share(0, block_in, block_all, win)
+    sh_in = share(1, low_rows, in_all, win)
+    sh_lay = share(2, red3.at[pl.ds(4 * cols_t, lay_t)], lay_all, lay_t)
+
+    signal_peers([mate, across, beside] + along[1:] + further)
+    share_start(sh_block)
+
+    small[0] = jnp.zeros_like(small[0])
+    small[0, 3:4, :] = sums_ref[2:3, :]
+    small[0, 4:6, :] = sums_ref[0:2, :]
+    small[0, 6:7, :] = sums_ref[3:4, :]
+
+    def own_row(base, r):
+        index = t
+        for bit in (1, 2):
+            if r & bit:
+                index = xor_index(index, bit)
+        return pl.ds(base + index, 1)
+
+    ld_dres.wait()
+
+    @pl.loop(0, win // block)
+    def _(i):
+        sl = pl.ds(pl.multiple_of(i * block, block), block)
+        low_rows[sl, :] = dres[sl, :].astype(bf16)
+
+    for j, r in enumerate(order):
+        ld_hid[r].wait()
+
+        @pl.loop(0, 3)
+        def _(c, r=r):
+            sl = pl.ds(pl.multiple_of(c * third, third), third)
+            part2[r, sl, :] = tn(hidb[h_rows(r), sl], low_rows[...]).astype(bf16)
+
+        if j == 1:
+            for g in s2:
+                g.go(0)
+
+    ld_rest[0].wait()
+    nlow_t[...] = nlow[...].astype(f32).T.astype(bf16)
+    for j, r in enumerate(order):
+        ld_pre[r].wait()
+        ld_w2[r].wait()
+        ld_w1[r].wait()
+
+        @pl.loop(0, 2)
+        def _(i, j=j, r=r):
+            count = win // 2
+            sl = pl.ds(pl.multiple_of(i * count, count), count)
+            hs = pl.ds(pl.multiple_of(r * win + i * count, count), count)
+            dhid = nt(low_rows[sl, :], arena[w_rows(r), :])
+            dpre = (dhid * gelu_slope(preb[j % 2, sl, :])).astype(bf16)
+            hidb[hs, :] = dpre
+            row = own_row(8, r)
+            small[0, row, :] += jnp.sum(dpre.astype(f32), axis=0, keepdims=True)
+            more = nt(dpre, arena[w_rows(4 + r), :])
+            dn[sl, :] = more if j == 0 else dn[sl, :] + more
+
+        if j + 2 < 4:
+            ld_pre[order[j + 2]].start()
+
+        @pl.loop(0, 3)
+        def _(c, r=r):
+            sl = pl.ds(pl.multiple_of(c * third, third), third)
+            part1[r, sl, :] = nn(nlow_t[sl, :], hidb[h_rows(r), :]).astype(bf16)
+
+        if j == 0:
+            for g in s2:
+                g.next(0)
+        if j == 1:
+            for g in s1:
+                g.go(0)
+
+    for c in ld_wqkv:
+        c.start()
+
+    def p_load(h, slot):
+        return pltpu.make_async_copy(probs_in.at[h], preb.at[slot, :, pl.ds(0, win)], p_sem.at[slot])
+
+    for h in range(2):
+        p_load(h, h).start()
+    for g in s1:
+        g.next(0)
+    share_pass(sh_block)
+    for g in s2:
+        g.sent(0)
+
+    ld_rest[1].wait()
+
+    @pl.loop(0, win // block)
+    def _(i):
+        sl = pl.ds(pl.multiple_of(i * block, block), block)
+        up = dres[sl, :] + dn[sl, :]
+        units = unit[sl, :]
+        scaled = up * vec_ref[1:2, :]
+        mean_one = jnp.mean(scaled, axis=1, keepdims=True)
+        mean_two = jnp.mean(scaled * units, axis=1, keepdims=True)
+        value = (scaled - mean_one - units * mean_two) * inv_ref[sl, :]
+        dn[sl, :] = value
+        low_rows[sl, :] = value.astype(bf16)
+        small[0, 0:1, :] += jnp.sum(value, axis=0, keepdims=True)
+        small[0, 1:2, :] += jnp.sum(up * units, axis=0, keepdims=True)
+        small[0, 2:3, :] += jnp.sum(up, axis=0, keepdims=True)
+
+    for c in ld_rest[2:]:
+        c.wait()
+
+    @pl.loop(0, 4)
+    def _(r):
+        sl = pl.ds(pl.multiple_of(r * cols_t, cols_t), cols_t)
+        part2[r, cols_t : 2 * cols_t, :] = nn(ctxtb[sl, :], low_rows[...]).astype(bf16)
+        dctx[sl, :] = nt(wob[sl, :], low_rows[...]).astype(bf16)
+
+    def events(index, table):
+        for at, todo in table.items():
+            @pl.when(index == at)
+            def _(todo=todo):
+                for f in todo:
+                    f()
+
+    def ev(g, stage):
+        return lambda: g.next(stage)
+
+    in_heads = {
+        3: [ev(s2[0], 1)],
+        6: [ev(s1[0], 1), ev(s2[1], 1)],
+        9: [ev(s1[1], 1), ev(s2[0], 2)],
+        11: [ev(s2[2], 1), ev(s1[2], 1)],
+    }
+
+    @pl.loop(0, heads)
+    def _(h):
+        slot = h % 2
+        sl = pl.ds(pl.multiple_of(h * HD, HD), HD)
+        dc_t = dctx[sl, :]
+        dc = dc_t.astype(f32).T.astype(bf16)
+        p_load(h, slot).wait()
+        p = preb[slot, :, 0:win]
+        dp = nn(dc, qkvb[2, sl, :])
+        row_dot = jnp.sum(p * dp, axis=1, keepdims=True)
+        ds = (p * (dp - row_dot)).astype(bf16)
+        qkvb[2, sl, :] = nn(dc_t, p.astype(bf16)).astype(bf16)
+        dq = nt(qkvb[1, sl, :], ds) * HD ** (-0.5)
+        dk = nn(qkvb[0, sl, :], ds) * HD ** (-0.5)
+        qkvb[0, sl, :] = dq.astype(bf16)
+        qkvb[1, sl, :] = dk.astype(bf16)
+        arena[pl.ds(pl.multiple_of(h * win, win), win), 0:win] = ds
+
+        @pl.when(h + 2 < heads)
+        def _():
+            p_load(h + 2, slot).start()
+
+        events(h, in_heads)
+
+    for c in ld_wqkv:
+        c.wait()
+    for n, at, g in ((2, 0, s3[0]), (0, 2 * cols_t, None), (1, 3 * cols_t, s3[1])):
+        @pl.loop(0, 4)
+        def _(r, n=n, at=at):
+            sl = pl.ds(pl.multiple_of(r * cols_t, cols_t), cols_t)
+            part2[r, at : at + cols_t, :] = nn(qkvb[n, sl, :], lowb[...]).astype(bf16)
+
+        if g is not None:
+            g.go(0)
+
+    @pl.loop(0, win // block)
+    def _(i):
+        sl = pl.ds(pl.multiple_of(i * block, block), block)
+        value = dn[sl, :]
+        for n in range(3):
+            value = value + tn(qkvb[n, :, sl], hidb[pl.ds(n * model, model), :])
+        low_rows[sl, :] = value.astype(bf16)
+
+    share_start(sh_in)
+    for c in range(4):
+        rows = [c ^ r for r in range(4)]
+        value = tn(featb[:, c * lay_t : (c + 1) * lay_t], low_rows[...]).astype(bf16)
+        part3[xor_level(t, c)] = value
+    s3[2].go(0)
+    for g in s3:
+        g.next(0)
+
+    ones = jnp.ones((8, win), bf16)
+    short[...] = jnp.zeros_like(short)
+    for n, at in ((0, 0), (2, cols_t)):
+        total = nt(ones, qkvb[n])
+        for r in range(4):
+            short[r : r + 1, at : at + cols_t] = total[0:1, r * cols_t : (r + 1) * cols_t]
+
+    acc[...] = jnp.zeros_like(acc)
+    one, zero = bf16(1), bf16(0)
+    hots = BUCKETS * ROWS
+    in_table = {
+        1: [ev(s1[0], 2), ev(s2[1], 2)],
+        3: [ev(s2[0], 3), ev(s1[1], 2)],
+        5: [ev(s1[0], 3), ev(s2[2], 2)],
+        7: [ev(s2[1], 3), ev(s1[2], 2), ev(s2[0], 4)],
+        9: [ev(s1[1], 3), ev(s2[2], 3), ev(s1[0], 4)],
+        11: [ev(s1[2], 3), ev(s2[1], 4)],
+        13: [ev(s1[1], 4), ev(s2[2], 4), ev(s1[2], 4)],
+        15: [ev(s3[0], 1)],
+    }
+
+    @pl.loop(0, win // ROWS // 2)
+    def _(i):
+        total = None
+        for u in range(2):
+            at = pl.multiple_of(i * 2 * ROWS + u * ROWS, ROWS)
+            x = rxb[pl.ds(at, ROWS), :].astype(f32).astype(bf16)
+            y = ryb[pl.ds(at, ROWS), :].astype(f32).astype(bf16)
+            for b in range(BUCKETS):
+                hot[u, b * ROWS : (b + 1) * ROWS, :] = jnp.where(x == bf16(b), one, zero)
+                hot[u, hots + b * ROWS : hots + (b + 1) * ROWS, :] = jnp.where(y == bf16(b), one, zero)
+            left = jnp.concatenate(
+                [arena[pl.ds(pl.multiple_of(h * win + at, ROWS), ROWS), 0:win] for h in range(heads)], axis=0
+            )
+            more = nt(left, hot[u])
+            total = more if total is None else total + more
+        acc[...] += total
+        events(i, in_table)
+
+    row = lax.broadcasted_iota(jnp.int32, (ROWS, 2 * hots), 0)
+    col = lax.broadcasted_iota(jnp.int32, (ROWS, 2 * hots), 1) % ROWS
+    picked = jnp.concatenate(
+        [
+            jnp.sum(jnp.where(row == col, acc[h * ROWS : (h + 1) * ROWS, :], 0.0), axis=0, keepdims=True)
+            for h in range(heads)
+        ]
+        + [jnp.zeros((16 - heads, 2 * hots), f32)],
+        axis=0,
+    )
+    fold = (
+        lax.broadcasted_iota(jnp.int32, (2 * hots, 128), 0) // ROWS
+        == lax.broadcasted_iota(jnp.int32, (2 * hots, 128), 1)
+    ).astype(f32)
+    table = jnp.dot(picked, fold, preferred_element_type=f32, precision=lax.Precision.HIGHEST)
+    for r in range(4):
+        for a in range(HEADS_T):
+            lane = 2 * cols_t + a * 2 * BUCKETS
+            short[r : r + 1, lane : lane + 2 * BUCKETS] = table[
+                r * HEADS_T + a : r * HEADS_T + a + 1, 0 : 2 * BUCKETS
+            ]
+    for r in range(4):
+        small[0, own_row(12, r), :] = short[r : r + 1, :]
+
+    bits = [mate, across, beside, along[1], along[2]] + further
+
+    def small_move(k):
+        return remote(small.at[k], small_in.at[k], small_send.at[k], small_recv.at[k], bits[k])
+
+    def small_step(k):
+        def run():
+            small_move(k).wait()
+            small[k + 1] = small[k] + small_in[k]
+            if k + 1 < len(bits):
+                small_move(k + 1).start()
+
+        return run
+
+    small_move(0).start()
+    steps = [small_step(k) for k in range(len(bits))]
+    tail = [
+        ev(s3[1], 1), steps[0], ev(s3[2], 1), ev(s3[0], 2), steps[1], ev(s3[1], 2), ev(s3[2], 2), ev(s3[0], 3),
+        steps[2], ev(s3[1], 3), ev(s3[2], 3), ev(s3[2], 4), ev(s3[0], 4), ev(s3[1], 4), steps[3],
+        ev(s3[2], 5), lambda: share_start(sh_lay), steps[4], ev(s3[0], 5), ev(s3[1], 5),
+        lambda: share_pass(sh_in), lambda: share_pass(sh_lay),
+    ] + steps[5:] + [ev(g, 5) for g in s2 + s1]
+    for f in tail:
+        f()
+    small_out[...] = small[len(bits)]
+    for c in (sh_block, sh_in, sh_lay):
+        share_end(c)
+    for g in s1 + s3:
+        g.sent(0)
+    for g in s2 + s1 + s3:
+        for stage in range(1, 6):
+            g.sent(stage)
+
+
+def backward_window(n_dp, lay_rows, inv, vec, sums, dres, hid, pre, unit, nlow, low, feat, qkvt, ctxt, probs, rx, ry, w1, w2, wo, wqkv, block_own):
+    win, model = dres.shape
+    heads = 4 * HEADS_T
+    cols_t = HEADS_T * HD
+    lay_t = lay_rows // 4
+    rest = 4 * cols_t + lay_t
+    more = max(0, len(bits_of(n_dp)) - 3)
+    levels = 5 + more
+    f32, bf16 = jnp.float32, jnp.bfloat16
+    shape = jax.ShapeDtypeStruct
+    here = pl.BlockSpec(memory_space=pltpu.VMEM)
+    away = pl.BlockSpec(memory_space=pl.ANY)
+    outs = [
+        (shape((4 * win, model), bf16), away),
+        (shape((4 * win, model), bf16), away),
+        (shape((model, model), bf16), away),
+        (shape((model, model), bf16), away),
+        (shape((rest, model), bf16), away),
+        (shape((lay_rows, model), bf16), away),
+        (shape((SMALL, model), f32), here),
+    ]
+    V = pltpu.VMEM
+    S = pltpu.SemaphoreType.DMA
+    return pl.pallas_call(
+        functools.partial(backward_kernel, n_dp),
+        in_specs=[here] * 3 + [away] * 17,
+        out_specs=[spec for _, spec in outs],
+        out_shape=[s for s, _ in outs],
+        scratch_shapes=[
+            V((8 * model, model), bf16), V((3 * model, model), bf16), V((2, win, model), f32), V((win, model), f32),
+            V((win, model), f32), V((win, model), bf16), V((model, win), bf16), V((win, model), f32),
+            V((win, model), bf16), V((3, model, win), bf16), V((model, win), bf16), V((model, win), bf16),
+            V((win, model), bf16), V((win, lay_rows), bf16), V((model, model), bf16), V((win, win), jnp.int32),
+            V((win, win), jnp.int32), V((2, 2 * BUCKETS * ROWS, win), bf16), V((heads * ROWS, 2 * BUCKETS * ROWS), f32),
+            V((4, model, model), bf16), V((4, model, model), bf16), V((4, lay_t, model), bf16),
+            V((2, model, model), bf16), V((2, model, model), bf16), V((2, rest, model), bf16),
+            V((model, model), bf16), V((model, model), bf16), V((rest, model), bf16),
+            V((model // 2, model), bf16), V((model // 2, model), bf16), V((rest // 2, model), bf16),
+            V((3, model // 8, model), bf16), V((3, model // 8, model), bf16), V((3, rest // 8, model), bf16),
+            V((model // 8, model), bf16), V((model // 8, model), bf16), V((rest // 8, model), bf16),
+            V((2 * more + 1, model // 8, model), bf16), V((2 * more + 1, model // 8, model), bf16),
+            V((2 * more + 1, rest // 8, model), bf16),
+            V((levels + 1, SMALL, model), f32), V((levels, SMALL, model), f32), V((8, model), f32),
+            S((29,)), S((9, 12 + max(1, more))), S((9, 12 + max(1, more))), S((9,)), S((3, 4)), S((3, 3)),
+            S((levels,)), S((levels,)), S((2,)),
+        ],
+        compiler_params=pltpu.CompilerParams(
+            vmem_limit_bytes=63 * 2**20, collective_id=1, has_side_effects=True
+        ),
+        name="backward_window",
+    )(inv, vec, sums, dres, hid, pre, unit, nlow, low, feat, qkvt, ctxt, probs, rx, ry, w1, w2, wo, wqkv, block_own)
 
 
 def local(
@@ -606,7 +1044,6 @@
     zero = jnp.zeros_like(out_bias)
     vec = jnp.stack([out_bias, ln1_gain, ln1_bias, ffn_out_bias, ln2_gain, ln2_bias, zero, zero])
     relx, rely = mine(rel_x)[0], mine(rel_y)[0]
-    count = sum_small(jnp.sum(mask_tokens.astype(jnp.float32)).reshape(1), "dp", n_dp)[0]
 
     (
         probs, qkvt, context_t, layer_low, features, unit_one, inverse_one, normed_low, pre_all, hid_all,
@@ -615,99 +1052,32 @@
         n_dp, mine(tokens_in), mine(box_coords), relx, rely, mine(mask_tokens)[:, None], mine(cotangent), freq,
         layout_weight, vec, cols_own, rows_own, jnp.transpose(qkv_weight, (0, 2, 1)), out_weight, ffn_in_weight, ffn_out_weight,
     )
-    queries, key_rows, values = qkvt[0], qkvt[1], qkvt[2]
-    block_out = lax.all_gather(block_own, "tensor", axis=0, tiled=True)
-    grad_g2, grad_b2, grad_c2 = sums[0], sums[1], sums[2]
-    dffn_low = dresid_two.astype(jnp.bfloat16)
-    grad_w2, grad_w1, grad_c1, dnormed = [], [], [], dresid_two
-    for r in range(n_t):
-        grad_w2.append(nn(hid_all[r].T, dffn_low))
-        gelu_back = jax.vjp(jax.nn.gelu, pre_all[r])[1]
-        dpre = gelu_back(nt(dffn_low, w2[r]))[0].astype(jnp.bfloat16)
-        grad_c1.append(jnp.sum(dpre, axis=0, dtype=jnp.float32))
-        grad_w1.append(nn(normed_low.T, dpre))
-        dnormed = dnormed + nt(dpre, w1[r])
-    grad_w2 = jnp.concatenate(grad_w2, axis=0)
-    grad_w1 = jnp.concatenate(grad_w1, axis=0)
-    grad_c1 = jnp.concatenate(grad_c1)
-    dresidual, grad_g1, grad_b1 = normalize_back(dnormed, unit_one, inverse_one, ln1_gain)
-
-    def reduced(parts):
-        pieces = [
-            jnp.concatenate([part[r * rows : (r + 1) * rows] for part, rows in parts], axis=0)
-            for r in range(n_t)
-        ]
-        return reduce_rows(scatter_pieces(pieces, "tensor", n_t), "dp", n_dp)
-
-    w2_sum = reduced([(grad_w2, hid_t)])
-    w1_sum = reduced([(grad_w1, hid_t)])
-
-    grad_ob = jnp.sum(dresidual, axis=0)
-    dattn_low = dresidual.astype(jnp.bfloat16)
-    grad_ow = nn(context_t, dattn_low)
-    dcontext = nt(wo, dattn_low).astype(jnp.bfloat16)
-    dq, dk, dv, grad_table = attend_back(
-        queries, key_rows, values, probs, dcontext, relx, rely
+    block_out, in_all, sum1, sum2, sum3, lay_all, small = backward_window(
+        n_dp, layout_weight.shape[0], inverse_one, vec, sums, dresid_two, hid_all, pre_all, unit_one, normed_low, layer_low,
+        features, qkvt, context_t, probs, relx, rely, w1, w2, wo, wqkv, block_own,
     )
-    grad_qkv = [nn(d, layer_low) for d in (dq, dk, dv)]
-    grad_bq = jnp.sum(dq, axis=1, dtype=jnp.float32)
-    grad_bv = jnp.sum(dv, axis=1, dtype=jnp.float32)
-    dlayer = dresidual + sum(nn(d.T, w) for d, w in zip((dq, dk, dv), wqkv))
-    grad_lay = nn(features.T, dlayer.astype(jnp.bfloat16))
-    lay_rows = grad_lay.shape[0] // n_t
-    lay_pieces = [
-        lax.dynamic_slice_in_dim(grad_lay, (me ^ r) * lay_rows, lay_rows) for r in range(n_t)
-    ]
-    rest_sum = reduced(
-        [(g, cols_t) for g in grad_qkv]
-        + [(grad_ow, cols_t), (jnp.concatenate(lay_pieces, axis=0), lay_rows)]
-    )
-    din = (dlayer / count).astype(jnp.bfloat16)
-    input_grad = place_pieces(gather_pieces(din, "tensor", n_t), me).astype(jnp.float32)
-    lay_sum = place_pieces(gather_pieces(rest_sum[4 * cols_t :], "tensor", n_t), me)
-
-    def pieces_of(vec, size):
-        return vec.reshape(n_t, size)
-
-    split = jnp.concatenate(
-        [
-            pieces_of(grad_bq, cols_t),
-            pieces_of(grad_bv, cols_t),
-            pieces_of(grad_c1, hid_t),
-            pieces_of(grad_table.T, heads_t * 2 * BUCKETS),
-        ],
-        axis=1,
-    )
-    common = jnp.concatenate([grad_ob, grad_g1, grad_b1, grad_c2, grad_g2, grad_b2])
-    whole = jnp.zeros_like(split)
-    for r in range(n_t):
-        whole = lax.dynamic_update_slice_in_dim(whole, split[r : r + 1], me ^ r, 0)
-    flat = jnp.concatenate([whole.reshape(-1), common])
-    flat = sum_small(sum_small(flat, "tensor", n_t), "dp", n_dp)
-    width = split.shape[1]
-    own = lax.dynamic_slice_in_dim(flat, me * width, width)
-    common = flat[n_t * width :].reshape(6, model)
-
+    f32 = jnp.float32
+    count = small[6, 0]
     factor = group_rates / count
-    f32 = jnp.float32
-    qkv_sum = rest_sum[: 3 * cols_t].reshape(3, cols_t, model)
+    own = lax.dynamic_slice_in_dim(small, 12 + me, 1)[0]
+    qkv_sum = jnp.stack([sum3[2 * cols_t : 3 * cols_t], sum3[3 * cols_t : 4 * cols_t], sum3[:cols_t]])
     return (
         block_out,
-        input_grad,
-        lay_sum.astype(f32) * factor[6],
+        in_all.astype(f32) / count,
+        lay_all.astype(f32) * factor[6],
         jnp.transpose(qkv_sum, (0, 2, 1)).astype(f32) * factor[0],
         own[: 2 * cols_t].reshape(2, cols_t) * factor[0],
-        own[2 * cols_t + hid_t :].reshape(heads_t, 2 * BUCKETS).T * factor[7],
-        rest_sum[3 * cols_t : 4 * cols_t].astype(f32) * factor[1],
-        common[0] * factor[1],
-        common[1] * factor[2],
-        common[2] * factor[2],
-        w1_sum.astype(f32) * factor[3],
-        own[2 * cols_t : 2 * cols_t + hid_t] * factor[3],
-        w2_sum.astype(f32) * factor[4],
-        common[3] * factor[4],
-        common[4] * factor[5],
-        common[5] * factor[5],
+        own[2 * cols_t : 3 * cols_t].reshape(heads_t, 2 * BUCKETS).T * factor[7],
+        sum3[cols_t : 2 * cols_t].astype(f32) * factor[1],
+        small[0] * factor[1],
+        small[1] * factor[2],
+        small[2] * factor[2],
+        sum1.astype(f32) * factor[3],
+        lax.dynamic_slice_in_dim(small, 8 + me, 1)[0] * factor[3],
+        sum2.astype(f32) * factor[4],
+        small[3] * factor[4],
+        small[4] * factor[5],
+        small[5] * factor[5],
     )
 
 

time: 457 us -> 301 us (0.66); the launches traced: 449 us -> 300 us
  Pallas kernels: 104 us -> 260 us
  waiting for transfers between devices: 140 us -> 0 us
  matrix products: 59.5 us -> 0 us
  starting transfers between devices: 44.2 us -> 0 us
  local copies, waits for them, and re-layouts: 46.3 us -> 15.4 us
  between operations: 18 us -> 0.87 us
  other arithmetic: 37.7 us -> 24.3 us
    pallas_call x1, Pallas kernels: 31.9 us -> 188 us  [backward_window(): pl.pallas_call(functools.partial(backward_kernel, n_dp), in_specs=[here]...]
    ppermute x41 -> x0, waiting for transfers between devices: 140 us -> none  [swap(): return lax.ppermute(value, axis, [(i, i ^ bit) for i in range(size)])]
    dot_general x25 -> x0, matrix products: 59.5 us -> none  [the longest x16 40.6 us: nn(): return jnp.dot(a, b, preferred_element_type=jnp.float32)]
    ppermute x41 -> x0, starting transfers between devices: 44.2 us -> none  [swap(): return lax.ppermute(value, axis, [(i, i ^ bit) for i in range(size)])]
    unnamed x110 -> x36, local copies, waits for them, and re-layouts: 19 us -> 2.6 us
    add x14 -> x0, other arithmetic: 8.32 us -> none  [the longest x3 7.77 us: scatter_pieces(): pieces[r ^ bit].astype(jnp.float32) + got.astype(jnp.float32)]
    convert_element_type x6 -> x0, other arithmetic: 8.31 us -> none  [the longest x1 3.53 us: scatter_pieces(): got = swap(pieces.pop(r).astype(jnp.bfloat16), axis, size, bit)]
  transfers between devices with their start and end apart: 42 -> 0, of which waited for: 21 -> 0; matrix products, arithmetic and copies ran while one was open for 25% -> 0% of each run, Pallas kernels for 7% -> 0%
where the time goes in v3:
time: 301 us; the launch traced here: 300 us
  Pallas kernels  260 us (86%)
  other arithmetic  24.3 us (8%)
  local copies, waits for them, and re-layouts  15.4 us (5%)
    pallas_call x1, Pallas kernels, backward_window(): pl.pallas_call(functools.partial(backward_kernel, n_dp), in_specs=[here]...  188 us
    pallas_call x1, Pallas kernels, forward_window(): pl.pallas_call(forward_kernel, in_specs=[here] * 9 + [away] * 6, out_spec...  71.7 us

profile of v3, /device:TPU:0, one launch (start us, length us, event | category | flops | bytes accessed | tf_op | source)
XLA Modules:
  0.0 300.1 jit_solution(3795490998973151530)
XLA Ops:
  0.6 0.0 copy-start
  0.7 2.6 constant_dynamic-slice_fusion.1
  3.3 0.0 copy-done
  3.3 0.9 copy.45.box_ref
  4.2 0.8 dynamic_slice.28
  4.9 0.0 copy-start.11
  4.9 0.0 copy-start.12
  4.9 0.9 copy.44.mask_ref
  5.8 3.1 %dynamic-slice_bitcast_fusion = (s32[512,512]{1,0:T(8,128)}, s32[512,512]{1,0:T(8,128)}) fusion(s32[4,512,512]{2,1,0:T(8,128)} %param.24, s32[]{:T(128)S(6)} %select_n.17, s32[4,512,512]{2,1,0:T(8,128)} %param.23), kind=kLoop, calls=%fused_computation.5 | loop fusion | bytes 4194308 | tf_op jit(solution)/shard_map/squeeze | solution.py:1046
  8.9 0.0 copy-done.14
  8.9 0.1 pad.21.clone
  8.9 0.1 pad_maximum_fusion
  9.0 0.1 copy.43
  9.1 0.7 pad.11.cols_own
  9.8 0.0 copy-done.7
  9.8 0.0 copy-done.8
  9.8 0.0 copy-done.9
  9.8 0.0 copy-done.10
  9.9 0.0 copy-done.11
  9.9 0.7 stack.46.vec_ref
  10.6 0.1 pad.19.clone
  10.7 0.7 maximum_maximum_fusion.rows_own
  11.4 0.1 pad_maximum_fusion.1
  11.4 0.6 broadcast_in_dim.16.freq_ref
  12.0 71.7 %forward_window.1 = (f32[12,512,512]{2,1,0:T(8,128)}, bf16[3,768,512]{2,1,0:T(8,128)(2,1)}, bf16[768,512]{1,0:T(8,128)(2,1)}, bf16[512,768]{1,0:T(8,128)(2,1)}, ...) custom-call(bf16[512,768]{1,0:T(8,128)(2,1)} %get-tuple-element.85.t, ...), custom_call_target="tpu_custom_call" | custom-call | tf_op jit(solution)/shard_map/forward_window/pallas_call | solution.py:385
  83.8 0.0 copy-start.16
  83.8 187.8 %backward_window.1 = (bf16[2048,768]{1,0:T(8,128)(2,1)}, bf16[2048,768]{1,0:T(8,128)(2,1)}, bf16[768,768]{1,0:T(8,128)(2,1)}, bf16[768,768]{1,0:T(8,128)(2,1)}, ...) custom-call(f32[512,1]{1,0:T(8,128)} %get-tuple-element.40.inv_ref, ...), custom_call_target="tpu_custom_call" | custom-call | tf_op jit(solution)/shard_map/backward_window/pallas_call | solution.py:984
  271.6 0.0 copy-start.4
  271.6 1.3 slice.79
  272.9 0.0 copy-done.16
  272.9 0.6 broadcast_divide_fusion
  273.6 0.6 fusion.3
  274.2 3.5 %convert_multiply_fusion = f32[768,768]{1,0:T(8,128)} fusion(bf16[768,768]{1,0:T(8,128)(2,1)} %get-tuple-element.63, f32[]{:T(128)} %bitcast.19), kind=kLoop, calls=%fused_computation.1 | loop fusion | flops 1179648 | bytes 3538948 | tf_op jit(solution)/shard_map/mul | solution.py:1077
  277.7 0.0 copy-done.4
  277.7 2.3 convert_multiply_fusion.1
  280.0 4.9 %multiply_reduce_fusion = (f32[768]{0:T(1024)}, f32[768]{0:T(1024)}, f32[768]{0:T(1024)}, f32[768]{0:T(1024)}, f32[768]{0:T(1024)}, /*index=5*/f32[768]{0:T(1024)}, f32[768]{0:T(1024)}) fusion(f32[16,768]{1,0:T(8,128)} %get-tuple-element.59, f32[]{:T(128)} %bitcast.20, f32[]{:T(128)} %bitcast.19, f32[]{:T(128)} %bitcast.18, s32[]{:T(128)S(6)} %select_n.19, ...), kind=kLoop, calls=%fused_computation.14 | loop fusion | flops 5376 | bytes 43032 | tf_op jit(solution)/shard_map/mul | solution.py:1080
  284.9 0.0 copy-done.5
  284.9 1.5 convert_multiply_fusion.3
  286.4 1.5 fusion.2
  287.9 0.7 mul.140
  288.5 1.3 fusion.1
  289.9 0.7 mul.137
  290.5 0.1 slice_bitcast_fusion.2
  290.6 2.1 multiply_bitcast_fusion
  292.7 1.8 convert_multiply_fusion.2
  294.5 3.9 %convert_divide_fusion = f32[2048,768]{1,0:T(8,128)} fusion(bf16[2048,768]{1,0:T(8,128)(2,1)S(1)} %copy-done.3, f32[]{:T(128)} %bitcast.7), kind=kLoop, calls=%fused_computation | loop fusion | flops 3145728 | bytes 9437188 | tf_op jit(solution)/shard_map/div | solution.py:1066
  298.4 1.7 copy.47
  300.1 0.0 copy-done.1
  (31 shorter events, 0.1 us)
Async XLA Ops:
  0.6 2.6 copy-start
  3.3 5.6 %copy-start.14 = (f32[2,192]{1,0:T(2,128)S(1)}, f32[2,192]{1,0:T(2,128)}, u32[]{:S(2)}) copy-start(f32[2,192]{1,0:T(2,128)} %param.29) | copy-start | bytes 4612
  4.9 4.9 %copy-start.7 = (f32[768]{0:T(1024)S(1)}, f32[768]{0:T(1024)}, u32[]{:S(2)}) copy-start(f32[768]{0:T(1024)} %param.32) | copy-start | bytes 9220
  4.9 4.9 %copy-start.8 = (f32[768]{0:T(1024)S(1)}, f32[768]{0:T(1024)}, u32[]{:S(2)}) copy-start(f32[768]{0:T(1024)} %param.33) | copy-start | bytes 9220
  4.9 4.9 %copy-start.9 = (f32[768]{0:T(1024)S(1)}, f32[768]{0:T(1024)}, u32[]{:S(2)}) copy-start(f32[768]{0:T(1024)} %param.34) | copy-start | bytes 9220
  4.9 4.9 %copy-start.10 = (f32[768]{0:T(1024)S(1)}, f32[768]{0:T(1024)}, u32[]{:S(2)}) copy-start(f32[768]{0:T(1024)} %param.38) | copy-start | bytes 9220
  4.9 5.0 %copy-start.11 = (f32[768]{0:T(1024)S(1)}, f32[768]{0:T(1024)}, u32[]{:S(2)}) copy-start(f32[768]{0:T(1024)} %param.39) | copy-start | bytes 9220
  4.9 5.0 %copy-start.12 = (f32[768]{0:T(1024)S(1)}, f32[768]{0:T(1024)}, u32[]{:S(2)}) copy-start(f32[768]{0:T(1024)} %param.40) | copy-start | bytes 9220
  5.8 4.8 %copy-start.15 = (bf16[64,3]{0,1:T(4,128)(2,1)S(1)}, bf16[64,3]{0,1:T(4,128)(2,1)}, u32[]{:S(2)}) copy-start(bf16[64,3]{0,1:T(4,128)(2,1)} %param.30) | copy-start | bytes 1156
  5.8 4.8 %copy-start.13 = (f32[768]{0:T(1024)S(1)}, f32[768]{0:T(1024)}, u32[]{:S(2)}) copy-start(f32[768]{0:T(1024)} %param.36) | copy-start | bytes 9220
  83.8 189.1 %copy-start.16 = (f32[8]{0:T(128)S(1)}, f32[8]{0:T(128)}, u32[]{:S(2)}) copy-start(f32[8]{0:T(128)} %param.41) | copy-start | bytes 100
  271.6 6.1 %copy-start.4 = (bf16[768,768]{1,0:T(8,128)(2,1)S(1)}, bf16[768,768]{1,0:T(8,128)(2,1)}, u32[]{:S(2)}) copy-start(bf16[768,768]{1,0:T(8,128)(2,1)} %get-tuple-element.62) | copy-start | bytes 3538948
  277.7 7.2 %copy-start.5 = (bf16[896,768]{1,0:T(8,128)(2,1)S(1)}, bf16[896,768]{1,0:T(8,128)(2,1)}, u32[]{:S(2)}) copy-start(bf16[896,768]{1,0:T(8,128)(2,1)} %get-tuple-element.61) | copy-start | bytes 4128772
  286.4 6.3 %copy-start.6 = (bf16[512,768]{1,0:T(8,128)(2,1)S(1)}, bf16[512,768]{1,0:T(8,128)(2,1)}, u32[]{:S(2)}) copy-start(bf16[512,768]{1,0:T(8,128)(2,1)} %get-tuple-element.60) | copy-start | bytes 2359300
  290.6 3.9 %copy-start.3 = (bf16[2048,768]{1,0:T(8,128)(2,1)S(1)}, bf16[2048,768]{1,0:T(8,128)(2,1)}, u32[]{:S(2)}) copy-start(bf16[2048,768]{1,0:T(8,128)(2,1)} %get-tuple-element.58) | copy-start | bytes 9437188
  294.5 3.9 %copy-start.2 = (bf16[2048,768]{1,0:T(8,128)(2,1)S(1)}, bf16[2048,768]{1,0:T(8,128)(2,1)}, u32[]{:S(2)}) copy-start(bf16[2048,768]{1,0:T(8,128)(2,1)} %get-tuple-element.104) | copy-start | bytes 9437188
  298.4 1.7 copy-start.1

commit v4 on v3

--- a/solution.py
+++ b/solution.py
@@ -15,6 +15,40 @@
 ROWS = 16
 HEADS_T = 3
 MESH = pl.DeviceIdType.MESH
+
+ORDERS = {
+    "A": (True, False, True),
+    "B": (True, False, False),
+    "C": (True, False, True),
+}
+SCHEDULE = {
+    "start": ("blk0", "blk1",),
+    "ffn0.1": ("blkpass0",),
+    "ffn1.0": ("blkpass1",),
+    "ffn3.1": ("A1.1", "A0.1",),
+    "h0": ("A2.1",),
+    "h2": ("A0.2",),
+    "h5": ("B1.1", "B0.1", "A0.3",),
+    "h6": ("B2.1", "A1.2",),
+    "h8": ("A0.4", "A2.2", "B1.2",),
+    "h10": ("A1.3", "B0.2", "B2.2",),
+    "h11": ("blk2", "blk3",),
+    "pq": ("A2.3",),
+    "pk": ("B1.3", "blkpass2",),
+    "dl0": ("A1.4", "blkpass3",),
+    "dl3": ("B0.3",),
+    "t0": ("Cb.1", "B2.3", "Ca.1", "A2.4",),
+    "t3": ("Cc.1", "B1.4",),
+    "t6": ("B0.4", "Ca.2",),
+    "t9": ("B2.4",),
+    "t11": ("Cc.2",),
+    "t14": ("Ca.3",),
+    "t15": ("Cc.3", "igpass",),
+    "tail": (
+        "A0.5", "A1.5", "A2.5", "B1.5", "B0.5", "sm0", "Ca.4", "Cb.2", "B2.5", "sm1", "Cc.4", "Ca.5", "Cb.3", "sm2",
+        "Cc.5", "lay", "Cb.4", "laypass", "sm3", "sm4", "Cb.5",
+    ),
+}
 
 
 def nt(a, b):
@@ -435,16 +469,17 @@
         total = dst[sl, :].astype(jnp.float32)
         for ref in more:
             total = total + ref[sl, :].astype(jnp.float32)
-        dst[sl, :] = total.astype(jnp.bfloat16)
+        dst[sl, :] = total.astype(dst.dtype)
 
 
 class Reduce:
-    def __init__(self, slot, rows, x_first, part, core, first, second, quarters, final, extra, result, sems, peers):
-        self.slot, self.rows, self.x_first, self.part = slot, rows, x_first, part
+    def __init__(self, slot, rows, x_first, part, core, first, second, quarters, final, extra, result, acc, sems, peers):
+        self.slot, self.rows, self.x_first, self.part, self.acc = slot, rows, x_first, part, acc
         self.core, self.first, self.second, self.quarters, self.final = core, first, second, quarters, final
         self.extra, self.result = extra, result
         self.send, self.recv, self.here = sems
         self.mate, self.across, self.beside, self.along, self.further, self.side, self.level = peers
+        self.total = core.at[0] if acc is None else acc
 
     def move(self, k, src, dst, peer):
         return remote(src, dst, self.send.at[self.slot, k], self.recv.at[self.slot, k], peer)
@@ -458,16 +493,17 @@
         q = self.rows // 8
         return pl.ds(pl.multiple_of(self.side * (self.rows // 2) + level * q, q), q)
 
-    def moves(self, stage):
+    def moves(self, stage, piece=None):
+        h = self.rows // 2
         if stage == 0:
-            return [self.move(k, self.part(2 * k + 1), self.core.at[k], self.mate) for k in range(2)]
+            return [self.move(p, self.part(p), self.core.at[p], self.mate) for p in range(2) if piece in (None, p)]
         if stage == 1 and self.x_first:
-            return [self.move(2, self.core.at[1], self.first, self.across)]
+            return [self.move(2, self.core.at[1], self.first, self.across)] if piece != 0 else []
         if stage == 1:
-            h = self.rows // 2
             return [
-                self.move(2 + k, self.core.at[k, self.half(False)], self.first.at[pl.ds(k * h, h)], self.beside)
-                for k in range(2)
+                self.move(2 + p, self.core.at[p, self.half(False)], self.first.at[pl.ds(p * h, h)], self.beside)
+                for p in range(2)
+                if piece in (None, p)
             ]
         if stage == 2 and self.x_first:
             return [self.move(4, self.core.at[0, self.half(False)], self.second, self.beside)]
@@ -495,23 +531,37 @@
     def final_of(self, k):
         return self.final if k == 0 else self.extra.at[len(self.further) + k]
 
+    def round_off(self, rows):
+        if self.acc is not None:
+            self.core[0, rows, :] = self.acc[rows, :].astype(jnp.bfloat16)
+
+    def merge(self, piece, rows, value):
+        value = value + self.core[piece, rows, :].astype(jnp.float32)
+        if piece == 0:
+            self.total[rows, :] = value.astype(self.total.dtype)
+        else:
+            self.core[1, rows, :] = value.astype(jnp.bfloat16)
+
+    def from_mate(self, piece):
+        for m in self.moves(0, piece):
+            m.wait_recv()
+
     def take(self, stage):
         for m in self.moves(stage):
             m.wait_recv()
         h = self.rows // 2
-        if stage == 0:
-            for k in range(2):
-                add_into(self.core.at[k], [self.part(2 * k)])
         if stage == 1 and self.x_first:
-            add_into(self.core.at[0], [self.first])
+            add_into(self.total, [self.first])
         if stage == 1 and not self.x_first:
-            for k in range(2):
-                add_into(self.core.at[k, self.half(True)], [self.first.at[pl.ds(k * h, h)]])
+            add_into(self.core.at[1, self.half(True)], [self.first.at[pl.ds(h, h)]])
+            add_into(self.total.at[self.half(True)], [self.first.at[pl.ds(0, h)]])
         if stage == 2:
-            add_into(self.core.at[0, self.half(True)], [self.second])
+            add_into(self.total.at[self.half(True)], [self.second])
         if stage == 3:
-            self.final[...] = self.core[0, self.quarter(self.level), :]
-            add_into(self.final, [self.quarters.at[k] for k in range(3)])
+            value = self.total[self.quarter(self.level), :].astype(jnp.float32)
+            for k in range(3):
+                value = value + self.quarters[k].astype(jnp.float32)
+            self.final[...] = value.astype(jnp.bfloat16)
             for k in range(len(self.further)):
                 self.more(k).start()
                 self.more(k).wait()
@@ -523,8 +573,14 @@
         if stage == 4:
             self.own_copy().wait()
 
-    def go(self, stage):
-        for m in self.moves(stage):
+    def go(self, stage, piece=None):
+        if stage == 1 and not self.x_first and piece == 0:
+            self.round_off(self.half(False))
+        if stage == 2 and self.x_first:
+            self.round_off(self.half(False))
+        if stage == 3:
+            self.round_off(self.half(True))
+        for m in self.moves(stage, piece):
             m.start()
 
     def next(self, stage):
@@ -560,7 +616,7 @@
     block_all, in_all, red1, red2, red3, lay_all, small_out,
     arena, hidb, preb, dres, unit, nlow, nlow_t, dn, low_rows, qkvb, ctxtb, dctx, lowb, featb, wob, rxb, ryb, hot, acc,
     part1, part2, part3, core1, core2, core3, first1, first2, first3, second1, second2, second3,
-    quarters1, quarters2, quarters3, final1, final2, final3, extra1, extra2, extra3, small, small_in, short,
+    quarters1, quarters2, quarters3, final1, final2, final3, extra1, extra2, extra3, acc3, small, small_in, short,
     load_sem, send, recv, here, share_send, share_recv, small_send, small_recv, p_sem,
 ):
     t, d = lax.axis_index("tensor"), lax.axis_index("dp")
@@ -586,7 +642,7 @@
     def h_rows(r):
         return pl.ds(r * win, win)
 
-    order = (1, 3, 2, 0)
+    order = (3, 1, 2, 0)
     ld_dres = load(0, dres_in, dres)
     ld_hid = {r: load(1 + r, hid_in.at[r], hidb.at[h_rows(r)]) for r in order}
     ld_w2 = {r: load(5 + r, w2_in.at[r], arena.at[w_rows(r)]) for r in order}
@@ -615,18 +671,17 @@
     for c in ld_rest[1:]:
         c.start()
 
-    def reduce_of(slot, rows, at, x_first, part, core, first, second, quarters, final, extra, result):
-        h, q = rows // 2, rows // 8
-        return Reduce(
-            slot, rows, x_first, part, core.at[:, pl.ds(at, rows)], first.at[pl.ds(at, rows)],
-            second.at[pl.ds(at // 2, h)], quarters.at[:, pl.ds(at // 8, q)], final.at[pl.ds(at // 8, q)],
-            extra.at[:, pl.ds(at // 8, q)], result.at[pl.ds(at, rows)], sems, peers,
-        )
-
-    def chunks(slot, sizes, x_first, parts, *buffers):
+    def chunks(slot, sizes, orders, parts, core, first, second, quarters, final, extra, result, acc=None):
         out, at = [], 0
-        for k, (rows, part) in enumerate(zip(sizes, parts)):
-            out.append(reduce_of(slot + k, rows, at, x_first, part, *buffers))
+        for k, (rows, x_first, part) in enumerate(zip(sizes, orders, parts)):
+            q = pl.ds(at // 8, rows // 8)
+            out.append(
+                Reduce(
+                    slot + k, rows, x_first, part, core.at[:, pl.ds(at, rows)], first.at[pl.ds(at, rows)],
+                    second.at[pl.ds(at // 2, rows // 2)], quarters.at[:, q], final.at[q], extra.at[:, q],
+                    result.at[pl.ds(at, rows)], None if acc is None else acc.at[pl.ds(at, rows)], sems, peers,
+                )
+            )
             at += rows
         return out
 
@@ -634,24 +689,28 @@
     sizes = [third] * 3
 
     def thirds(ref):
-        return [lambda r, k=k: ref.at[r, pl.ds(k * third, third)] for k in range(3)]
-
-    s2 = chunks(0, sizes, True, thirds(part2), core2, first2, second2, quarters2, final2, extra2, red2)
-    s1 = chunks(3, sizes, False, thirds(part1), core1, first1, second1, quarters1, final1, extra1, red1)
+        return [lambda p, k=k: ref.at[p, pl.ds(k * third, third)] for k in range(3)]
+
+    s2 = chunks(
+        0, sizes, ORDERS["A"], thirds(part2), core2, first2, second2, quarters2, final2, extra2, red2
+    )
+    s1 = chunks(
+        3, sizes, ORDERS["B"], thirds(part1), core1, first1, second1, quarters1, final1, extra1, red1
+    )
     lay_t = lay_all.shape[0] // 4
     s3 = chunks(
-        6, [2 * cols_t, 2 * cols_t, lay_t], True,
+        6, [2 * cols_t, 2 * cols_t, lay_t], ORDERS["C"],
         [
-            lambda r: part2.at[r, pl.ds(0, 2 * cols_t)],
-            lambda r: part2.at[r, pl.ds(2 * cols_t, 2 * cols_t)],
-            lambda r: part3.at[r],
+            lambda p: part2.at[p, pl.ds(0, 2 * cols_t)],
+            lambda p: part2.at[p, pl.ds(2 * cols_t, 2 * cols_t)],
+            lambda p: part3.at[p],
         ],
-        core3, first3, second3, quarters3, final3, extra3, red3,
+        core3, first3, second3, quarters3, final3, extra3, red3, acc3,
     )
 
-    def share(k, src, whole, rows):
+    def share(k, src, whole, rows, part=0, parts=1):
         def at(index):
-            return whole.at[pl.ds(pl.multiple_of(index * rows, rows), rows)]
+            return whole.at[pl.ds(pl.multiple_of((index * parts + part) * rows, rows), rows)]
 
         def moved(j, from_ref, index, peer):
             return remote(from_ref, at(index), share_send.at[k, j], share_recv.at[k, j], peer)
@@ -679,12 +738,57 @@
         for name in ("across", "mate", "pass"):
             c[name].wait_send()
 
-    sh_block = share(0, block_in, block_all, win)
-    sh_in = share(1, low_rows, in_all, win)
-    sh_lay = share(2, red3.at[pl.ds(4 * cols_t, lay_t)], lay_all, lay_t)
+    quarter_win = win // 4
+    sh_block = [
+        share(k, block_in.at[pl.ds(k * quarter_win, quarter_win)], block_all, quarter_win, k, 4) for k in range(4)
+    ]
+    sh_in = share(4, low_rows, in_all, win)
+    sh_lay = share(5, red3.at[pl.ds(4 * cols_t, lay_t)], lay_all, lay_t)
+    bits = [mate, across, beside, along[1], along[2]] + further
+
+    def small_move(k):
+        return remote(small.at[k], small_in.at[k], small_send.at[k], small_recv.at[k], bits[k])
+
+    def small_step(k):
+        small_move(k).wait()
+        small[k + 1] = small[k] + small_in[k]
+        if k + 1 < len(bits):
+            small_move(k + 1).start()
+
+    named = {f"A{k}": g for k, g in enumerate(s2)}
+    named.update({f"B{k}": g for k, g in enumerate(s1)})
+    named.update({f"C{k}": g for k, g in zip("abc", s3)})
+
+    def run(event):
+        if event[:2] in named:
+            named[event[:2]].next(int(event[3:]))
+        elif event[:7] == "blkpass":
+            share_pass(sh_block[int(event[7:])])
+        elif event[:3] == "blk":
+            share_start(sh_block[int(event[3:])])
+        elif event == "igpass":
+            share_pass(sh_in)
+        elif event == "lay":
+            share_start(sh_lay)
+        elif event == "laypass":
+            share_pass(sh_lay)
+        elif event[:2] == "sm":
+            small_step(int(event[2:]))
+
+    def at_slot(name, index=None):
+        if index is None:
+            for event in SCHEDULE.get(name, ()):
+                run(event)
+            return
+        for key, todo in SCHEDULE.items():
+            if key.startswith(name) and key[len(name) :].isdigit():
+                @pl.when(index == int(key[len(name) :]))
+                def _(todo=todo):
+                    for event in todo:
+                        run(event)
 
     signal_peers([mate, across, beside] + along[1:] + further)
-    share_start(sh_block)
+    at_slot("start")
 
     small[0] = jnp.zeros_like(small[0])
     small[0, 3:4, :] = sums_ref[2:3, :]
@@ -705,17 +809,31 @@
         sl = pl.ds(pl.multiple_of(i * block, block), block)
         low_rows[sl, :] = dres[sl, :].astype(bf16)
 
-    for j, r in enumerate(order):
+    def grad_w2(r, c):
+        sl = pl.ds(pl.multiple_of(c * third, third), third)
+        return tn(hidb[h_rows(r), sl], low_rows[...])
+
+    def grad_w1(r, c):
+        sl = pl.ds(pl.multiple_of(c * third, third), third)
+        return nn(nlow_t[sl, :], hidb[h_rows(r), :])
+
+    def for_mate(group, grad, r, part):
+        @pl.loop(0, 3)
+        def _(c):
+            part[r // 2, pl.ds(pl.multiple_of(c * third, third), third), :] = grad(r, c).astype(bf16)
+
+        for g in group:
+            g.go(0, r // 2)
+
+    def for_own(group, grad, r):
+        for c, g in enumerate(group):
+            g.from_mate(r // 2)
+            g.merge(r // 2, pl.ds(0, third), grad(r, c))
+            g.go(1, r // 2)
+
+    for r in order[:2]:
         ld_hid[r].wait()
-
-        @pl.loop(0, 3)
-        def _(c, r=r):
-            sl = pl.ds(pl.multiple_of(c * third, third), third)
-            part2[r, sl, :] = tn(hidb[h_rows(r), sl], low_rows[...]).astype(bf16)
-
-        if j == 1:
-            for g in s2:
-                g.go(0)
+        for_mate(s2, grad_w2, r, part2)
 
     ld_rest[0].wait()
     nlow_t[...] = nlow[...].astype(f32).T.astype(bf16)
@@ -736,21 +854,19 @@
             small[0, row, :] += jnp.sum(dpre.astype(f32), axis=0, keepdims=True)
             more = nt(dpre, arena[w_rows(4 + r), :])
             dn[sl, :] = more if j == 0 else dn[sl, :] + more
+            at_slot(f"ffn{j}.", i)
 
         if j + 2 < 4:
             ld_pre[order[j + 2]].start()
-
-        @pl.loop(0, 3)
-        def _(c, r=r):
-            sl = pl.ds(pl.multiple_of(c * third, third), third)
-            part1[r, sl, :] = nn(nlow_t[sl, :], hidb[h_rows(r), :]).astype(bf16)
-
+        if j < 2:
+            for_mate(s1, grad_w1, r, part1)
+        else:
+            for_own(s1, grad_w1, r)
         if j == 0:
-            for g in s2:
-                g.next(0)
-        if j == 1:
-            for g in s1:
-                g.go(0)
+            for q in order[2:]:
+                ld_hid[q].wait()
+                for_own(s2, grad_w2, q)
+        at_slot(f"ffn{j}.g")
 
     for c in ld_wqkv:
         c.start()
@@ -760,9 +876,6 @@
 
     for h in range(2):
         p_load(h, h).start()
-    for g in s1:
-        g.next(0)
-    share_pass(sh_block)
     for g in s2:
         g.sent(0)
 
@@ -783,31 +896,16 @@
         small[0, 1:2, :] += jnp.sum(up * units, axis=0, keepdims=True)
         small[0, 2:3, :] += jnp.sum(up, axis=0, keepdims=True)
 
+    at_slot("ln")
     for c in ld_rest[2:]:
         c.wait()
 
     @pl.loop(0, 4)
     def _(r):
         sl = pl.ds(pl.multiple_of(r * cols_t, cols_t), cols_t)
-        part2[r, cols_t : 2 * cols_t, :] = nn(ctxtb[sl, :], low_rows[...]).astype(bf16)
         dctx[sl, :] = nt(wob[sl, :], low_rows[...]).astype(bf16)
 
-    def events(index, table):
-        for at, todo in table.items():
-            @pl.when(index == at)
-            def _(todo=todo):
-                for f in todo:
-                    f()
-
-    def ev(g, stage):
-        return lambda: g.next(stage)
-
-    in_heads = {
-        3: [ev(s2[0], 1)],
-        6: [ev(s1[0], 1), ev(s2[1], 1)],
-        9: [ev(s1[1], 1), ev(s2[0], 2)],
-        11: [ev(s2[2], 1), ev(s1[2], 1)],
-    }
+    at_slot("ow")
 
     @pl.loop(0, heads)
     def _(h):
@@ -831,18 +929,37 @@
         def _():
             p_load(h + 2, slot).start()
 
-        events(h, in_heads)
+        at_slot("h", h)
 
     for c in ld_wqkv:
         c.wait()
-    for n, at, g in ((2, 0, s3[0]), (0, 2 * cols_t, None), (1, 3 * cols_t, s3[1])):
-        @pl.loop(0, 4)
-        def _(r, n=n, at=at):
-            sl = pl.ds(pl.multiple_of(r * cols_t, cols_t), cols_t)
-            part2[r, at : at + cols_t, :] = nn(qkvb[n, sl, :], lowb[...]).astype(bf16)
-
-        if g is not None:
-            g.go(0)
+    def rows_of(r):
+        return pl.ds(r * cols_t, cols_t)
+
+    def grad_out(r):
+        return nn(ctxtb[rows_of(r), :], low_rows[...])
+
+    def grad_proj(n, r):
+        return nn(qkvb[n, rows_of(r), :], lowb[...])
+
+    halves = (
+        (s3[0], lambda r: grad_proj(2, r), grad_out),
+        (s3[1], lambda r: grad_proj(0, r), lambda r: grad_proj(1, r)),
+    )
+    for k, (g, upper, lower) in enumerate(halves):
+        for r in (3, 1):
+            at = 2 * cols_t * k
+            part2[r // 2, at : at + cols_t, :] = upper(r).astype(bf16)
+            part2[r // 2, at + cols_t : at + 2 * cols_t, :] = lower(r).astype(bf16)
+            g.go(0, r // 2)
+    at_slot("pq")
+    for g, upper, lower in halves:
+        for r in (2, 0):
+            g.from_mate(r // 2)
+            g.merge(r // 2, pl.ds(0, cols_t), upper(r))
+            g.merge(r // 2, pl.ds(cols_t, cols_t), lower(r))
+            g.go(1, r // 2)
+    at_slot("pk")
 
     @pl.loop(0, win // block)
     def _(i):
@@ -850,16 +967,27 @@
         value = dn[sl, :]
         for n in range(3):
             value = value + tn(qkvb[n, :, sl], hidb[pl.ds(n * model, model), :])
-        low_rows[sl, :] = value.astype(bf16)
-
+        dn[sl, :] = value
+        at_slot("dl", i)
+
+    low_rows[...] = dn[...].astype(bf16)
+
+    def grad_lay(r):
+        index = t
+        for bit in (1, 2):
+            if r & bit:
+                index = xor_index(index, bit)
+        return tn(featb[:, pl.ds(pl.multiple_of(index * lay_t, lay_t), lay_t)], low_rows[...])
+
+    for r in (3, 1):
+        part3[r // 2] = grad_lay(r).astype(bf16)
+        s3[2].go(0, r // 2)
+    at_slot("la")
+    for r in (2, 0):
+        s3[2].from_mate(r // 2)
+        s3[2].merge(r // 2, pl.ds(0, lay_t), grad_lay(r))
+        s3[2].go(1, r // 2)
     share_start(sh_in)
-    for c in range(4):
-        rows = [c ^ r for r in range(4)]
-        value = tn(featb[:, c * lay_t : (c + 1) * lay_t], low_rows[...]).astype(bf16)
-        part3[xor_level(t, c)] = value
-    s3[2].go(0)
-    for g in s3:
-        g.next(0)
 
     ones = jnp.ones((8, win), bf16)
     short[...] = jnp.zeros_like(short)
@@ -871,17 +999,6 @@
     acc[...] = jnp.zeros_like(acc)
     one, zero = bf16(1), bf16(0)
     hots = BUCKETS * ROWS
-    in_table = {
-        1: [ev(s1[0], 2), ev(s2[1], 2)],
-        3: [ev(s2[0], 3), ev(s1[1], 2)],
-        5: [ev(s1[0], 3), ev(s2[2], 2)],
-        7: [ev(s2[1], 3), ev(s1[2], 2), ev(s2[0], 4)],
-        9: [ev(s1[1], 3), ev(s2[2], 3), ev(s1[0], 4)],
-        11: [ev(s1[2], 3), ev(s2[1], 4)],
-        13: [ev(s1[1], 4), ev(s2[2], 4), ev(s1[2], 4)],
-        15: [ev(s3[0], 1)],
-    }
-
     @pl.loop(0, win // ROWS // 2)
     def _(i):
         total = None
@@ -898,7 +1015,7 @@
             more = nt(left, hot[u])
             total = more if total is None else total + more
         acc[...] += total
-        events(i, in_table)
+        at_slot("t", i)
 
     row = lax.broadcasted_iota(jnp.int32, (ROWS, 2 * hots), 0)
     col = lax.broadcasted_iota(jnp.int32, (ROWS, 2 * hots), 1) % ROWS
@@ -924,32 +1041,12 @@
     for r in range(4):
         small[0, own_row(12, r), :] = short[r : r + 1, :]
 
-    bits = [mate, across, beside, along[1], along[2]] + further
-
-    def small_move(k):
-        return remote(small.at[k], small_in.at[k], small_send.at[k], small_recv.at[k], bits[k])
-
-    def small_step(k):
-        def run():
-            small_move(k).wait()
-            small[k + 1] = small[k] + small_in[k]
-            if k + 1 < len(bits):
-                small_move(k + 1).start()
-
-        return run
-
     small_move(0).start()
-    steps = [small_step(k) for k in range(len(bits))]
-    tail = [
-        ev(s3[1], 1), steps[0], ev(s3[2], 1), ev(s3[0], 2), steps[1], ev(s3[1], 2), ev(s3[2], 2), ev(s3[0], 3),
-        steps[2], ev(s3[1], 3), ev(s3[2], 3), ev(s3[2], 4), ev(s3[0], 4), ev(s3[1], 4), steps[3],
-        ev(s3[2], 5), lambda: share_start(sh_lay), steps[4], ev(s3[0], 5), ev(s3[1], 5),
-        lambda: share_pass(sh_in), lambda: share_pass(sh_lay),
-    ] + steps[5:] + [ev(g, 5) for g in s2 + s1]
-    for f in tail:
-        f()
+    at_slot("tail")
+    for k in range(5, len(bits)):
+        small_step(k)
     small_out[...] = small[len(bits)]
-    for c in (sh_block, sh_in, sh_lay):
+    for c in sh_block + [sh_in, sh_lay]:
         share_end(c)
     for g in s1 + s3:
         g.sent(0)
@@ -992,7 +1089,7 @@
             V((win, model), bf16), V((3, model, win), bf16), V((model, win), bf16), V((model, win), bf16),
             V((win, model), bf16), V((win, lay_rows), bf16), V((model, model), bf16), V((win, win), jnp.int32),
             V((win, win), jnp.int32), V((2, 2 * BUCKETS * ROWS, win), bf16), V((heads * ROWS, 2 * BUCKETS * ROWS), f32),
-            V((4, model, model), bf16), V((4, model, model), bf16), V((4, lay_t, model), bf16),
+            V((2, model, model), bf16), V((2, model, model), bf16), V((2, lay_t, model), bf16),
             V((2, model, model), bf16), V((2, model, model), bf16), V((2, rest, model), bf16),
             V((model, model), bf16), V((model, model), bf16), V((rest, model), bf16),
             V((model // 2, model), bf16), V((model // 2, model), bf16), V((rest // 2, model), bf16),
@@ -1000,8 +1097,8 @@
             V((model // 8, model), bf16), V((model // 8, model), bf16), V((rest // 8, model), bf16),
             V((2 * more + 1, model // 8, model), bf16), V((2 * more + 1, model // 8, model), bf16),
             V((2 * more + 1, rest // 8, model), bf16),
-            V((levels + 1, SMALL, model), f32), V((levels, SMALL, model), f32), V((8, model), f32),
-            S((29,)), S((9, 12 + max(1, more))), S((9, 12 + max(1, more))), S((9,)), S((3, 4)), S((3, 3)),
+            V((rest, model), f32), V((levels + 1, SMALL, model), f32), V((levels, SMALL, model), f32), V((8, model), f32),
+            S((29,)), S((9, 12 + max(1, more))), S((9, 12 + max(1, more))), S((9,)), S((6, 4)), S((6, 3)),
             S((levels,)), S((levels,)), S((2,)),
         ],
         compiler_params=pltpu.CompilerParams(

time: 301 us -> 248 us (0.82)
  Pallas kernels: 260 us -> 206 us
    pallas_call x1, Pallas kernels: 188 us -> 135 us  [backward_window(): pl.pallas_call(functools.partial(backward_kernel, n_dp), in_specs=[here]...]
where the time goes in v4:
time: 248 us; the launch traced here: 247 us
  Pallas kernels  206 us (83%)
  other arithmetic  24.3 us (10%)
  local copies, waits for them, and re-layouts  15.4 us (6%)
    pallas_call x1, Pallas kernels, backward_window(): pl.pallas_call(functools.partial(backward_kernel, n_dp), in_specs=[here]...  135 us
    pallas_call x1, Pallas kernels, forward_window(): pl.pallas_call(forward_kernel, in_specs=[here] * 9 + [away] * 6, out_spec...  71.7 us

profile of v4, /device:TPU:0, one launch (start us, length us, event | category | flops | bytes accessed | tf_op | source)
XLA Modules:
  0.0 247.0 jit_solution(4525708640097165496)
XLA Ops:
  0.6 0.0 copy-start
  0.7 2.6 %constant_dynamic-slice_fusion.1 = (bf16[512,768]{1,0:T(8,128)(2,1)}, bf16[512,768]{1,0:T(8,128)(2,1)}) fusion(bf16[2048,768]{1,0:T(8,128)(2,1)} %param.26, s32[]{:T(128)S(6)} %select_n.16, bf16[2048,768]{1,0:T(8,128)(2,1)} %param.21), kind=kLoop, calls=%fused_computation.22 | loop fusion | bytes 3145732 | tf_op jit(solution)/shard_map/dynamic_slice | solution.py:1126
  3.3 0.0 copy-done
  3.3 0.9 copy.45.box_ref
  4.2 0.8 dynamic_slice.28
  4.9 0.0 copy-start.11
  4.9 0.0 copy-start.12
  4.9 0.9 copy.44.mask_ref
  5.8 3.1 %dynamic-slice_bitcast_fusion = (s32[512,512]{1,0:T(8,128)}, s32[512,512]{1,0:T(8,128)}) fusion(s32[4,512,512]{2,1,0:T(8,128)} %param.24, s32[]{:T(128)S(6)} %select_n.17, s32[4,512,512]{2,1,0:T(8,128)} %param.23), kind=kLoop, calls=%fused_computation.5 | loop fusion | bytes 4194308 | tf_op jit(solution)/shard_map/squeeze | solution.py:1143
  8.9 0.0 copy-done.14
  8.9 0.1 pad.21.clone
  8.9 0.1 pad_maximum_fusion
  9.0 0.1 copy.43
  9.1 0.7 pad.11.cols_own
  9.8 0.0 copy-done.7
  9.8 0.0 copy-done.8
  9.8 0.0 copy-done.9
  9.8 0.0 copy-done.10
  9.9 0.0 copy-done.11
  9.9 0.0 copy-done.12
  9.9 0.7 stack.46.vec_ref
  10.6 0.0 copy-done.15
  10.6 0.1 pad.19.clone
  10.7 0.7 maximum_maximum_fusion.rows_own
  11.4 0.1 pad_maximum_fusion.1
  11.4 0.6 broadcast_in_dim.16.freq_ref
  12.0 71.7 %forward_window.1 = (f32[12,512,512]{2,1,0:T(8,128)}, bf16[3,768,512]{2,1,0:T(8,128)(2,1)}, bf16[768,512]{1,0:T(8,128)(2,1)}, bf16[512,768]{1,0:T(8,128)(2,1)}, ...) custom-call(bf16[512,768]{1,0:T(8,128)(2,1)} %get-tuple-element.85.t, ...), custom_call_target="tpu_custom_call" | custom-call | tf_op jit(solution)/shard_map/forward_window/pallas_call | solution.py:419
  83.8 0.0 copy-start.16
  83.8 134.7 %backward_window.1 = (bf16[2048,768]{1,0:T(8,128)(2,1)}, bf16[2048,768]{1,0:T(8,128)(2,1)}, bf16[768,768]{1,0:T(8,128)(2,1)}, bf16[768,768]{1,0:T(8,128)(2,1)}, ...) custom-call(f32[512,1]{1,0:T(8,128)} %get-tuple-element.40.inv_ref, ...), custom_call_target="tpu_custom_call" | custom-call | tf_op jit(solution)/shard_map/backward_window/pallas_call | solution.py:1081
  218.6 1.3 slice.79
  219.9 0.6 broadcast_divide_fusion
  220.5 0.6 fusion.3
  221.1 3.5 %convert_multiply_fusion = f32[768,768]{1,0:T(8,128)} fusion(bf16[768,768]{1,0:T(8,128)(2,1)} %get-tuple-element.63, f32[]{:T(128)} %bitcast.19), kind=kLoop, calls=%fused_computation.1 | loop fusion | flops 1179648 | bytes 3538948 | tf_op jit(solution)/shard_map/mul | solution.py:1174
  224.6 2.3 convert_multiply_fusion.1
  226.9 4.9 %multiply_reduce_fusion = (f32[768]{0:T(1024)}, f32[768]{0:T(1024)}, f32[768]{0:T(1024)}, f32[768]{0:T(1024)}, f32[768]{0:T(1024)}, /*index=5*/f32[768]{0:T(1024)}, f32[768]{0:T(1024)}) fusion(f32[16,768]{1,0:T(8,128)} %get-tuple-element.59, f32[]{:T(128)} %bitcast.20, f32[]{:T(128)} %bitcast.19, f32[]{:T(128)} %bitcast.18, s32[]{:T(128)S(6)} %select_n.19, ...), kind=kLoop, calls=%fused_computation.14 | loop fusion | flops 5376 | bytes 43032 | tf_op jit(solution)/shard_map/mul | solution.py:1177
  231.8 1.5 convert_multiply_fusion.3
  233.3 1.5 fusion.2
  234.8 0.7 mul.140
  235.5 1.3 fusion.1
  236.8 0.7 mul.137
  237.4 0.1 slice_bitcast_fusion.2
  237.5 2.1 multiply_bitcast_fusion
  239.6 0.0 copy-done.6
  239.6 1.8 convert_multiply_fusion.2
  241.4 0.0 copy-done.3
  241.4 3.9 %convert_divide_fusion = f32[2048,768]{1,0:T(8,128)} fusion(bf16[2048,768]{1,0:T(8,128)(2,1)S(1)} %copy-done.3, f32[]{:T(128)} %bitcast.7), kind=kLoop, calls=%fused_computation | loop fusion | flops 3145728 | bytes 9437188 | tf_op jit(solution)/shard_map/div | solution.py:1163
  245.3 0.0 copy-done.2
  245.4 1.7 copy.47
  (31 shorter events, 0.1 us)
Async XLA Ops:
  0.6 2.6 %copy-start = (s32[2048,4]{0,1:T(4,128)S(1)}, s32[2048,4]{0,1:T(4,128)}, u32[]{:S(2)}) copy-start(s32[2048,4]{0,1:T(4,128)} %param.22) | copy-start | bytes 98308
  3.3 5.6 %copy-start.14 = (f32[2,192]{1,0:T(2,128)S(1)}, f32[2,192]{1,0:T(2,128)}, u32[]{:S(2)}) copy-start(f32[2,192]{1,0:T(2,128)} %param.29) | copy-start | bytes 4612
  4.9 4.9 %copy-start.7 = (f32[768]{0:T(1024)S(1)}, f32[768]{0:T(1024)}, u32[]{:S(2)}) copy-start(f32[768]{0:T(1024)} %param.32) | copy-start | bytes 9220
  4.9 4.9 %copy-start.8 = (f32[768]{0:T(1024)S(1)}, f32[768]{0:T(1024)}, u32[]{:S(2)}) copy-start(f32[768]{0:T(1024)} %param.33) | copy-start | bytes 9220
  4.9 4.9 %copy-start.9 = (f32[768]{0:T(1024)S(1)}, f32[768]{0:T(1024)}, u32[]{:S(2)}) copy-start(f32[768]{0:T(1024)} %param.34) | copy-start | bytes 9220
  4.9 4.9 %copy-start.10 = (f32[768]{0:T(1024)S(1)}, f32[768]{0:T(1024)}, u32[]{:S(2)}) copy-start(f32[768]{0:T(1024)} %param.38) | copy-start | bytes 9220
  4.9 5.0 %copy-start.11 = (f32[768]{0:T(1024)S(1)}, f32[768]{0:T(1024)}, u32[]{:S(2)}) copy-start(f32[768]{0:T(1024)} %param.39) | copy-start | bytes 9220
  4.9 5.0 %copy-start.12 = (f32[768]{0:T(1024)S(1)}, f32[768]{0:T(1024)}, u32[]{:S(2)}) copy-start(f32[768]{0:T(1024)} %param.40) | copy-start | bytes 9220
  5.8 4.8 %copy-start.15 = (bf16[64,3]{0,1:T(4,128)(2,1)S(1)}, bf16[64,3]{0,1:T(4,128)(2,1)}, u32[]{:S(2)}) copy-start(bf16[64,3]{0,1:T(4,128)(2,1)} %param.30) | copy-start | bytes 1156
  5.8 4.8 %copy-start.13 = (f32[768]{0:T(1024)S(1)}, f32[768]{0:T(1024)}, u32[]{:S(2)}) copy-start(f32[768]{0:T(1024)} %param.36) | copy-start | bytes 9220
  83.8 136.1 %copy-start.16 = (f32[8]{0:T(128)S(1)}, f32[8]{0:T(128)}, u32[]{:S(2)}) copy-start(f32[8]{0:T(128)} %param.41) | copy-start | bytes 100
  218.6 6.1 %copy-start.4 = (bf16[768,768]{1,0:T(8,128)(2,1)S(1)}, bf16[768,768]{1,0:T(8,128)(2,1)}, u32[]{:S(2)}) copy-start(bf16[768,768]{1,0:T(8,128)(2,1)} %get-tuple-element.62) | copy-start | bytes 3538948
  224.6 7.2 %copy-start.5 = (bf16[896,768]{1,0:T(8,128)(2,1)S(1)}, bf16[896,768]{1,0:T(8,128)(2,1)}, u32[]{:S(2)}) copy-start(bf16[896,768]{1,0:T(8,128)(2,1)} %get-tuple-element.61) | copy-start | bytes 4128772
  233.3 6.3 %copy-start.6 = (bf16[512,768]{1,0:T(8,128)(2,1)S(1)}, bf16[512,768]{1,0:T(8,128)(2,1)}, u32[]{:S(2)}) copy-start(bf16[512,768]{1,0:T(8,128)(2,1)} %get-tuple-element.60) | copy-start | bytes 2359300
  237.5 3.9 %copy-start.3 = (bf16[2048,768]{1,0:T(8,128)(2,1)S(1)}, bf16[2048,768]{1,0:T(8,128)(2,1)}, u32[]{:S(2)}) copy-start(bf16[2048,768]{1,0:T(8,128)(2,1)} %get-tuple-element.58) | copy-start | bytes 9437188
  241.4 3.9 %copy-start.2 = (bf16[2048,768]{1,0:T(8,128)(2,1)S(1)}, bf16[2048,768]{1,0:T(8,128)(2,1)}, u32[]{:S(2)}) copy-start(bf16[2048,768]{1,0:T(8,128)(2,1)} %get-tuple-element.104) | copy-start | bytes 9437188
  245.3 1.7 copy-start.1

commit v5 on v4

--- a/solution.py
+++ b/solution.py
@@ -16,37 +16,69 @@
 HEADS_T = 3
 MESH = pl.DeviceIdType.MESH
 
-ORDERS = {
-    "A": (True, False, True),
-    "B": (True, False, False),
-    "C": (True, False, True),
+F_FEAT, F_NEAR, F_HEAD, F_FAR, F_BOTH, F_OUT, F_CONTEXT, F_NORM, F_UP, F_THIRD, F_DONE = range(11)
+AT_R, AT_Q, AT_K, AT_V, AT_O, U0, D0, U1, D1, U2, D2 = range(11)
+WAYS = {
+    AT_R: (1, 0),
+    AT_Q: (2, 1),
+    AT_K: (2, 1),
+    AT_V: (2, 0),
+    AT_O: (2, 1),
+    U0: (4, 0),
+    D0: (4, 0),
+    U1: (4, 0),
+    D1: (4, 0),
+    U2: (2, 1),
+    D2: (1, 0),
 }
+SEND_ORDER = (AT_Q, AT_K, AT_V, AT_O, AT_R, D1, D0, U0, U1, U2, D2)
+FORWARD = {
+    (F_NEAR, 0): ((AT_Q, 0),),
+    (F_HEAD, 2): ((AT_K, 0), (AT_V, 0), (AT_Q, 1),),
+    (F_HEAD, 4): ((AT_O, 0), (AT_K, 1), (AT_R, 0), (AT_V, 1),),
+    (F_HEAD, 5): ((D1, 0),),
+    (F_BOTH, 0): ((D0, 0),),
+    (F_HEAD, 6): ((D1, 1),),
+    (F_HEAD, 7): ((U0, 0),),
+    (F_HEAD, 8): ((U1, 0), (D0, 1), (D1, 2),),
+    (F_HEAD, 9): ((AT_O, 1),),
+    (F_HEAD, 10): ((U0, 1),),
+    (F_HEAD, 11): ((U1, 1),),
+    (F_CONTEXT, 0): ((U2, 0), (D0, 2),),
+    (F_NORM, 1): ((U0, 2),),
+    (F_NORM, 3): ((U1, 2),),
+    (F_UP, 2): ((D2, 0), (U2, 1),),
+}
+
+START, FFN, NORM, OUT, HEAD, SENT, MERGED, DLAYER, LAYOUT, TABLE, TAIL = range(11)
+A0, A1, A2, B0, B1, B2, CA, CB, CC, BLOCK, BLOCK_ON, INPUT_ON, LAY, LAY_ON, SMALL_STEP = range(15)
+X_FIRST = (False, True, True, True, False, True, True, False, True)
 SCHEDULE = {
-    "start": ("blk0", "blk1",),
-    "ffn0.1": ("blkpass0",),
-    "ffn1.0": ("blkpass1",),
-    "ffn3.1": ("A1.1", "A0.1",),
-    "h0": ("A2.1",),
-    "h2": ("A0.2",),
-    "h5": ("B1.1", "B0.1", "A0.3",),
-    "h6": ("B2.1", "A1.2",),
-    "h8": ("A0.4", "A2.2", "B1.2",),
-    "h10": ("A1.3", "B0.2", "B2.2",),
-    "h11": ("blk2", "blk3",),
-    "pq": ("A2.3",),
-    "pk": ("B1.3", "blkpass2",),
-    "dl0": ("A1.4", "blkpass3",),
-    "dl3": ("B0.3",),
-    "t0": ("Cb.1", "B2.3", "Ca.1", "A2.4",),
-    "t3": ("Cc.1", "B1.4",),
-    "t6": ("B0.4", "Ca.2",),
-    "t9": ("B2.4",),
-    "t11": ("Cc.2",),
-    "t14": ("Ca.3",),
-    "t15": ("Cc.3", "igpass",),
-    "tail": (
-        "A0.5", "A1.5", "A2.5", "B1.5", "B0.5", "sm0", "Ca.4", "Cb.2", "B2.5", "sm1", "Cc.4", "Ca.5", "Cb.3", "sm2",
-        "Cc.5", "lay", "Cb.4", "laypass", "sm3", "sm4", "Cb.5",
+    (START, 0): ((BLOCK, 2),),
+    (FFN, 2): ((BLOCK_ON, 2),),
+    (FFN, 8): ((A0, 1),),
+    (FFN, 9): ((A1, 1),),
+    (OUT, 0): ((A1, 2),),
+    (HEAD, 1): ((A2, 1),),
+    (HEAD, 2): ((B1, 1),),
+    (HEAD, 4): ((A1, 3), (B0, 1), (A2, 2),),
+    (HEAD, 8): ((A1, 4),),
+    (HEAD, 10): ((B0, 2), (A2, 3), (B2, 1),),
+    (SENT, 0): ((A0, 2), (B2, 2),),
+    (MERGED, 0): ((B1, 2),),
+    (DLAYER, 2): ((A0, 3),),
+    (TABLE, 2): ((CA, 1), (A2, 4), (B1, 3),),
+    (TABLE, 3): ((CB, 1),),
+    (TABLE, 4): ((B2, 3), (A0, 4),),
+    (TABLE, 5): ((BLOCK, 0), (BLOCK, 1), (BLOCK, 3),),
+    (TABLE, 6): ((CA, 2), (CC, 1), (B1, 4),),
+    (TABLE, 8): ((B0, 3),),
+    (TABLE, 11): ((B2, 4),),
+    (TAIL, 0): (
+        (A1, 5), (A0, 5), (A2, 5), (CA, 3), (CC, 2), (SMALL_STEP, 0), (INPUT_ON, 0), (B0, 4), (B1, 5), (CB, 2),
+        (B2, 5), (CA, 4), (CC, 3), (BLOCK_ON, 0), (B0, 5), (BLOCK_ON, 1), (CB, 3), (CA, 5), (CC, 4), (BLOCK_ON, 3),
+        (SMALL_STEP, 1), (CC, 5), (LAY, 0), (SMALL_STEP, 2), (CB, 4), (SMALL_STEP, 3), (LAY_ON, 0), (SMALL_STEP, 4),
+        (CB, 5),
     ),
 }
 
@@ -67,7 +99,10 @@
     barrier = pltpu.get_barrier_semaphore()
     for peer in peers:
         pl.semaphore_signal(barrier, inc=1, device_id=peer, device_id_type=MESH)
-    pl.semaphore_wait(barrier, len(peers))
+
+
+def wait_peers(peers):
+    pl.semaphore_wait(pltpu.get_barrier_semaphore(), len(peers))
 
 
 def remote(src, dst, send, recv, peer):
@@ -76,61 +111,96 @@
     )
 
 
+HERE, MATE, ACROSS, PASS, BESIDE, PASS_BESIDE, ALONG, PASS_ALONG, LAST_BESIDE, LAST_ALONG, PASS_LAST = range(11)
+
+
 class Gather:
-    def __init__(self, own, place, rows, split, sems, slot, peers):
-        self.own, self.place, self.rows, self.split = own, place, rows, split
+    def __init__(self, own, place, rows, kind, bit, sems, slot, peers):
+        self.own, self.place, self.rows, self.kind, self.bit = own, place, rows, kind, bit
         self.send, self.recv, self.here = sems
         self.slot = slot
-        self.mate, self.across, self.beside, self.side = peers
+        self.mate, self.across, self.near, self.sides = peers
+
+    def part(self, flip_zero, flip_one):
+        if self.kind == 1:
+            return pl.ds(0, self.rows)
+        if self.kind == 2:
+            side = self.sides[self.bit]
+            side = 1 - side if flip_zero else side
+            return pl.ds(pl.multiple_of(side * (self.rows // 2), 16), self.rows // 2)
+        zero = 1 - self.sides[0] if flip_zero else self.sides[0]
+        one = 1 - self.sides[1] if flip_one else self.sides[1]
+        return pl.ds(pl.multiple_of((zero + 2 * one) * (self.rows // 4), 16), self.rows // 4)
+
+    def halved(self, part, second):
+        h = part.size // 2
+        return pl.ds(pl.multiple_of(part.start + (h if second else 0), 16), h)
 
     def copy(self, name):
         s = self.slot
-        half = self.rows // 2 if self.split else self.rows
-        mine = pl.ds(pl.multiple_of(self.side * half, half), half) if self.split else pl.ds(0, half)
-        yours = pl.ds(pl.multiple_of((1 - self.side) * half, half), half)
         whole = pl.ds(0, self.rows)
-        if name == "here":
+        mine = self.part(False, False)
+        if name == HERE:
             return pltpu.make_async_copy(self.own(whole), self.place(0, whole), self.here.at[s])
+
+        def pass_on(rows, k):
+            return self.place(2, rows), self.place(3, rows), self.mate, k
+
+        def relay(rows, to, k):
+            return self.place(2, rows), self.place(2, rows), self.near[to], k
+
         src, dst, peer, k = {
-            "mate": lambda: (self.own(whole), self.place(1, whole), self.mate, 0),
-            "across": lambda: (self.own(mine), self.place(2, mine), self.across, 1),
-            "pass": lambda: (self.place(2, mine), self.place(3, mine), self.mate, 2),
-            "beside": lambda: (self.place(2, mine), self.place(2, mine), self.beside, 3),
-            "pass_two": lambda: (self.place(2, yours), self.place(3, yours), self.mate, 4),
+            MATE: lambda: (self.own(whole), self.place(1, whole), self.mate, 0),
+            ACROSS: lambda: (self.own(mine), self.place(2, mine), self.across, 1),
+            PASS: lambda: pass_on(mine, 2),
+            BESIDE: lambda: relay(mine, self.bit, 3),
+            PASS_BESIDE: lambda: pass_on(self.part(True, False), 4),
+            ALONG: lambda: relay(mine, 1, 5),
+            PASS_ALONG: lambda: pass_on(self.part(False, True), 6),
+            LAST_BESIDE: lambda: relay(self.halved(self.part(False, True), False), 0, 7),
+            LAST_ALONG: lambda: relay(self.halved(self.part(True, False), True), 1, 8),
+            PASS_LAST: lambda: pass_on(self.part(True, True), 9),
         }[name]()
         return remote(src, dst, self.send.at[s, k], self.recv.at[s, k], peer)
 
+    def names(self, stage):
+        return {
+            1: (((PASS,), (ACROSS,)),),
+            2: (((BESIDE, PASS), (ACROSS,)), ((PASS_BESIDE,), (BESIDE,))),
+            4: (
+                ((BESIDE, ALONG, PASS), (ACROSS,)),
+                ((LAST_BESIDE, LAST_ALONG, PASS_BESIDE, PASS_ALONG), (BESIDE, ALONG)),
+                ((PASS_LAST,), (LAST_BESIDE, LAST_ALONG)),
+            ),
+        }[self.kind][stage]
+
+    def stages(self):
+        return {1: 1, 2: 2, 4: 3}[self.kind]
+
     def start(self):
-        self.copy("across").start()
-        self.copy("mate").start()
-        self.copy("here").start()
-
-    def forward(self):
-        self.copy("across").wait_recv()
-        if self.split:
-            self.copy("beside").start()
-        self.copy("pass").start()
-
-    def forward_two(self):
-        if self.split:
-            self.copy("beside").wait_recv()
-            self.copy("pass_two").start()
+        self.copy(ACROSS).start()
+        self.copy(MATE).start()
+        self.copy(HERE).start()
+
+    def forward(self, stage):
+        starts, waits = self.names(stage)
+        for name in waits:
+            self.copy(name).wait_recv()
+        for name in starts:
+            self.copy(name).start()
 
     def arrive_near(self):
-        self.copy("here").wait()
-        self.copy("mate").wait_recv()
+        self.copy(HERE).wait()
+        self.copy(MATE).wait_recv()
 
     def arrive_far(self):
-        self.copy("pass").wait_recv()
-        if self.split:
-            self.copy("pass_two").wait_recv()
-
-    def arrive(self):
-        self.arrive_near()
-        self.arrive_far()
+        for stage in range(self.stages()):
+            for name in self.names(stage)[0]:
+                if name in (PASS, PASS_BESIDE, PASS_ALONG, PASS_LAST):
+                    self.copy(name).wait_recv()
 
     def finish(self):
-        for name in ("mate", "across", "pass") + (("beside", "pass_two") if self.split else ()):
+        for name in (MATE, ACROSS) + sum((self.names(stage)[0] for stage in range(self.stages())), ()):
             self.copy(name).wait_send()
 
 
@@ -150,95 +220,147 @@
     return 0.5 * v * (1.0 + jnp.tanh(math.sqrt(2.0 / math.pi) * (v + 0.044715 * (v * v * v))))
 
 
+def row_of(ref):
+    return ref[...].reshape(1, ref.shape[0])
+
+
+def column_of(row):
+    return jnp.broadcast_to(row, (8, 128)).T[:, 0:1]
+
+
 def forward_kernel(
-    tok_ref, box_ref, rx_ref, ry_ref, mask_ref, cot_ref, freq_ref, lay_ref, vec_ref,
-    cols_own, rows_own, qkv_own, wo_own, w1_own, w2_own,
+    box_ref, mask_ref, lay_ref, qvb_ref, b1_ref, table_ref, ob_ref, g1_ref, s1_ref, c2_ref, g2_ref, s2_ref,
+    tok_in, cot_in, rx_in, ry_in, qkv_own, wo_own, w1_own, w2_own,
     probs_out, qkvt_out, ctxt_out, low_out, feat_out, unit_out, inv_out, nlow_out, pre_out, hid_out,
     block_out, dres_out, sums_out, wqkv_out, wo_out, w1_out, w2_out,
-    wqkv, wo, w1, w2, cols, rows, tabs, layer_in, qkvt, pbuf, ctxt, ctx, normed, pre, hid, acc,
-    send, recv, here, out_sem, p_sem,
+    tokb, cotb, rxb, ryb, vec, rows_own, wqkv, wo, w1, w2, rows, cols, tabs, layer_in, qkvt, pbuf, ctxt, ctx, normed, pre,
+    hid, acc, send, recv, here, out_sem, p_sem, in_sem,
 ):
     t, d = lax.axis_index("tensor"), lax.axis_index("dp")
     mate, across = {"tensor": xor_index(t, 1)}, {"tensor": xor_index(t, 2)}
-    beside = {"dp": xor_index(d, 1)}
-    peers = (mate, across, beside, d % 2)
-    win, model = tok_ref.shape
+    near = [{"dp": xor_index(d, 1)}, {"dp": xor_index(d, 2)}]
+    peers = (mate, across, near, (d % 2, (d // 2) % 2))
+    win, model = tokb.shape
     heads = 4 * HEADS_T
     cols_t = HEADS_T * HD
+    hid_t = w1_own.shape[1]
     sems = (send, recv, here)
     f32, bf16 = jnp.float32, jnp.bfloat16
-
-    def chunk(slot, own, place, count, split=True):
-        return Gather(own, place, count, split, sems, slot, peers)
-
-    g_cols = chunk(0, lambda s: cols_own.at[s], lambda r, s: cols.at[r, s], cols_t, False)
-    g_rows = chunk(1, lambda s: rows_own.at[s], lambda r, s: rows.at[r, s], 8, False)
+    block = 128
+
+    everyone = [mate, across] + near
+    signal_peers(everyone)
+    own_rows = pl.ds(pl.multiple_of(t * win, win), win)
+    loads = [
+        pltpu.make_async_copy(src, dst, in_sem.at[k])
+        for k, (src, dst) in enumerate(
+            [(tok_in.at[own_rows], tokb), (rx_in.at[t], rxb), (ry_in.at[t], ryb), (cot_in.at[own_rows], cotb)]
+        )
+    ]
+    for c in loads:
+        c.start()
+    for k, ref in enumerate((ob_ref, g1_ref, s1_ref, c2_ref, g2_ref, s2_ref)):
+        vec[k : k + 1, :] = row_of(ref)
+    rows_own[...] = jnp.zeros_like(rows_own)
+    rows_own[0:1, :] = row_of(b1_ref)
+    rows_own[1 : 1 + HEADS_T, 0 : 2 * BUCKETS] = table_ref[...].astype(f32)
+    rows_own[4:6, 0:cols_t] = qvb_ref[...]
 
     def piece_rows(r, s, count):
         return pl.ds(pl.multiple_of(r * count + s.start, 16), s.size)
 
-    g_qkv = [
+    gathers = {}
+
+    def chunk(name, own, place, count):
+        gathers[name] = Gather(own, place, count, *WAYS[name], sems, name, peers)
+
+    chunk(AT_R, lambda s: rows_own.at[s], lambda r, s: rows.at[r, s], 8)
+    for n, name in enumerate((AT_Q, AT_K, AT_V)):
         chunk(
-            2 + n,
+            name,
             lambda s, n=n: qkv_own.at[n, s],
             lambda r, s, n=n: wqkv.at[n, piece_rows(r, s, cols_t)],
             cols_t,
         )
-        for n in range(3)
-    ]
-    g_wo = chunk(5, lambda s: wo_own.at[s], lambda r, s: wo.at[piece_rows(r, s, cols_t)], cols_t)
-
-    def part(slot, own, whole, half):
-        count = own.shape[0] // 2
-
-        def moved(s):
-            return pl.ds(pl.multiple_of(s.start + half * count, 16), s.size)
-
-        return chunk(slot, lambda s: own.at[moved(s)], lambda r, s: whole.at[r, moved(s)], count)
-
-    g_w1 = [part(6 + h, w1_own, w1, h) for h in range(2)]
-    g_w2 = [part(8 + h, w2_own, w2, h) for h in range(2)]
-    everything = [g_cols, g_rows] + g_qkv + [g_wo] + g_w1 + g_w2
-
-    signal_peers((mate, across, beside))
-    for g in [g_cols, g_rows] + g_qkv:
-        g.start()
+    chunk(AT_O, lambda s: wo_own.at[s], lambda r, s: wo.at[piece_rows(r, s, cols_t)], cols_t)
+    third = hid_t // 3
+    for k in range(3):
+        units = pl.ds(k * third, third)
+        chunk(
+            U0 + 2 * k, lambda s, units=units: w1_own.at[s, units], lambda r, s, units=units: w1.at[r, s, units], model
+        )
+
+        def moved(s, k=k):
+            return pl.ds(pl.multiple_of(s.start + k * third, 16), s.size)
+
+        chunk(
+            D0 + 2 * k, lambda s, moved=moved: w2_own.at[moved(s)], lambda r, s, moved=moved: w2.at[r, moved(s)], third
+        )
+
+    def at_slot(phase, index=0):
+        for name, stage in FORWARD.get((phase, index), ()):
+            gathers[name].forward(stage)
+
+    def at_loop(phase, index, count, first=0, step=1):
+        for k in range(count):
+            if (phase, first + step * k) in FORWARD:
+                @pl.when(index == k)
+                def _(k=k):
+                    at_slot(phase, first + step * k)
+
+    def near_pieces(names):
+        for name in names:
+            gathers[name].arrive_near()
+
+    def far_pieces(names):
+        for name in names:
+            gathers[name].arrive_far()
+
+    wait_peers(everyone)
+    for name in SEND_ORDER:
+        gathers[name].start()
 
     lane = lax.broadcasted_iota(jnp.int32, (1, 128), 1)
     quarter = jnp.where(lane >= LFREQ, 1, 0)
-    block = 128
+    frequency = jnp.exp((lane % LFREQ).astype(f32) * (-math.log(1000.0) / LFREQ))
+    loads[0].wait()
 
     @pl.loop(0, win // block)
     def _(i):
         sl = pl.ds(pl.multiple_of(i * block, block), block)
-        box = box_ref[sl, :].astype(f32)
+        box = box_ref[:, pl.ds(pl.multiple_of(t * win + i * block, block), block)].astype(f32)
         for m in range(4):
             feat_out[sl, 2 * LFREQ * m : 2 * LFREQ * (m + 1)] = waves(
-                box[:, m : m + 1], freq_ref[0:1, :], quarter
+                column_of(box[m : m + 1, :]), frequency, quarter
             ).astype(bf16)
-        value = tok_ref[sl, :].astype(f32) + nn(feat_out[sl, :], lay_ref[...])
+        value = tokb[sl, :].astype(f32) + nn(feat_out[sl, :], lay_ref[...])
         layer_in[sl, :] = value
         low_out[sl, :] = value.astype(bf16)
-
-    for g in [g_cols, g_rows] + g_qkv:
-        g.forward()
-    g_wo.start()
-    g_w1[0].start()
-    for g in g_qkv:
-        g.forward_two()
-    g_cols.arrive()
-    g_rows.arrive()
-    for r in range(4):
-        tabs[HEADS_T * r : HEADS_T * (r + 1), :] = rows[r, 1 : 1 + HEADS_T, 0:128]
-
-    for n in range(3):
-        g_qkv[n].arrive()
-
-        @pl.loop(0, 4)
-        def _(r, n=n):
-            sl = pl.ds(pl.multiple_of(r * cols_t, 16), cols_t)
-            value = nt(wqkv[n, sl, :], low_out[...])
-            qkvt[n, sl, :] = (value + cols[r, :, n : n + 1]).astype(bf16)
+        at_loop(F_FEAT, i, 4)
+
+    def bias_columns(pieces):
+        for r in pieces:
+            for n, row in ((0, 4), (2, 5)):
+                for c in range(0, cols_t, 64):
+                    part = jnp.broadcast_to(rows[r, row : row + 1, 0:256][:, 0:256], (8, 256)).T
+                    cols[n, pl.ds(r * cols_t + c, 64), :] = part[c : c + 64, 0:1]
+            tabs[HEADS_T * r : HEADS_T * (r + 1), :] = rows[r, 1 : 1 + HEADS_T, 0:128]
+
+    def project(pieces):
+        for n in range(3):
+            for r in pieces:
+                sl = pl.ds(r * cols_t, cols_t)
+                value = nt(wqkv[n, sl, :], low_out[...])
+                if n != 1:
+                    value = value + cols[n, sl, :]
+                qkvt[n, sl, :] = value.astype(bf16)
+
+    near_pieces((AT_R, AT_Q, AT_K, AT_V))
+    bias_columns((0, 1))
+    project((0, 1))
+    at_slot(F_NEAR)
+    for c in loads[1:3]:
+        c.wait()
 
     def table_row(h):
         return (tabs[pl.ds(h, 1), :] * 2048.0 + 32768.5).astype(jnp.int32) - 32768
@@ -246,8 +368,7 @@
     def p_copy(i, slot):
         return pltpu.make_async_copy(pbuf.at[slot], probs_out.at[pl.ds(2 * i, 2)], p_sem.at[slot])
 
-    @pl.loop(0, heads // 2)
-    def _(i):
+    def two_heads(i):
         slot = i % 2
         sl = pl.ds(pl.multiple_of(i * 2 * HD, 2 * HD), 2 * HD)
         q = (qkvt[0, sl, :].astype(f32).T * HD ** (-0.5)).astype(bf16)
@@ -255,8 +376,8 @@
         bias = ([], [])
         for c in range(win // 128):
             at = slice(128 * c, 128 * c + 128)
-            word = jnp.take_along_axis(tab, rx_ref[:, at], axis=1) + jnp.take_along_axis(
-                tab, ry_ref[:, at] + BUCKETS, axis=1
+            word = jnp.take_along_axis(tab, rxb[:, at], axis=1) + jnp.take_along_axis(
+                tab, ryb[:, at] + BUCKETS, axis=1
             )
             second = word << 16
             bias[0].append((word - (second >> 16)).astype(f32) * 2.0**-27)
@@ -274,32 +395,16 @@
             p = e * (1.0 / jnp.sum(e, axis=1, keepdims=True))
             pbuf[slot, u] = p
             ctxt[rows_u, :] = nt(qkvt[2, rows_u, :], p.astype(bf16)).astype(bf16)
+            at_loop(F_HEAD, i, heads // 2, u, 2)
         p_copy(i, slot).start()
 
-        @pl.when(i == 0)
-        def _():
-            g_wo.forward()
-            g_w1[1].start()
-
-        @pl.when(i == 1)
-        def _():
-            g_w1[0].forward()
-            g_wo.forward_two()
-            g_w2[0].start()
-
-        @pl.when(i == 2)
-        def _():
-            g_w2[1].start()
-
-        @pl.when(i == 3)
-        def _():
-            g_w1[1].forward()
-            g_w1[0].forward_two()
-
-        @pl.when(i == 5)
-        def _():
-            g_w2[0].forward()
-            g_w1[1].forward_two()
+    pl.loop(0, heads // 4)(two_heads)
+    at_slot(F_FAR)
+    far_pieces((AT_R, AT_Q, AT_K, AT_V))
+    bias_columns((2, 3))
+    project((2, 3))
+    at_slot(F_BOTH)
+    pl.loop(heads // 4, heads // 2)(two_heads)
 
     last = heads // 2
     outs = [
@@ -314,38 +419,32 @@
 
     for src, dst in outs:
         leave(src, dst)
-    g_wo.arrive()
+    at_slot(F_OUT)
+    near_pieces((AT_O,))
+    far_pieces((AT_O,))
     leave(wo, wo_out)
-
     ctx[...] = ctxt[...].astype(f32).T.astype(bf16)
+    at_slot(F_CONTEXT)
 
     @pl.loop(0, win // block)
     def _(i):
         sl = pl.ds(pl.multiple_of(i * block, block), block)
-        value = layer_in[sl, :] + nn(ctx[sl, :], wo[...]) + vec_ref[0:1, :]
+        value = layer_in[sl, :] + nn(ctx[sl, :], wo[...]) + vec[0:1, :]
         mean = jnp.mean(value, axis=1, keepdims=True)
         centered = value - mean
         inverse = lax.rsqrt(jnp.mean(centered * centered, axis=1, keepdims=True) + EPSILON)
         unit = centered * inverse
         unit_out[sl, :] = unit
         inv_out[sl, :] = inverse
-        value = unit * vec_ref[1:2, :] + vec_ref[2:3, :]
+        value = unit * vec[1:2, :] + vec[2:3, :]
         normed[sl, :] = value
         nlow_out[sl, :] = value.astype(bf16)
-
-    g_w2[0].forward_two()
-    g_w2[1].forward()
-    for r in range(4):
-        if r == 0:
-            for g in g_w1 + g_w2:
-                g.arrive_near()
-        if r == 2:
-            g_w2[1].forward_two()
-            for g in g_w1 + g_w2:
-                g.arrive_far()
-            leave(w1, w1_out)
-            leave(w2, w2_out)
-
+        at_loop(F_NORM, i, 4)
+
+    near_pieces(range(U0, D2 + 1))
+    for src, dst in ((w1, w1_out), (w2, w2_out)):
+        leave(src.at[pl.ds(0, 2)], dst.at[pl.ds(0, 2)])
+    for r in range(2):
         @pl.loop(0, win // 256)
         def _(i, r=r):
             sl = pl.ds(pl.multiple_of(i * 256, 256), 256)
@@ -355,23 +454,47 @@
             hid[r, sl, :] = low_hid
             more = nn(low_hid, w2[r])
             acc[sl, :] = more if r == 0 else acc[sl, :] + more
+            at_loop(F_UP, i, 2, 2 * r)
 
         leave(pre.at[r], pre_out.at[r])
         leave(hid.at[r], hid_out.at[r])
+
+    for k in range(3):
+        at_slot(F_THIRD, k)
+        far_pieces((U0 + 2 * k, D0 + 2 * k))
+        units = pl.ds(k * third, third)
+
+        @pl.loop(2, 4)
+        def _(r, units=units):
+            value = nn(nlow_out[...], w1[r, :, units]) + rows[r, 0:1, units]
+            pre[r, :, units] = value
+            low_hid = gelu(value).astype(bf16)
+            hid[r, :, units] = low_hid
+            acc[...] += nn(low_hid, w2[r, units, :])
+
+        at_slot(F_DONE, k)
+
+        for src, dst in ((pre, pre_out), (hid, hid_out)):
+            leave(src.at[pl.ds(2, 2), :, units], dst.at[pl.ds(2, 2), :, units])
+        leave(w1.at[pl.ds(2, 2), :, units], w1_out.at[pl.ds(2, 2), :, units])
+        leave(w2.at[pl.ds(2, 2), units], w2_out.at[pl.ds(2, 2), units])
+
+    loads[3].wait()
 
     sums_out[...] = jnp.zeros_like(sums_out)
 
     @pl.loop(0, win // block)
     def _(i):
         sl = pl.ds(pl.multiple_of(i * block, block), block)
-        value = normed[sl, :] + acc[sl, :] + vec_ref[3:4, :]
+        value = normed[sl, :] + acc[sl, :] + vec[3:4, :]
         mean = jnp.mean(value, axis=1, keepdims=True)
         centered = value - mean
         inverse = lax.rsqrt(jnp.mean(centered * centered, axis=1, keepdims=True) + EPSILON)
         unit = centered * inverse
-        block_out[sl, :] = (unit * vec_ref[4:5, :] + vec_ref[5:6, :]).astype(bf16)
-        selected = mask_ref[sl, :].astype(f32) * cot_ref[sl, :].astype(f32)
-        scaled = selected * vec_ref[4:5, :]
+        block_out[sl, :] = (unit * vec[4:5, :] + vec[5:6, :]).astype(bf16)
+        mask = column_of(mask_ref[pl.ds((win // block) * t + i, 1), :].astype(f32))
+        selected = mask * cotb[sl, :].astype(f32)
+        scaled = selected * vec[4:5, :]
         mean_one = jnp.mean(scaled, axis=1, keepdims=True)
         mean_two = jnp.mean(scaled * unit, axis=1, keepdims=True)
         dres = (scaled - mean_one - unit * mean_two) * inverse
@@ -379,18 +502,19 @@
         sums_out[0:1, :] += jnp.sum(selected * unit, axis=0, keepdims=True)
         sums_out[1:2, :] += jnp.sum(selected, axis=0, keepdims=True)
         sums_out[2:3, :] += jnp.sum(dres, axis=0, keepdims=True)
-        sums_out[3:4, :] += jnp.sum(mask_ref[sl, :].astype(f32), axis=0, keepdims=True)
+        sums_out[3:4, :] += jnp.sum(mask, axis=0, keepdims=True)
 
     for i in (last - 2, last - 1):
         p_copy(i, i % 2).wait()
     for c in done:
         c.wait()
-    for g in everything:
+    for g in gathers.values():
         g.finish()
 
 
-def forward_window(n_dp, tok, box, rx, ry, mask, cot, freq, lay, vec, cols_own, rows_own, qkv_own, wo_own, w1_own, w2_own):
-    win, model = tok.shape
+def forward_window(small, large):
+    wo_own, w1_own = large[5:7]
+    win, model = large[2].shape[1], large[0].shape[1]
     cols_t, hid_t = wo_own.shape[0], w1_own.shape[1]
     heads = 4 * HEADS_T
     f32, bf16 = jnp.float32, jnp.bfloat16
@@ -418,16 +542,22 @@
     ]
     return pl.pallas_call(
         forward_kernel,
-        in_specs=[here] * 9 + [away] * 6,
+        in_specs=[here] * len(small) + [away] * len(large),
         out_specs=[spec for _, spec in outs],
         out_shape=[s for s, _ in outs],
         scratch_shapes=[
+            pltpu.VMEM((win, model), bf16),
+            pltpu.VMEM((win, model), bf16),
+            pltpu.VMEM((win, win), jnp.int32),
+            pltpu.VMEM((win, win), jnp.int32),
+            pltpu.VMEM((8, model), f32),
+            pltpu.VMEM((8, model), f32),
             pltpu.VMEM((3, model, model), bf16),
             pltpu.VMEM((model, model), bf16),
             pltpu.VMEM((4, model, hid_t), bf16),
             pltpu.VMEM((4, hid_t, model), bf16),
-            pltpu.VMEM((4, cols_t, 128), f32),
             pltpu.VMEM((4, 8, model), f32),
+            pltpu.VMEM((3, model, 1), f32),
             pltpu.VMEM((heads, 128), f32),
             pltpu.VMEM((win, model), f32),
             pltpu.VMEM((3, model, win), bf16),
@@ -438,17 +568,18 @@
             pltpu.VMEM((4, win, hid_t), f32),
             pltpu.VMEM((4, win, hid_t), bf16),
             pltpu.VMEM((win, model), f32),
-            pltpu.SemaphoreType.DMA((10, 5)),
-            pltpu.SemaphoreType.DMA((10, 5)),
-            pltpu.SemaphoreType.DMA((10,)),
-            pltpu.SemaphoreType.DMA((16,)),
+            pltpu.SemaphoreType.DMA((11, 10)),
+            pltpu.SemaphoreType.DMA((11, 10)),
+            pltpu.SemaphoreType.DMA((11,)),
+            pltpu.SemaphoreType.DMA((24,)),
             pltpu.SemaphoreType.DMA((2,)),
+            pltpu.SemaphoreType.DMA((4,)),
         ],
         compiler_params=pltpu.CompilerParams(
             vmem_limit_bytes=60 * 2**20, collective_id=0, has_side_effects=True
         ),
         name="forward_window",
-    )(tok, box, rx, ry, mask, cot, freq, lay, vec, cols_own, rows_own, qkv_own, wo_own, w1_own, w2_own)
+    )(*small, *large)
 
 
 def bits_of(size):
@@ -611,7 +742,7 @@
 
 
 def backward_kernel(
-    n_dp, inv_ref, vec_ref, sums_ref, dres_in, hid_in, pre_in, unit_in, nlow_in, low_in, feat_in, qkvt_in, ctxt_in,
+    n_dp, inv_ref, gain_ref, sums_ref, dres_in, hid_in, pre_in, unit_in, nlow_in, low_in, feat_in, qkvt_in, ctxt_in,
     probs_in, rx_in, ry_in, w1_in, w2_in, wo_in, wqkv_in, block_in,
     block_all, in_all, red1, red2, red3, lay_all, small_out,
     arena, hidb, preb, dres, unit, nlow, nlow_t, dn, low_rows, qkvb, ctxtb, dctx, lowb, featb, wob, rxb, ryb, hot, acc,
@@ -633,6 +764,9 @@
     hid_t = model
     block = 128
 
+    everyone = [mate, across, beside] + along[1:] + further
+    signal_peers(everyone)
+
     def load(k, src, dst):
         return pltpu.make_async_copy(src, dst, load_sem.at[k])
 
@@ -653,7 +787,7 @@
         for k, (src, dst) in enumerate(
             [
                 (nlow_in, nlow), (unit_in, unit), (ctxt_in, ctxtb), (wo_in, wob), (qkvt_in, qkvb), (low_in, lowb),
-                (feat_in, featb), (rx_in, rxb), (ry_in, ryb),
+                (feat_in, featb), (rx_in.at[t], rxb), (ry_in.at[t], ryb),
             ]
         )
     ]
@@ -692,14 +826,14 @@
         return [lambda p, k=k: ref.at[p, pl.ds(k * third, third)] for k in range(3)]
 
     s2 = chunks(
-        0, sizes, ORDERS["A"], thirds(part2), core2, first2, second2, quarters2, final2, extra2, red2
+        0, sizes, X_FIRST[:3], thirds(part2), core2, first2, second2, quarters2, final2, extra2, red2
     )
     s1 = chunks(
-        3, sizes, ORDERS["B"], thirds(part1), core1, first1, second1, quarters1, final1, extra1, red1
+        3, sizes, X_FIRST[3:6], thirds(part1), core1, first1, second1, quarters1, final1, extra1, red1
     )
     lay_t = lay_all.shape[0] // 4
     s3 = chunks(
-        6, [2 * cols_t, 2 * cols_t, lay_t], ORDERS["C"],
+        6, [2 * cols_t, 2 * cols_t, lay_t], X_FIRST[6:],
         [
             lambda p: part2.at[p, pl.ds(0, 2 * cols_t)],
             lambda p: part2.at[p, pl.ds(2 * cols_t, 2 * cols_t)],
@@ -755,40 +889,35 @@
         if k + 1 < len(bits):
             small_move(k + 1).start()
 
-    named = {f"A{k}": g for k, g in enumerate(s2)}
-    named.update({f"B{k}": g for k, g in enumerate(s1)})
-    named.update({f"C{k}": g for k, g in zip("abc", s3)})
-
-    def run(event):
-        if event[:2] in named:
-            named[event[:2]].next(int(event[3:]))
-        elif event[:7] == "blkpass":
-            share_pass(sh_block[int(event[7:])])
-        elif event[:3] == "blk":
-            share_start(sh_block[int(event[3:])])
-        elif event == "igpass":
+    named = dict(zip(range(A0, CC + 1), s2 + s1 + s3))
+
+    def run(what, stage):
+        if what in named:
+            named[what].next(stage)
+        elif what == BLOCK:
+            share_start(sh_block[stage])
+        elif what == BLOCK_ON:
+            share_pass(sh_block[stage])
+        elif what == INPUT_ON:
             share_pass(sh_in)
-        elif event == "lay":
+        elif what == LAY:
             share_start(sh_lay)
-        elif event == "laypass":
+        elif what == LAY_ON:
             share_pass(sh_lay)
-        elif event[:2] == "sm":
-            small_step(int(event[2:]))
-
-    def at_slot(name, index=None):
-        if index is None:
-            for event in SCHEDULE.get(name, ()):
-                run(event)
-            return
-        for key, todo in SCHEDULE.items():
-            if key.startswith(name) and key[len(name) :].isdigit():
-                @pl.when(index == int(key[len(name) :]))
-                def _(todo=todo):
-                    for event in todo:
-                        run(event)
-
-    signal_peers([mate, across, beside] + along[1:] + further)
-    at_slot("start")
+        elif what == SMALL_STEP:
+            small_step(stage)
+
+    def at_slot(phase, index=0):
+        for what, stage in SCHEDULE.get((phase, index), ()):
+            run(what, stage)
+
+    def at_loop(phase, index, count, first=0):
+        for k in range(count):
+            if (phase, first + k) in SCHEDULE:
+                @pl.when(index == k)
+                def _(k=k):
+                    at_slot(phase, first + k)
+
 
     small[0] = jnp.zeros_like(small[0])
     small[0, 3:4, :] = sums_ref[2:3, :]
@@ -833,7 +962,14 @@
 
     for r in order[:2]:
         ld_hid[r].wait()
-        for_mate(s2, grad_w2, r, part2)
+        if r == order[0]:
+            for_mate((), grad_w2, r, part2)
+            wait_peers(everyone)
+            at_slot(START)
+            for g in s2:
+                g.go(0, r // 2)
+        else:
+            for_mate(s2, grad_w2, r, part2)
 
     ld_rest[0].wait()
     nlow_t[...] = nlow[...].astype(f32).T.astype(bf16)
@@ -854,7 +990,7 @@
             small[0, row, :] += jnp.sum(dpre.astype(f32), axis=0, keepdims=True)
             more = nt(dpre, arena[w_rows(4 + r), :])
             dn[sl, :] = more if j == 0 else dn[sl, :] + more
-            at_slot(f"ffn{j}.", i)
+            at_loop(FFN, i, 2, 3 * j)
 
         if j + 2 < 4:
             ld_pre[order[j + 2]].start()
@@ -866,7 +1002,7 @@
             for q in order[2:]:
                 ld_hid[q].wait()
                 for_own(s2, grad_w2, q)
-        at_slot(f"ffn{j}.g")
+        at_slot(FFN, 3 * j + 2)
 
     for c in ld_wqkv:
         c.start()
@@ -886,7 +1022,7 @@
         sl = pl.ds(pl.multiple_of(i * block, block), block)
         up = dres[sl, :] + dn[sl, :]
         units = unit[sl, :]
-        scaled = up * vec_ref[1:2, :]
+        scaled = up * row_of(gain_ref)
         mean_one = jnp.mean(scaled, axis=1, keepdims=True)
         mean_two = jnp.mean(scaled * units, axis=1, keepdims=True)
         value = (scaled - mean_one - units * mean_two) * inv_ref[sl, :]
@@ -896,7 +1032,7 @@
         small[0, 1:2, :] += jnp.sum(up * units, axis=0, keepdims=True)
         small[0, 2:3, :] += jnp.sum(up, axis=0, keepdims=True)
 
-    at_slot("ln")
+    at_slot(NORM)
     for c in ld_rest[2:]:
         c.wait()
 
@@ -905,7 +1041,7 @@
         sl = pl.ds(pl.multiple_of(r * cols_t, cols_t), cols_t)
         dctx[sl, :] = nt(wob[sl, :], low_rows[...]).astype(bf16)
 
-    at_slot("ow")
+    at_slot(OUT)
 
     @pl.loop(0, heads)
     def _(h):
@@ -929,7 +1065,7 @@
         def _():
             p_load(h + 2, slot).start()
 
-        at_slot("h", h)
+        at_loop(HEAD, h, heads)
 
     for c in ld_wqkv:
         c.wait()
@@ -952,14 +1088,14 @@
             part2[r // 2, at : at + cols_t, :] = upper(r).astype(bf16)
             part2[r // 2, at + cols_t : at + 2 * cols_t, :] = lower(r).astype(bf16)
             g.go(0, r // 2)
-    at_slot("pq")
+    at_slot(SENT)
     for g, upper, lower in halves:
         for r in (2, 0):
             g.from_mate(r // 2)
             g.merge(r // 2, pl.ds(0, cols_t), upper(r))
             g.merge(r // 2, pl.ds(cols_t, cols_t), lower(r))
             g.go(1, r // 2)
-    at_slot("pk")
+    at_slot(MERGED)
 
     @pl.loop(0, win // block)
     def _(i):
@@ -968,7 +1104,7 @@
         for n in range(3):
             value = value + tn(qkvb[n, :, sl], hidb[pl.ds(n * model, model), :])
         dn[sl, :] = value
-        at_slot("dl", i)
+        at_loop(DLAYER, i, 4)
 
     low_rows[...] = dn[...].astype(bf16)
 
@@ -982,7 +1118,7 @@
     for r in (3, 1):
         part3[r // 2] = grad_lay(r).astype(bf16)
         s3[2].go(0, r // 2)
-    at_slot("la")
+    at_slot(LAYOUT)
     for r in (2, 0):
         s3[2].from_mate(r // 2)
         s3[2].merge(r // 2, pl.ds(0, lay_t), grad_lay(r))
@@ -1015,7 +1151,7 @@
             more = nt(left, hot[u])
             total = more if total is None else total + more
         acc[...] += total
-        at_slot("t", i)
+        at_loop(TABLE, i, 16)
 
     row = lax.broadcasted_iota(jnp.int32, (ROWS, 2 * hots), 0)
     col = lax.broadcasted_iota(jnp.int32, (ROWS, 2 * hots), 1) % ROWS
@@ -1042,7 +1178,7 @@
         small[0, own_row(12, r), :] = short[r : r + 1, :]
 
     small_move(0).start()
-    at_slot("tail")
+    at_slot(TAIL)
     for k in range(5, len(bits)):
         small_step(k)
     small_out[...] = small[len(bits)]
@@ -1055,7 +1191,7 @@
             g.sent(stage)
 
 
-def backward_window(n_dp, lay_rows, inv, vec, sums, dres, hid, pre, unit, nlow, low, feat, qkvt, ctxt, probs, rx, ry, w1, w2, wo, wqkv, block_own):
+def backward_window(n_dp, lay_rows, inv, gain, sums, dres, hid, pre, unit, nlow, low, feat, qkvt, ctxt, probs, rx, ry, w1, w2, wo, wqkv, block_own):
     win, model = dres.shape
     heads = 4 * HEADS_T
     cols_t = HEADS_T * HD
@@ -1105,7 +1241,110 @@
             vmem_limit_bytes=63 * 2**20, collective_id=1, has_side_effects=True
         ),
         name="backward_window",
-    )(inv, vec, sums, dres, hid, pre, unit, nlow, low, feat, qkvt, ctxt, probs, rx, ry, w1, w2, wo, wqkv, block_own)
+    )(inv, gain, sums, dres, hid, pre, unit, nlow, low, feat, qkvt, ctxt, probs, rx, ry, w1, w2, wo, wqkv, block_own)
+
+
+def finish_kernel(
+    rates, small_ref, block_in, in_in, red1, red2, red3, lay_in,
+    block_out, in_out, lay_out, qkv_out, qvb_out, table_out, wo_out, ob_out, g1_out, s1_out, w1_out, b1_out, w2_out, c2_out,
+    g2_out, s2_out, in_low, low1, low2, low3, lay_low, in_wide, wide1, wide2, wide3, lay_wide, block_low, load_sem, store_sem,
+):
+    t = lax.axis_index("tensor")
+    cols_t = HEADS_T * HD
+    inverse = 1.0 / small_ref[6:7, 0:1]
+    order = [
+        (in_in, in_low, in_wide, in_out, None),
+        (red2, low2, wide2, w2_out, 4),
+        (red1, low1, wide1, w1_out, 3),
+        (red3, low3, wide3, None, None),
+        (lay_in, lay_low, lay_wide, lay_out, 6),
+    ]
+    loads = [pltpu.make_async_copy(src, low, load_sem.at[k]) for k, (src, low, _, _, _) in enumerate(order)]
+    for c in loads:
+        c.start()
+    whole_in = pltpu.make_async_copy(block_in, block_low, load_sem.at[5])
+    whole_in.start()
+    whole_out = pltpu.make_async_copy(block_low, block_out, store_sem.at[9])
+
+    def row(ref, index, rate):
+        ref[...] = (small_ref[index : index + 1, :] * (inverse * rates[rate])).reshape(ref.shape)
+
+    for ref, index, rate in ((ob_out, 0, 1), (g1_out, 1, 2), (s1_out, 2, 2), (c2_out, 3, 4), (g2_out, 4, 5), (s2_out, 5, 5)):
+        row(ref, index, rate)
+    b1_out[...] = (small_ref[pl.ds(8 + t, 1), :] * (inverse * rates[3])).reshape(b1_out.shape)
+    own = small_ref[pl.ds(12 + t, 1), :]
+    for k in range(2):
+        qvb_out[k : k + 1, :] = own[:, k * cols_t : (k + 1) * cols_t] * (inverse * rates[0])
+    for a in range(HEADS_T):
+        at = 2 * cols_t + a * 2 * BUCKETS
+        table_out[a : a + 1, :] = own[:, at : at + 2 * BUCKETS] * (inverse * rates[7])
+
+    stores = []
+
+    def store(k, src, dst):
+        stores.append(pltpu.make_async_copy(src, dst, store_sem.at[k]))
+
+    for k, (_, low, wide, out, rate) in enumerate(order):
+        loads[k].wait()
+        step = 128
+        if out is not None:
+            factor = inverse if rate is None else inverse * rates[rate]
+
+            @pl.loop(0, low.shape[0] // step)
+            def _(i, low=low, wide=wide, out=out, factor=factor, k=k):
+                sl = pl.ds(pl.multiple_of(i * step, step), step)
+                wide[sl, :] = low[sl, :].astype(jnp.float32) * factor
+                pltpu.make_async_copy(wide.at[sl], out.at[sl], store_sem.at[k]).start()
+
+            store(k, wide, out)
+            if k == 0:
+                whole_in.wait()
+                whole_out.start()
+            continue
+        parts = ((2, 0, 0), (None, 1, 1), (0, 2, 0), (1, 3, 0))
+        for j, (n, at, rate) in enumerate(parts):
+            sl = pl.ds(at * cols_t, cols_t)
+            wide[sl, :] = low[sl, :].astype(jnp.float32) * (inverse * rates[rate])
+            store(5 + j, wide.at[sl], wo_out if n is None else qkv_out.at[n])
+            stores[-1].start()
+    whole_out.wait()
+    for c in stores:
+        c.wait()
+
+
+def finish(rates, small, block_all, in_all, sum1, sum2, sum3, lay_all, cols_t):
+    f32, bf16 = jnp.float32, jnp.bfloat16
+    shape = jax.ShapeDtypeStruct
+    here = pl.BlockSpec(memory_space=pltpu.VMEM)
+    away = pl.BlockSpec(memory_space=pl.ANY)
+    model = in_all.shape[1]
+    vector = (shape((model,), f32), here)
+    outs = [
+        (shape(block_all.shape, bf16), away),
+        (shape(in_all.shape, f32), away),
+        (shape(lay_all.shape, f32), away),
+        (shape((3, cols_t, model), f32), away),
+        (shape((2, cols_t), f32), here),
+        (shape((HEADS_T, 2 * BUCKETS), f32), here),
+        (shape((cols_t, model), f32), away),
+        vector, vector, vector,
+        (shape(sum1.shape, f32), away),
+        vector,
+        (shape(sum2.shape, f32), away),
+        vector, vector, vector,
+    ]
+    wide = [in_all, sum1, sum2, sum3, lay_all]
+    return pl.pallas_call(
+        finish_kernel,
+        in_specs=[pl.BlockSpec(memory_space=pltpu.SMEM), here] + [away] * 6,
+        out_specs=[spec for _, spec in outs],
+        out_shape=[s for s, _ in outs],
+        scratch_shapes=[pltpu.VMEM(v.shape, bf16) for v in wide]
+        + [pltpu.VMEM(v.shape, f32) for v in wide]
+        + [pltpu.VMEM(block_all.shape, bf16), pltpu.SemaphoreType.DMA((6,)), pltpu.SemaphoreType.DMA((10,))],
+        compiler_params=pltpu.CompilerParams(vmem_limit_bytes=60 * 2**20),
+        name="finish",
+    )(rates, small, block_all, in_all, sum1, sum2, sum3, lay_all)
 
 
 def local(
@@ -1114,68 +1353,27 @@
     bias_table, out_weight, out_bias, ln1_gain, ln1_bias, ffn_in_weight, ffn_in_bias, ffn_out_weight,
     ffn_out_bias, ln2_gain, ln2_bias, group_rates,
 ):
-    me = lax.axis_index("tensor")
-    win = rel_x.shape[1]
-    model = tokens_in.shape[1]
-    heads_t = bias_table.shape[1]
-    cols_t = heads_t * HD
-    hid_t = ffn_in_weight.shape[1]
-    tok_rows = tokens_in.shape[0] // n_t
-
-    def mine(whole):
-        return lax.dynamic_slice_in_dim(whole, me * (whole.shape[0] // n_t), whole.shape[0] // n_t)
-
-    zeros = jnp.zeros((cols_t,), jnp.float32)
-    cols_own = jnp.pad(jnp.stack([qv_bias[0], zeros, qv_bias[1]], axis=1), ((0, 0), (0, 125)))
-    rows_own = jnp.concatenate(
-        [
-            ffn_in_bias[None, :],
-            jnp.pad(bias_table.T.astype(jnp.float32), ((0, 0), (0, hid_t - 2 * BUCKETS))),
-            jnp.zeros((8 - 1 - heads_t, hid_t), jnp.float32),
-        ],
-        axis=0,
-    )
-    freq_index = jnp.arange(LFREQ).astype(jnp.float32)
-    freq = jnp.exp(freq_index * (-math.log(1000.0) / LFREQ))
-    freq = jnp.broadcast_to(jnp.concatenate([freq, freq])[None, :], (8, 2 * LFREQ))
-    zero = jnp.zeros_like(out_bias)
-    vec = jnp.stack([out_bias, ln1_gain, ln1_bias, ffn_out_bias, ln2_gain, ln2_bias, zero, zero])
-    relx, rely = mine(rel_x)[0], mine(rel_y)[0]
-
     (
         probs, qkvt, context_t, layer_low, features, unit_one, inverse_one, normed_low, pre_all, hid_all,
         block_own, dresid_two, sums, wqkv, wo, w1, w2,
     ) = forward_window(
-        n_dp, mine(tokens_in), mine(box_coords), relx, rely, mine(mask_tokens)[:, None], mine(cotangent), freq,
-        layout_weight, vec, cols_own, rows_own, jnp.transpose(qkv_weight, (0, 2, 1)), out_weight, ffn_in_weight, ffn_out_weight,
+        [
+            box_coords.T, mask_tokens.reshape(-1, 128), layout_weight, qv_bias, ffn_in_bias, bias_table.T,
+            out_bias, ln1_gain, ln1_bias, ffn_out_bias, ln2_gain, ln2_bias,
+        ],
+        [
+            tokens_in, cotangent, rel_x, rel_y, jnp.transpose(qkv_weight, (0, 2, 1)), out_weight, ffn_in_weight,
+            ffn_out_weight,
+        ],
     )
-    block_out, in_all, sum1, sum2, sum3, lay_all, small = backward_window(
-        n_dp, layout_weight.shape[0], inverse_one, vec, sums, dresid_two, hid_all, pre_all, unit_one, normed_low, layer_low,
-        features, qkvt, context_t, probs, relx, rely, w1, w2, wo, wqkv, block_own,
+    block_all, in_all, sum1, sum2, sum3, lay_all, small = backward_window(
+        n_dp, layout_weight.shape[0], inverse_one, ln1_gain, sums, dresid_two, hid_all, pre_all, unit_one, normed_low,
+        layer_low, features, qkvt, context_t, probs, rel_x, rel_y, w1, w2, wo, wqkv, block_own,
     )
-    f32 = jnp.float32
-    count = small[6, 0]
-    factor = group_rates / count
-    own = lax.dynamic_slice_in_dim(small, 12 + me, 1)[0]
-    qkv_sum = jnp.stack([sum3[2 * cols_t : 3 * cols_t], sum3[3 * cols_t : 4 * cols_t], sum3[:cols_t]])
-    return (
-        block_out,
-        in_all.astype(f32) / count,
-        lay_all.astype(f32) * factor[6],
-        jnp.transpose(qkv_sum, (0, 2, 1)).astype(f32) * factor[0],
-        own[: 2 * cols_t].reshape(2, cols_t) * factor[0],
-        own[2 * cols_t : 3 * cols_t].reshape(heads_t, 2 * BUCKETS).T * factor[7],
-        sum3[cols_t : 2 * cols_t].astype(f32) * factor[1],
-        small[0] * factor[1],
-        small[1] * factor[2],
-        small[2] * factor[2],
-        sum1.astype(f32) * factor[3],
-        lax.dynamic_slice_in_dim(small, 8 + me, 1)[0] * factor[3],
-        sum2.astype(f32) * factor[4],
-        small[3] * factor[4],
-        small[4] * factor[5],
-        small[5] * factor[5],
-    )
+    out = list(finish(group_rates, small, block_all, in_all, sum1, sum2, sum3, lay_all, out_weight.shape[0]))
+    out[3] = jnp.transpose(out[3], (0, 2, 1))
+    out[5] = out[5].T
+    return tuple(out)
 
 
 def solution(mesh):

time: 248 us -> 195 us (0.79)
  other arithmetic: 24.3 us -> 0 us
  local copies, waits for them, and re-layouts: 15.4 us -> 0 us
  Pallas kernels: 206 us -> 194 us
    mul x8 -> x0, other arithmetic: 18.9 us -> none  [the longest x1 4.87 us: local(): small[5] * factor[5]]
    pallas_call x1, Pallas kernels: 135 us -> 125 us  [backward_window(): pl.pallas_call(functools.partial(backward_kernel, n_dp), in_specs=[here]...]
    div x2 -> x0, other arithmetic: 4.56 us -> none  [the longest x1 3.91 us: local(): in_all.astype(f32) / count]
    dynamic_slice x3 -> x0, local copies, waits for them, and re-layouts: 3.37 us -> none  [mine(): lax.dynamic_slice_in_dim(whole, me * (whole.shape[0] // n_t), whole.shape...]
    squeeze x1 -> x0, local copies, waits for them, and re-layouts: 3.05 us -> none  [local(): relx, rely = (mine(rel_x)[0], mine(rel_y)[0])]
    pallas_call x1 -> x2, Pallas kernels: 71.7 us -> 68.8 us  [the longest x1 56.6 us: forward_window(): pl.pallas_call(forward_kernel, in_specs=[here] * len(small) + [away] * le...]
    unnamed x36 -> x0, local copies, waits for them, and re-layouts: 2.6 us -> none
where the time goes in v5:
time: 195 us
  Pallas kernels  194 us (99%)
    pallas_call x1, Pallas kernels, backward_window(): pl.pallas_call(functools.partial(backward_kernel, n_dp), in_specs=[here]...  125 us
    pallas_call x1, Pallas kernels, forward_window(): pl.pallas_call(forward_kernel, in_specs=[here] * len(small) + [away] * le...  56.6 us
    pallas_call x1, Pallas kernels, finish(): pl.pallas_call(finish_kernel, in_specs=[pl.BlockSpec(memory_space=pltpu.S...  12.3 us

profile of v5, /device:TPU:0, one launch (start us, length us, event | category | flops | bytes accessed | tf_op | source)
XLA Modules:
  0.0 195.0 jit_solution(7465362678968258690)
XLA Ops:
  0.7 56.6 %forward_window.1 = (f32[12,512,512]{2,1,0:T(8,128)}, bf16[3,768,512]{2,1,0:T(8,128)(2,1)}, bf16[768,512]{1,0:T(8,128)(2,1)}, bf16[512,768]{1,0:T(8,128)(2,1)}, ...) custom-call(s32[4,2048]{1,0:T(4,128)} %bitcast.7, ...), custom_call_target="tpu_custom_call" | custom-call | tf_op jit(solution)/shard_map/forward_window/pallas_call | solution.py:543
  57.2 125.3 %backward_window.1 = (bf16[2048,768]{1,0:T(8,128)(2,1)}, bf16[2048,768]{1,0:T(8,128)(2,1)}, bf16[768,768]{1,0:T(8,128)(2,1)}, bf16[768,768]{1,0:T(8,128)(2,1)}, ...) custom-call(f32[512,1]{1,0:T(8,128)} %get-tuple-element.56.inv_ref, f32[768]{0:T(1024)} %gain_ref.1, ...), custom_call_target="tpu_custom_call" | custom-call | tf_op jit(solution)/shard_map/backward_window/pallas_call | solution.py:1217
  182.5 12.3 %finish.1 = (bf16[2048,768]{1,0:T(8,128)(2,1)}, f32[2048,768]{1,0:T(8,128)}, f32[512,768]{1,0:T(8,128)}, f32[3,192,768]{2,1,0:T(8,128)}, f32[2,192]{1,0:T(2,128)...) custom-call(f32[8]{0:T(128)} %rates.1, ...), custom_call_target="tpu_custom_call" | custom-call | tf_op jit(solution)/shard_map/finish/pallas_call | solution.py:1337

commit v6 on v5

--- a/solution.py
+++ b/solution.py
@@ -51,34 +51,57 @@
 }
 
 START, FFN, NORM, OUT, HEAD, SENT, MERGED, DLAYER, LAYOUT, TABLE, TAIL = range(11)
-A0, A1, A2, B0, B1, B2, CA, CB, CC, BLOCK, BLOCK_ON, INPUT_ON, LAY, LAY_ON, SMALL_STEP = range(15)
-X_FIRST = (False, True, True, True, False, True, True, False, True)
+A0, A1, A2, B0, B1, B2, C0, C1, C2, C3, C4, C5, C6, BLOCK, BLOCK_ON, INPUT_ON, LAY, LAY_ON, SMALL_STEP = range(19)
+X, Y, Z_NEAR, Z_FAR = range(4)
+ORDERS = (
+    ((Y, X, Z_NEAR, Z_FAR), (Z_FAR, Z_NEAR, Y)),
+    ((Z_NEAR, Z_FAR, X, Y), (Z_FAR, Z_NEAR, Y)),
+    ((X, Y, Z_NEAR, Z_FAR), (Z_FAR, Z_NEAR, Y)),
+    ((X, Y, Z_NEAR, Z_FAR), (Z_FAR, Z_NEAR, Y)),
+    ((X, Z_NEAR, Z_FAR, Y), (Z_FAR, Z_NEAR, Y)),
+    ((Y, Z_NEAR, Z_FAR, X), (Z_FAR, Z_NEAR, Y)),
+    ((Y, X, Z_NEAR, Z_FAR), (Z_FAR, Z_NEAR, Y)),
+    ((Y, X, Z_NEAR, Z_FAR), (Z_FAR, Z_NEAR, Y)),
+    ((Y, X, Z_NEAR, Z_FAR), (Z_FAR, Z_NEAR, Y)),
+    ((X, Y, Z_NEAR, Z_FAR), (Z_FAR, Z_NEAR, Y)),
+    ((Y, X, Z_NEAR, Z_FAR), (Y, Z_FAR, Z_NEAR)),
+    ((X, Z_NEAR, Z_FAR, Y), (Z_FAR, Z_NEAR, Y)),
+    ((X, Z_NEAR, Z_FAR, Y), (Z_FAR, Z_NEAR, Y)),
+)
 SCHEDULE = {
-    (START, 0): ((BLOCK, 2),),
-    (FFN, 2): ((BLOCK_ON, 2),),
-    (FFN, 8): ((A0, 1),),
-    (FFN, 9): ((A1, 1),),
-    (OUT, 0): ((A1, 2),),
-    (HEAD, 1): ((A2, 1),),
-    (HEAD, 2): ((B1, 1),),
-    (HEAD, 4): ((A1, 3), (B0, 1), (A2, 2),),
-    (HEAD, 8): ((A1, 4),),
-    (HEAD, 10): ((B0, 2), (A2, 3), (B2, 1),),
-    (SENT, 0): ((A0, 2), (B2, 2),),
-    (MERGED, 0): ((B1, 2),),
-    (DLAYER, 2): ((A0, 3),),
-    (TABLE, 2): ((CA, 1), (A2, 4), (B1, 3),),
-    (TABLE, 3): ((CB, 1),),
-    (TABLE, 4): ((B2, 3), (A0, 4),),
-    (TABLE, 5): ((BLOCK, 0), (BLOCK, 1), (BLOCK, 3),),
-    (TABLE, 6): ((CA, 2), (CC, 1), (B1, 4),),
-    (TABLE, 8): ((B0, 3),),
-    (TABLE, 11): ((B2, 4),),
+    (START, 0): ((BLOCK, 1), (BLOCK, 3),),
+    (FFN, 11): ((A1, 0),),
+    (NORM, 0): ((A2, 0), (BLOCK_ON, 3),),
+    (OUT, 0): ((BLOCK_ON, 1),),
+    (HEAD, 1): ((B2, 0),),
+    (HEAD, 5): ((A1, 1), (B0, 0), (A2, 1),),
+    (HEAD, 6): ((A0, 0), (B2, 1),),
+    (HEAD, 9): ((A2, 2),),
+    (HEAD, 10): ((B0, 1),),
+    (SENT, 0): ((B1, 0), (B2, 2), (A2, 3),),
+    (MERGED, 0): ((B0, 2), (B1, 1), (A0, 1),),
+    (DLAYER, 0): ((B2, 3),),
+    (DLAYER, 1): ((A1, 2), (A2, 4),),
+    (DLAYER, 3): ((BLOCK, 2), (B0, 3),),
+    (LAYOUT, 0): ((C3, 0),),
+    (TABLE, 0): ((C0, 0), (C1, 0), (C5, 0), (A0, 2), (B1, 2), (A2, 5), (B2, 4),),
+    (TABLE, 2): ((C4, 0),),
+    (TABLE, 3): ((A1, 3),),
+    (TABLE, 4): ((B0, 4),),
+    (TABLE, 5): ((C2, 0), (C6, 0),),
+    (TABLE, 6): ((B1, 3), (B2, 5),),
+    (TABLE, 7): ((C3, 1), (A0, 3),),
+    (TABLE, 8): ((A1, 4), (BLOCK_ON, 2),),
+    (TABLE, 10): ((BLOCK, 0), (C5, 1),),
+    (TABLE, 11): ((C6, 1), (B0, 5),),
+    (TABLE, 15): ((A0, 4),),
     (TAIL, 0): (
-        (A1, 5), (A0, 5), (A2, 5), (CA, 3), (CC, 2), (SMALL_STEP, 0), (INPUT_ON, 0), (B0, 4), (B1, 5), (CB, 2),
-        (B2, 5), (CA, 4), (CC, 3), (BLOCK_ON, 0), (B0, 5), (BLOCK_ON, 1), (CB, 3), (CA, 5), (CC, 4), (BLOCK_ON, 3),
-        (SMALL_STEP, 1), (CC, 5), (LAY, 0), (SMALL_STEP, 2), (CB, 4), (SMALL_STEP, 3), (LAY_ON, 0), (SMALL_STEP, 4),
-        (CB, 5),
+        (A1, 5), (C3, 2), (A2, 6), (B1, 4), (B2, 6), (B0, 6), (C5, 2), (SMALL_STEP, 0), (C6, 2), (INPUT_ON, 0),
+        (A0, 5), (C3, 3), (A1, 6), (C5, 3), (C0, 1), (C6, 3), (B1, 5), (C3, 4), (C1, 1), (C5, 4), (C0, 2), (C4, 1),
+        (A0, 6), (C6, 4), (C3, 5), (C1, 2), (C2, 1), (C5, 5), (C0, 3), (B1, 6), (C4, 2), (C6, 5), (BLOCK_ON, 0),
+        (C3, 6), (C1, 3), (C2, 2), (SMALL_STEP, 1), (C0, 4), (C5, 6), (C4, 3), (C1, 4), (C6, 6), (LAY, 0), (C2, 3),
+        (SMALL_STEP, 2), (C0, 5), (C4, 4), (C1, 5), (C2, 4), (SMALL_STEP, 3), (C0, 6), (LAY_ON, 0), (C2, 5),
+        (C4, 5), (C1, 6), (SMALL_STEP, 4), (C2, 6), (C4, 6),
     ),
 }
 
@@ -229,11 +252,11 @@
 
 
 def forward_kernel(
-    box_ref, mask_ref, lay_ref, qvb_ref, b1_ref, table_ref, ob_ref, g1_ref, s1_ref, c2_ref, g2_ref, s2_ref,
-    tok_in, cot_in, rx_in, ry_in, qkv_own, wo_own, w1_own, w2_own,
+    box_ref, mask_ref, qvb_ref, b1_ref, table_ref, ob_ref, g1_ref, s1_ref, c2_ref, g2_ref, s2_ref,
+    tok_in, cot_in, rx_in, ry_in, lay_in, qkv_own, wo_own, w1_own, w2_own,
     probs_out, qkvt_out, ctxt_out, low_out, feat_out, unit_out, inv_out, nlow_out, pre_out, hid_out,
     block_out, dres_out, sums_out, wqkv_out, wo_out, w1_out, w2_out,
-    tokb, cotb, rxb, ryb, vec, rows_own, wqkv, wo, w1, w2, rows, cols, tabs, layer_in, qkvt, pbuf, ctxt, ctx, normed, pre,
+    low, feat, unit_rows, nlow, block_rows, dres_rows, lay, tokb, cotb, rxb, ryb, vec, rows_own, wqkv, wo, w1, w2, rows, cols, tabs, layer_in, qkvt, pbuf, ctxt, ctx, normed, pre,
     hid, acc, send, recv, here, out_sem, p_sem, in_sem,
 ):
     t, d = lax.axis_index("tensor"), lax.axis_index("dp")
@@ -254,7 +277,7 @@
     loads = [
         pltpu.make_async_copy(src, dst, in_sem.at[k])
         for k, (src, dst) in enumerate(
-            [(tok_in.at[own_rows], tokb), (rx_in.at[t], rxb), (ry_in.at[t], ryb), (cot_in.at[own_rows], cotb)]
+            [(tok_in.at[own_rows], tokb), (rx_in.at[t], rxb), (ry_in.at[t], ryb), (cot_in.at[own_rows], cotb), (lay_in, lay)]
         )
     ]
     for c in loads:
@@ -316,41 +339,41 @@
         for name in names:
             gathers[name].arrive_far()
 
-    wait_peers(everyone)
-    for name in SEND_ORDER:
-        gathers[name].start()
-
     lane = lax.broadcasted_iota(jnp.int32, (1, 128), 1)
     quarter = jnp.where(lane >= LFREQ, 1, 0)
     frequency = jnp.exp((lane % LFREQ).astype(f32) * (-math.log(1000.0) / LFREQ))
     loads[0].wait()
-
-    @pl.loop(0, win // block)
-    def _(i):
+    loads[4].wait()
+
+    def layer_rows(i):
         sl = pl.ds(pl.multiple_of(i * block, block), block)
         box = box_ref[:, pl.ds(pl.multiple_of(t * win + i * block, block), block)].astype(f32)
         for m in range(4):
-            feat_out[sl, 2 * LFREQ * m : 2 * LFREQ * (m + 1)] = waves(
+            feat[sl, 2 * LFREQ * m : 2 * LFREQ * (m + 1)] = waves(
                 column_of(box[m : m + 1, :]), frequency, quarter
             ).astype(bf16)
-        value = tokb[sl, :].astype(f32) + nn(feat_out[sl, :], lay_ref[...])
+        value = tokb[sl, :].astype(f32) + nn(feat[sl, :], lay[...])
         layer_in[sl, :] = value
-        low_out[sl, :] = value.astype(bf16)
+        low[sl, :] = value.astype(bf16)
         at_loop(F_FEAT, i, 4)
+
+    wait_peers(everyone)
+    for name in SEND_ORDER:
+        gathers[name].start()
+    pl.loop(0, win // block)(layer_rows)
 
     def bias_columns(pieces):
         for r in pieces:
+            turned = rows[r, :, 0:256].T
             for n, row in ((0, 4), (2, 5)):
-                for c in range(0, cols_t, 64):
-                    part = jnp.broadcast_to(rows[r, row : row + 1, 0:256][:, 0:256], (8, 256)).T
-                    cols[n, pl.ds(r * cols_t + c, 64), :] = part[c : c + 64, 0:1]
+                cols[n, pl.ds(r * cols_t, cols_t), :] = turned[0:cols_t, row : row + 1]
             tabs[HEADS_T * r : HEADS_T * (r + 1), :] = rows[r, 1 : 1 + HEADS_T, 0:128]
 
     def project(pieces):
         for n in range(3):
             for r in pieces:
                 sl = pl.ds(r * cols_t, cols_t)
-                value = nt(wqkv[n, sl, :], low_out[...])
+                value = nt(wqkv[n, sl, :], low[...])
                 if n != 1:
                     value = value + cols[n, sl, :]
                 qkvt[n, sl, :] = value.astype(bf16)
@@ -408,7 +431,7 @@
 
     last = heads // 2
     outs = [
-        (qkvt, qkvt_out), (ctxt, ctxt_out), (wqkv, wqkv_out),
+        (qkvt, qkvt_out), (ctxt, ctxt_out), (wqkv, wqkv_out), (low, low_out), (feat, feat_out),
     ]
     done = []
 
@@ -434,13 +457,15 @@
         centered = value - mean
         inverse = lax.rsqrt(jnp.mean(centered * centered, axis=1, keepdims=True) + EPSILON)
         unit = centered * inverse
-        unit_out[sl, :] = unit
+        unit_rows[sl, :] = unit
         inv_out[sl, :] = inverse
         value = unit * vec[1:2, :] + vec[2:3, :]
         normed[sl, :] = value
-        nlow_out[sl, :] = value.astype(bf16)
+        nlow[sl, :] = value.astype(bf16)
         at_loop(F_NORM, i, 4)
 
+    leave(unit_rows, unit_out)
+    leave(nlow, nlow_out)
     near_pieces(range(U0, D2 + 1))
     for src, dst in ((w1, w1_out), (w2, w2_out)):
         leave(src.at[pl.ds(0, 2)], dst.at[pl.ds(0, 2)])
@@ -448,7 +473,7 @@
         @pl.loop(0, win // 256)
         def _(i, r=r):
             sl = pl.ds(pl.multiple_of(i * 256, 256), 256)
-            value = nn(nlow_out[sl, :], w1[r]) + rows[r, 0:1, :]
+            value = nn(nlow[sl, :], w1[r]) + rows[r, 0:1, :]
             pre[r, sl, :] = value
             low_hid = gelu(value).astype(bf16)
             hid[r, sl, :] = low_hid
@@ -466,7 +491,7 @@
 
         @pl.loop(2, 4)
         def _(r, units=units):
-            value = nn(nlow_out[...], w1[r, :, units]) + rows[r, 0:1, units]
+            value = nn(nlow[...], w1[r, :, units]) + rows[r, 0:1, units]
             pre[r, :, units] = value
             low_hid = gelu(value).astype(bf16)
             hid[r, :, units] = low_hid
@@ -491,14 +516,16 @@
         centered = value - mean
         inverse = lax.rsqrt(jnp.mean(centered * centered, axis=1, keepdims=True) + EPSILON)
         unit = centered * inverse
-        block_out[sl, :] = (unit * vec[4:5, :] + vec[5:6, :]).astype(bf16)
+        block_rows[sl, :] = (unit * vec[4:5, :] + vec[5:6, :]).astype(bf16)
         mask = column_of(mask_ref[pl.ds((win // block) * t + i, 1), :].astype(f32))
         selected = mask * cotb[sl, :].astype(f32)
         scaled = selected * vec[4:5, :]
         mean_one = jnp.mean(scaled, axis=1, keepdims=True)
         mean_two = jnp.mean(scaled * unit, axis=1, keepdims=True)
         dres = (scaled - mean_one - unit * mean_two) * inverse
-        dres_out[sl, :] = dres
+        dres_rows[sl, :] = dres
+        for src, dst, k in ((block_rows, block_out, 30), (dres_rows, dres_out, 31)):
+            pltpu.make_async_copy(src.at[sl], dst.at[sl], out_sem.at[k]).start()
         sums_out[0:1, :] += jnp.sum(selected * unit, axis=0, keepdims=True)
         sums_out[1:2, :] += jnp.sum(selected, axis=0, keepdims=True)
         sums_out[2:3, :] += jnp.sum(dres, axis=0, keepdims=True)
@@ -508,12 +535,14 @@
         p_copy(i, i % 2).wait()
     for c in done:
         c.wait()
+    for src, dst, k in ((block_rows, block_out, 30), (dres_rows, dres_out, 31)):
+        pltpu.make_async_copy(src, dst, out_sem.at[k]).wait()
     for g in gathers.values():
         g.finish()
 
 
 def forward_window(small, large):
-    wo_own, w1_own = large[5:7]
+    wo_own, w1_own = large[6:8]
     win, model = large[2].shape[1], large[0].shape[1]
     cols_t, hid_t = wo_own.shape[0], w1_own.shape[1]
     heads = 4 * HEADS_T
@@ -525,15 +554,15 @@
         (shape((heads, win, win), f32), away),
         (shape((3, model, win), bf16), away),
         (shape((model, win), bf16), away),
-        (shape((win, model), bf16), here),
-        (shape((win, 8 * LFREQ), bf16), here),
-        (shape((win, model), f32), here),
+        (shape((win, model), bf16), away),
+        (shape((win, 8 * LFREQ), bf16), away),
+        (shape((win, model), f32), away),
         (shape((win, 1), f32), here),
-        (shape((win, model), bf16), here),
+        (shape((win, model), bf16), away),
         (shape((4, win, hid_t), f32), away),
         (shape((4, win, hid_t), bf16), away),
-        (shape((win, model), bf16), here),
-        (shape((win, model), f32), here),
+        (shape((win, model), bf16), away),
+        (shape((win, model), f32), away),
         (shape((8, model), f32), here),
         (shape((3, model, model), bf16), away),
         (shape((model, model), bf16), away),
@@ -546,6 +575,13 @@
         out_specs=[spec for _, spec in outs],
         out_shape=[s for s, _ in outs],
         scratch_shapes=[
+            pltpu.VMEM((win, model), bf16),
+            pltpu.VMEM((win, 8 * LFREQ), bf16),
+            pltpu.VMEM((win, model), f32),
+            pltpu.VMEM((win, model), bf16),
+            pltpu.VMEM((win, model), bf16),
+            pltpu.VMEM((win, model), f32),
+            pltpu.VMEM((8 * LFREQ, model), bf16),
             pltpu.VMEM((win, model), bf16),
             pltpu.VMEM((win, model), bf16),
             pltpu.VMEM((win, win), jnp.int32),
@@ -571,9 +607,9 @@
             pltpu.SemaphoreType.DMA((11, 10)),
             pltpu.SemaphoreType.DMA((11, 10)),
             pltpu.SemaphoreType.DMA((11,)),
-            pltpu.SemaphoreType.DMA((24,)),
+            pltpu.SemaphoreType.DMA((32,)),
             pltpu.SemaphoreType.DMA((2,)),
-            pltpu.SemaphoreType.DMA((4,)),
+            pltpu.SemaphoreType.DMA((5,)),
         ],
         compiler_params=pltpu.CompilerParams(
             vmem_limit_bytes=60 * 2**20, collective_id=0, has_side_effects=True
@@ -590,109 +626,91 @@
     return lax.dot_general(a, b, (((0,), (0,)), ((), ())), preferred_element_type=jnp.float32)
 
 
-def add_into(dst, more):
-    rows = dst.shape[0]
-    step = 64 if rows % 64 == 0 else 16
-
-    @pl.loop(0, rows // step)
-    def _(i):
-        sl = pl.ds(pl.multiple_of(i * step, step), step)
-        total = dst[sl, :].astype(jnp.float32)
-        for ref in more:
-            total = total + ref[sl, :].astype(jnp.float32)
-        dst[sl, :] = total.astype(dst.dtype)
+UNIT = 128
 
 
 class Reduce:
-    def __init__(self, slot, rows, x_first, part, core, first, second, quarters, final, extra, result, acc, sems, peers):
-        self.slot, self.rows, self.x_first, self.part, self.acc = slot, rows, x_first, part, acc
-        self.core, self.first, self.second, self.quarters, self.final = core, first, second, quarters, final
-        self.extra, self.result = extra, result
+    def __init__(self, slot, order, part, core, landing, final, extra, result, acc, sems, peers):
+        self.slot, self.order, self.part, self.core, self.landing = slot, order, part, core, landing
+        self.final, self.extra, self.result, self.acc = final, extra, result, acc
         self.send, self.recv, self.here = sems
-        self.mate, self.across, self.beside, self.along, self.further, self.side, self.level = peers
+        self.mate, self.partners, self.further, self.sides = peers
         self.total = core.at[0] if acc is None else acc
+        self.steps = order[0] + order[1]
 
     def move(self, k, src, dst, peer):
         return remote(src, dst, self.send.at[self.slot, k], self.recv.at[self.slot, k], peer)
 
-    def half(self, mine):
-        h = self.rows // 2
-        side = self.side if mine else 1 - self.side
-        return pl.ds(pl.multiple_of(side * h, h), h)
-
-    def quarter(self, level):
-        q = self.rows // 8
-        return pl.ds(pl.multiple_of(self.side * (self.rows // 2) + level * q, q), q)
+    def region(self, fixed, other=None):
+        index = [slice(None)]
+        for axis in (Z_FAR, Z_NEAR, Y):
+            if axis == other:
+                index.append(pl.ds(1 - self.sides[axis], 1))
+            elif axis in fixed:
+                index.append(pl.ds(self.sides[axis], 1))
+            else:
+                index.append(slice(None))
+        return tuple(index)
+
+    def pieces(self, stage):
+        return (0,) if X in self.order[0][:stage] else (0, 1)
 
     def moves(self, stage, piece=None):
-        h = self.rows // 2
-        if stage == 0:
-            return [self.move(p, self.part(p), self.core.at[p], self.mate) for p in range(2) if piece in (None, p)]
-        if stage == 1 and self.x_first:
-            return [self.move(2, self.core.at[1], self.first, self.across)] if piece != 0 else []
-        if stage == 1:
-            return [
-                self.move(2 + p, self.core.at[p, self.half(False)], self.first.at[pl.ds(p * h, h)], self.beside)
-                for p in range(2)
-                if piece in (None, p)
-            ]
-        if stage == 2 and self.x_first:
-            return [self.move(4, self.core.at[0, self.half(False)], self.second, self.beside)]
-        if stage == 2:
-            return [self.move(4, self.core.at[1, self.half(True)], self.second, self.across)]
-        if stage == 3:
-            return [
-                self.move(
-                    4 + k, self.core.at[0, self.quarter(xor_level(self.level, k))], self.quarters.at[k - 1], self.along[k]
-                )
-                for k in range(1, 4)
-            ]
-        if stage == 4:
-            rows = self.quarter(self.level)
-            return [self.move(7 + k, self.final, self.result.at[rows], self.along[k]) for k in range(1, 4)]
-        rows = self.half(True)
-        return [self.move(11, self.result.at[rows], self.result.at[rows], self.beside)]
+        axis = self.steps[stage]
+        peer = self.partners[axis]
+        if stage >= len(self.order[0]):
+            done = self.order[1][: stage - len(self.order[0])]
+            rows = self.region([a for a in (Z_FAR, Z_NEAR, Y) if a not in done])
+            src = self.result.at[rows] if done else self.final
+            return [self.move(10 + len(done), src, self.result.at[rows], peer)]
+        fixed = self.order[0][:stage]
+        if axis == X:
+            return [self.move(2 + 2 * stage, self.core.at[(1,) + self.region(fixed)], self.landing[stage].at[0], peer)] if piece != 0 else []
+        return [
+            self.move(2 + 2 * stage + p, self.core.at[(p,) + self.region(fixed, axis)], self.landing[stage].at[p], peer)
+            for p in self.pieces(stage)
+            if piece in (None, p)
+        ]
+
+    def to_mate(self, piece):
+        return self.move(piece, self.part(piece), self.core.at[piece], self.mate)
 
     def own_copy(self):
-        return pltpu.make_async_copy(self.final, self.result.at[self.quarter(self.level)], self.here.at[self.slot])
+        rows = self.region((Z_FAR, Z_NEAR, Y))
+        return pltpu.make_async_copy(self.final, self.result.at[rows], self.here.at[self.slot])
 
     def more(self, k):
-        return self.move(12 + k, self.final_of(k), self.extra.at[k], self.further[k])
+        return self.move(13 + k, self.final_of(k), self.extra.at[k], self.further[k])
 
     def final_of(self, k):
         return self.final if k == 0 else self.extra.at[len(self.further) + k]
 
-    def round_off(self, rows):
-        if self.acc is not None:
-            self.core[0, rows, :] = self.acc[rows, :].astype(jnp.bfloat16)
-
-    def merge(self, piece, rows, value):
-        value = value + self.core[piece, rows, :].astype(jnp.float32)
+    def merge(self, piece, unit, half, value):
+        at = (unit, half)
+        value = value.reshape(2, 2, 16, value.shape[-1]) + self.core[(piece,) + at].astype(jnp.float32)
         if piece == 0:
-            self.total[rows, :] = value.astype(self.total.dtype)
+            self.total[at] = value.astype(self.total.dtype)
         else:
-            self.core[1, rows, :] = value.astype(jnp.bfloat16)
-
-    def from_mate(self, piece):
-        for m in self.moves(0, piece):
-            m.wait_recv()
+            self.core[(1,) + at] = value.astype(jnp.bfloat16)
 
     def take(self, stage):
         for m in self.moves(stage):
             m.wait_recv()
-        h = self.rows // 2
-        if stage == 1 and self.x_first:
-            add_into(self.total, [self.first])
-        if stage == 1 and not self.x_first:
-            add_into(self.core.at[1, self.half(True)], [self.first.at[pl.ds(h, h)]])
-            add_into(self.total.at[self.half(True)], [self.first.at[pl.ds(0, h)]])
-        if stage == 2:
-            add_into(self.total.at[self.half(True)], [self.second])
-        if stage == 3:
-            value = self.total[self.quarter(self.level), :].astype(jnp.float32)
-            for k in range(3):
-                value = value + self.quarters[k].astype(jnp.float32)
-            self.final[...] = value.astype(jnp.bfloat16)
+        count = len(self.order[0])
+        if stage == count:
+            self.own_copy().wait()
+        if stage >= count:
+            return
+        axis = self.steps[stage]
+        rows = self.region(self.order[0][: stage + 1])
+        for p in (0,) if axis == X else self.pieces(stage):
+            dst = self.total if p == 0 else self.core.at[p]
+            value = dst[rows].astype(jnp.float32) + self.landing[stage][p].astype(jnp.float32)
+            if stage + 1 == count:
+                self.final[...] = value.astype(jnp.bfloat16)
+            else:
+                dst[rows] = value.astype(dst.dtype)
+        if stage + 1 == count:
             for k in range(len(self.further)):
                 self.more(k).start()
                 self.more(k).wait()
@@ -701,27 +719,34 @@
             if self.further:
                 self.final[...] = self.final_of(len(self.further))[...]
             self.own_copy().start()
-        if stage == 4:
-            self.own_copy().wait()
 
     def go(self, stage, piece=None):
-        if stage == 1 and not self.x_first and piece == 0:
-            self.round_off(self.half(False))
-        if stage == 2 and self.x_first:
-            self.round_off(self.half(False))
-        if stage == 3:
-            self.round_off(self.half(True))
+        if stage < len(self.order[0]) and self.steps[stage] != X and self.acc is not None and piece != 1:
+            rows = self.region(self.order[0][:stage], self.steps[stage])
+            self.core[(0,) + rows] = self.acc[rows].astype(jnp.bfloat16)
         for m in self.moves(stage, piece):
             m.start()
 
     def next(self, stage):
         self.take(stage)
-        if stage < 5:
+        if stage + 1 < len(self.steps):
             self.go(stage + 1)
 
-    def sent(self, stage):
-        for m in self.moves(stage):
-            m.wait_send()
+    def sent(self):
+        for stage in range(len(self.steps)):
+            for m in self.moves(stage):
+                m.wait_send()
+
+
+def landing_shapes(units, order):
+    shapes, pieces, dims = [], 2, {Z_FAR: 2, Z_NEAR: 2, Y: 2}
+    for axis in order[0]:
+        if axis == X:
+            pieces = 1
+        else:
+            dims[axis] = 1
+        shapes.append((pieces, units, dims[Z_FAR], dims[Z_NEAR], dims[Y], 16))
+    return shapes
 
 
 def xor_level(level, k):
@@ -746,8 +771,7 @@
     probs_in, rx_in, ry_in, w1_in, w2_in, wo_in, wqkv_in, block_in,
     block_all, in_all, red1, red2, red3, lay_all, small_out,
     arena, hidb, preb, dres, unit, nlow, nlow_t, dn, low_rows, qkvb, ctxtb, dctx, lowb, featb, wob, rxb, ryb, hot, acc,
-    part1, part2, part3, core1, core2, core3, first1, first2, first3, second1, second2, second3,
-    quarters1, quarters2, quarters3, final1, final2, final3, extra1, extra2, extra3, acc3, small, small_in, short,
+    part1, part2, part3, core1, core2, core3, landings, finals, extras, acc3, small, small_in, short,
     load_sem, send, recv, here, share_send, share_recv, small_send, small_recv, p_sem,
 ):
     t, d = lax.axis_index("tensor"), lax.axis_index("dp")
@@ -755,7 +779,8 @@
     beside = {"dp": xor_index(d, 1)}
     along = [None] + [{"dp": d + 2 * (xor_level((d // 2) % 4, k) - (d // 2) % 4)} for k in range(1, 4)]
     further = [{"dp": xor_index(d, bit)} for bit in bits_of(n_dp) if bit >= 8]
-    peers = (mate, across, beside, along, further, d % 2, (d // 2) % 4)
+    partners = {X: across, Y: beside, Z_NEAR: along[1], Z_FAR: along[2]}
+    peers = (mate, partners, further, {Y: d % 2, Z_NEAR: (d // 2) % 2, Z_FAR: (d // 4) % 2})
     sems = (send, recv, here)
     f32, bf16 = jnp.float32, jnp.bfloat16
     win, model = dres.shape
@@ -805,42 +830,33 @@
     for c in ld_rest[1:]:
         c.start()
 
-    def chunks(slot, sizes, orders, parts, core, first, second, quarters, final, extra, result, acc=None):
+    def chunks(first, units, parts, core, result, acc=None):
         out, at = [], 0
-        for k, (rows, x_first, part) in enumerate(zip(sizes, orders, parts)):
-            q = pl.ds(at // 8, rows // 8)
+        for k, (count, part) in enumerate(zip(units, parts)):
+            rows = pl.ds(at, count)
+            slot = first + k
             out.append(
                 Reduce(
-                    slot + k, rows, x_first, part, core.at[:, pl.ds(at, rows)], first.at[pl.ds(at, rows)],
-                    second.at[pl.ds(at // 2, rows // 2)], quarters.at[:, q], final.at[q], extra.at[:, q],
-                    result.at[pl.ds(at, rows)], None if acc is None else acc.at[pl.ds(at, rows)], sems, peers,
+                    slot, ORDERS[slot], part, core.at[:, rows], landings[slot], finals[slot], extras[slot],
+                    result.at[rows], None if acc is None else acc.at[rows], sems, peers,
                 )
             )
-            at += rows
+            at += count
         return out
 
     third = hid_t // 3
-    sizes = [third] * 3
-
-    def thirds(ref):
-        return [lambda p, k=k: ref.at[p, pl.ds(k * third, third)] for k in range(3)]
-
-    s2 = chunks(
-        0, sizes, X_FIRST[:3], thirds(part2), core2, first2, second2, quarters2, final2, extra2, red2
+
+    def pairs(ref):
+        return [lambda p, k=k: ref.at[p, pl.ds(2 * k, 2)] for k in range(3)]
+
+    s2 = chunks(0, [2] * 3, pairs(part2), core2, red2)
+    s1 = chunks(3, [2] * 3, pairs(part1), core1, red1)
+    s3 = chunks(
+        6, [1] * 7,
+        [lambda p, k=k: part2.at[p, pl.ds(k, 1)] for k in range(6)] + [lambda p: part3.at[p]],
+        core3, red3, acc3,
     )
-    s1 = chunks(
-        3, sizes, X_FIRST[3:6], thirds(part1), core1, first1, second1, quarters1, final1, extra1, red1
-    )
-    lay_t = lay_all.shape[0] // 4
-    s3 = chunks(
-        6, [2 * cols_t, 2 * cols_t, lay_t], X_FIRST[6:],
-        [
-            lambda p: part2.at[p, pl.ds(0, 2 * cols_t)],
-            lambda p: part2.at[p, pl.ds(2 * cols_t, 2 * cols_t)],
-            lambda p: part3.at[p],
-        ],
-        core3, first3, second3, quarters3, final3, extra3, red3, acc3,
-    )
+    lay_t = featb.shape[1] // 4
 
     def share(k, src, whole, rows, part=0, parts=1):
         def at(index):
@@ -877,7 +893,7 @@
         share(k, block_in.at[pl.ds(k * quarter_win, quarter_win)], block_all, quarter_win, k, 4) for k in range(4)
     ]
     sh_in = share(4, low_rows, in_all, win)
-    sh_lay = share(5, red3.at[pl.ds(4 * cols_t, lay_t)], lay_all, lay_t)
+    sh_lay = share(5, red3.at[pl.ds(6, 1)], lay_all, 1)
     bits = [mate, across, beside, along[1], along[2]] + further
 
     def small_move(k):
@@ -889,7 +905,7 @@
         if k + 1 < len(bits):
             small_move(k + 1).start()
 
-    named = dict(zip(range(A0, CC + 1), s2 + s1 + s3))
+    named = dict(zip(range(A0, C6 + 1), s2 + s1 + s3))
 
     def run(what, stage):
         if what in named:
@@ -946,19 +962,27 @@
         sl = pl.ds(pl.multiple_of(c * third, third), third)
         return nn(nlow_t[sl, :], hidb[h_rows(r), :])
 
+    def blocks(value):
+        return value.reshape(value.shape[0] // UNIT, 2, 2, 2, 16, value.shape[1])
+
     def for_mate(group, grad, r, part):
         @pl.loop(0, 3)
         def _(c):
-            part[r // 2, pl.ds(pl.multiple_of(c * third, third), third), :] = grad(r, c).astype(bf16)
+            part[r // 2, pl.ds(2 * c, 2)] = blocks(grad(r, c).astype(bf16))
 
         for g in group:
-            g.go(0, r // 2)
+            g.to_mate(r // 2).start()
+
+    def merge_all(g, piece, value):
+        half = UNIT // 2
+        for k in range(value.shape[0] // half):
+            g.merge(piece, k // 2, k % 2, value[k * half : (k + 1) * half])
 
     def for_own(group, grad, r):
         for c, g in enumerate(group):
-            g.from_mate(r // 2)
-            g.merge(r // 2, pl.ds(0, third), grad(r, c))
-            g.go(1, r // 2)
+            g.to_mate(r // 2).wait_recv()
+            merge_all(g, r // 2, grad(r, c))
+            g.go(0, r // 2)
 
     for r in order[:2]:
         ld_hid[r].wait()
@@ -967,7 +991,7 @@
             wait_peers(everyone)
             at_slot(START)
             for g in s2:
-                g.go(0, r // 2)
+                g.to_mate(r // 2).start()
         else:
             for_mate(s2, grad_w2, r, part2)
 
@@ -1013,7 +1037,8 @@
     for h in range(2):
         p_load(h, h).start()
     for g in s2:
-        g.sent(0)
+        for p in range(2):
+            g.to_mate(p).wait_send()
 
     ld_rest[1].wait()
 
@@ -1078,23 +1103,30 @@
     def grad_proj(n, r):
         return nn(qkvb[n, rows_of(r), :], lowb[...])
 
-    halves = (
-        (s3[0], lambda r: grad_proj(2, r), grad_out),
-        (s3[1], lambda r: grad_proj(0, r), lambda r: grad_proj(1, r)),
-    )
-    for k, (g, upper, lower) in enumerate(halves):
-        for r in (3, 1):
-            at = 2 * cols_t * k
-            part2[r // 2, at : at + cols_t, :] = upper(r).astype(bf16)
-            part2[r // 2, at + cols_t : at + 2 * cols_t, :] = lower(r).astype(bf16)
-            g.go(0, r // 2)
+    halves = (lambda r: grad_proj(2, r), grad_out, lambda r: grad_proj(0, r), lambda r: grad_proj(1, r))
+    sixth = UNIT // 2
+    each = cols_t // sixth
+    for r in (3, 1):
+        for k, grad in enumerate(halves):
+            value = grad(r).astype(bf16)
+            for j in range(each):
+                at = k * each + j
+                part2[r // 2, at // 2, at % 2] = value[j * sixth : (j + 1) * sixth].reshape(2, 2, 16, model)
+            if k % 2 == 1:
+                for g in s3[:6][3 * (k // 2) : 3 * (k // 2) + 3]:
+                    g.to_mate(r // 2).start()
     at_slot(SENT)
-    for g, upper, lower in halves:
-        for r in (2, 0):
-            g.from_mate(r // 2)
-            g.merge(r // 2, pl.ds(0, cols_t), upper(r))
-            g.merge(r // 2, pl.ds(cols_t, cols_t), lower(r))
-            g.go(1, r // 2)
+    for r in (2, 0):
+        for k, grad in enumerate(halves):
+            value = grad(r)
+            for j in range(each):
+                at = k * each + j
+                g = s3[at // 2]
+                if at % 2 == 0:
+                    g.to_mate(r // 2).wait_recv()
+                g.merge(r // 2, 0, at % 2, value[j * sixth : (j + 1) * sixth])
+                if at % 2 == 1:
+                    g.go(0, r // 2)
     at_slot(MERGED)
 
     @pl.loop(0, win // block)
@@ -1116,13 +1148,11 @@
         return tn(featb[:, pl.ds(pl.multiple_of(index * lay_t, lay_t), lay_t)], low_rows[...])
 
     for r in (3, 1):
-        part3[r // 2] = grad_lay(r).astype(bf16)
-        s3[2].go(0, r // 2)
+        part3[r // 2] = blocks(grad_lay(r).astype(bf16))
+        s3[6].to_mate(r // 2).start()
     at_slot(LAYOUT)
-    for r in (2, 0):
-        s3[2].from_mate(r // 2)
-        s3[2].merge(r // 2, pl.ds(0, lay_t), grad_lay(r))
-        s3[2].go(1, r // 2)
+    for_own(s3[6:], lambda r, c: grad_lay(r), 2)
+    for_own(s3[6:], lambda r, c: grad_lay(r), 0)
     share_start(sh_in)
 
     ones = jnp.ones((8, win), bf16)
@@ -1185,10 +1215,10 @@
     for c in sh_block + [sh_in, sh_lay]:
         share_end(c)
     for g in s1 + s3:
-        g.sent(0)
+        for p in range(2):
+            g.to_mate(p).wait_send()
     for g in s2 + s1 + s3:
-        for stage in range(1, 6):
-            g.sent(stage)
+        g.sent()
 
 
 def backward_window(n_dp, lay_rows, inv, gain, sums, dres, hid, pre, unit, nlow, low, feat, qkvt, ctxt, probs, rx, ry, w1, w2, wo, wqkv, block_own):
@@ -1196,9 +1226,12 @@
     heads = 4 * HEADS_T
     cols_t = HEADS_T * HD
     lay_t = lay_rows // 4
-    rest = 4 * cols_t + lay_t
+    units = model // UNIT
+    rest = (4 * cols_t + lay_t) // UNIT
+    block = (2, 2, 2, 16, model)
     more = max(0, len(bits_of(n_dp)) - 3)
     levels = 5 + more
+    sizes = [2] * 6 + [1] * 7
     f32, bf16 = jnp.float32, jnp.bfloat16
     shape = jax.ShapeDtypeStruct
     here = pl.BlockSpec(memory_space=pltpu.VMEM)
@@ -1206,10 +1239,10 @@
     outs = [
         (shape((4 * win, model), bf16), away),
         (shape((4 * win, model), bf16), away),
-        (shape((model, model), bf16), away),
-        (shape((model, model), bf16), away),
-        (shape((rest, model), bf16), away),
-        (shape((lay_rows, model), bf16), away),
+        (shape((units,) + block, bf16), away),
+        (shape((units,) + block, bf16), away),
+        (shape((rest,) + block, bf16), away),
+        (shape((4,) + block, bf16), away),
         (shape((SMALL, model), f32), here),
     ]
     V = pltpu.VMEM
@@ -1225,16 +1258,13 @@
             V((win, model), bf16), V((3, model, win), bf16), V((model, win), bf16), V((model, win), bf16),
             V((win, model), bf16), V((win, lay_rows), bf16), V((model, model), bf16), V((win, win), jnp.int32),
             V((win, win), jnp.int32), V((2, 2 * BUCKETS * ROWS, win), bf16), V((heads * ROWS, 2 * BUCKETS * ROWS), f32),
-            V((2, model, model), bf16), V((2, model, model), bf16), V((2, lay_t, model), bf16),
-            V((2, model, model), bf16), V((2, model, model), bf16), V((2, rest, model), bf16),
-            V((model, model), bf16), V((model, model), bf16), V((rest, model), bf16),
-            V((model // 2, model), bf16), V((model // 2, model), bf16), V((rest // 2, model), bf16),
-            V((3, model // 8, model), bf16), V((3, model // 8, model), bf16), V((3, rest // 8, model), bf16),
-            V((model // 8, model), bf16), V((model // 8, model), bf16), V((rest // 8, model), bf16),
-            V((2 * more + 1, model // 8, model), bf16), V((2 * more + 1, model // 8, model), bf16),
-            V((2 * more + 1, rest // 8, model), bf16),
-            V((rest, model), f32), V((levels + 1, SMALL, model), f32), V((levels, SMALL, model), f32), V((8, model), f32),
-            S((29,)), S((9, 12 + max(1, more))), S((9, 12 + max(1, more))), S((9,)), S((6, 4)), S((6, 3)),
+            V((2, units) + block, bf16), V((2, units) + block, bf16), V((2, 1) + block, bf16),
+            V((2, units) + block, bf16), V((2, units) + block, bf16), V((2, rest) + block, bf16),
+            [[V(s + (model,), bf16) for s in landing_shapes(n, o)] for n, o in zip(sizes, ORDERS)],
+            [V((n, 1, 1, 1, 16, model), bf16) for n in sizes],
+            [V((2 * more + 1, n, 1, 1, 1, 16, model), bf16) for n in sizes], V((rest,) + block, f32),
+            V((levels + 1, SMALL, model), f32), V((levels, SMALL, model), f32), V((8, model), f32),
+            S((29,)), S((len(sizes), 13 + more)), S((len(sizes), 13 + more)), S((len(sizes),)), S((6, 4)), S((6, 3)),
             S((levels,)), S((levels,)), S((2,)),
         ],
         compiler_params=pltpu.CompilerParams(
@@ -1358,19 +1388,20 @@
         block_own, dresid_two, sums, wqkv, wo, w1, w2,
     ) = forward_window(
         [
-            box_coords.T, mask_tokens.reshape(-1, 128), layout_weight, qv_bias, ffn_in_bias, bias_table.T,
+            box_coords.T, mask_tokens.reshape(-1, 128), qv_bias, ffn_in_bias, bias_table.T,
             out_bias, ln1_gain, ln1_bias, ffn_out_bias, ln2_gain, ln2_bias,
         ],
         [
-            tokens_in, cotangent, rel_x, rel_y, jnp.transpose(qkv_weight, (0, 2, 1)), out_weight, ffn_in_weight,
-            ffn_out_weight,
+            tokens_in, cotangent, rel_x, rel_y, layout_weight, jnp.transpose(qkv_weight, (0, 2, 1)), out_weight,
+            ffn_in_weight, ffn_out_weight,
         ],
     )
     block_all, in_all, sum1, sum2, sum3, lay_all, small = backward_window(
         n_dp, layout_weight.shape[0], inverse_one, ln1_gain, sums, dresid_two, hid_all, pre_all, unit_one, normed_low,
         layer_low, features, qkvt, context_t, probs, rel_x, rel_y, w1, w2, wo, wqkv, block_own,
     )
-    out = list(finish(group_rates, small, block_all, in_all, sum1, sum2, sum3, lay_all, out_weight.shape[0]))
+    sums = [v.reshape(-1, v.shape[-1]) for v in (sum1, sum2, sum3, lay_all)]
+    out = list(finish(group_rates, small, block_all, in_all, *sums, out_weight.shape[0]))
     out[3] = jnp.transpose(out[3], (0, 2, 1))
     out[5] = out[5].T
     return tuple(out)

time: 195 us -> 189 us (0.969)
  Pallas kernels: 194 us -> 187 us
    pallas_call x1, Pallas kernels: 125 us -> 119 us  [backward_window(): pl.pallas_call(functools.partial(backward_kernel, n_dp), in_specs=[here]...]
where the time goes in v6:
time: 189 us; the launch traced here: 188 us
  Pallas kernels  187 us (99%)
    pallas_call x1, Pallas kernels, backward_window(): pl.pallas_call(functools.partial(backward_kernel, n_dp), in_specs=[here]...  119 us
    pallas_call x1, Pallas kernels, forward_window(): pl.pallas_call(forward_kernel, in_specs=[here] * len(small) + [away] * le...  56.1 us
    pallas_call x1, Pallas kernels, finish(): pl.pallas_call(finish_kernel, in_specs=[pl.BlockSpec(memory_space=pltpu.S...  12.3 us

profile of v6, /device:TPU:0, one launch (start us, length us, event | category | flops | bytes accessed | tf_op | source)
XLA Modules:
  0.0 188.2 jit_solution(4806301637417959207)
XLA Ops:
  0.7 56.1 %forward_window.1 = (f32[12,512,512]{2,1,0:T(8,128)}, bf16[3,768,512]{2,1,0:T(8,128)(2,1)}, bf16[768,512]{1,0:T(8,128)(2,1)}, bf16[512,768]{1,0:T(8,128)(2,1)}, ...) custom-call(s32[4,2048]{1,0:T(4,128)} %bitcast.15, ...), custom_call_target="tpu_custom_call" | custom-call | tf_op jit(solution)/shard_map/forward_window/pallas_call | solution.py:572
  56.7 119.0 %backward_window.1 = (bf16[2048,768]{1,0:T(8,128)(2,1)}, bf16[2048,768]{1,0:T(8,128)(2,1)}, bf16[6,2,2,2,16,768]{5,4,3,2,1,0:T(8,128)(2,1)}, bf16[6,2,2,2,16,768...) custom-call(f32[512,1]{1,0:T(8,128)} %get-tuple-element.56.inv_ref, ...), custom_call_target="tpu_custom_call" | custom-call | tf_op jit(solution)/shard_map/backward_window/pallas_call | solution.py:1250
  175.8 12.3 %finish.1 = (bf16[2048,768]{1,0:T(8,128)(2,1)}, f32[2048,768]{1,0:T(8,128)}, f32[512,768]{1,0:T(8,128)}, f32[3,192,768]{2,1,0:T(8,128)}, f32[2,192]{1,0:T(2,128)...) custom-call(f32[8]{0:T(128)} %rates.1, ...), custom_call_target="tpu_custom_call" | custom-call | tf_op jit(solution)/shard_map/finish/pallas_call | solution.py:1367

commit v7 on v6

--- a/solution.py
+++ b/solution.py
@@ -20,88 +20,83 @@
 AT_R, AT_Q, AT_K, AT_V, AT_O, U0, D0, U1, D1, U2, D2 = range(11)
 WAYS = {
     AT_R: (1, 0),
-    AT_Q: (2, 1),
-    AT_K: (2, 1),
-    AT_V: (2, 0),
-    AT_O: (2, 1),
+    AT_Q: (2, 0),
+    AT_K: (2, 0),
+    AT_V: (2, 1),
+    AT_O: (2, 0),
     U0: (4, 0),
     D0: (4, 0),
     U1: (4, 0),
-    D1: (4, 0),
-    U2: (2, 1),
+    D1: (2, 1),
+    U2: (2, 0),
     D2: (1, 0),
 }
-SEND_ORDER = (AT_Q, AT_K, AT_V, AT_O, AT_R, D1, D0, U0, U1, U2, D2)
+SEND_ORDER = (AT_Q, AT_V, AT_K, D0, AT_R, U0, U1, AT_O, D1, U2, D2)
 FORWARD = {
     (F_NEAR, 0): ((AT_Q, 0),),
-    (F_HEAD, 2): ((AT_K, 0), (AT_V, 0), (AT_Q, 1),),
-    (F_HEAD, 4): ((AT_O, 0), (AT_K, 1), (AT_R, 0), (AT_V, 1),),
-    (F_HEAD, 5): ((D1, 0),),
-    (F_BOTH, 0): ((D0, 0),),
-    (F_HEAD, 6): ((D1, 1),),
-    (F_HEAD, 7): ((U0, 0),),
-    (F_HEAD, 8): ((U1, 0), (D0, 1), (D1, 2),),
-    (F_HEAD, 9): ((AT_O, 1),),
-    (F_HEAD, 10): ((U0, 1),),
-    (F_HEAD, 11): ((U1, 1),),
-    (F_CONTEXT, 0): ((U2, 0), (D0, 2),),
-    (F_NORM, 1): ((U0, 2),),
-    (F_NORM, 3): ((U1, 2),),
-    (F_UP, 2): ((D2, 0), (U2, 1),),
+    (F_HEAD, 1): ((AT_V, 0),),
+    (F_HEAD, 2): ((AT_K, 0), (AT_Q, 1),),
+    (F_HEAD, 3): ((D0, 0),),
+    (F_HEAD, 4): ((AT_V, 1), (AT_R, 0), (U0, 0), (AT_K, 1),),
+    (F_HEAD, 5): ((U1, 0), (D0, 1),),
+    (F_HEAD, 6): ((AT_O, 0),),
+    (F_HEAD, 7): ((U0, 1),),
+    (F_HEAD, 9): ((U1, 1), (D0, 2), (D1, 0), (AT_O, 1),),
+    (F_HEAD, 10): ((U0, 2),),
+    (F_CONTEXT, 0): ((U2, 0),),
+    (F_NORM, 1): ((U1, 2),),
+    (F_NORM, 3): ((D1, 1),),
+    (F_UP, 2): ((U2, 1), (D2, 0),),
 }
 
 START, FFN, NORM, OUT, HEAD, SENT, MERGED, DLAYER, LAYOUT, TABLE, TAIL = range(11)
 A0, A1, A2, B0, B1, B2, C0, C1, C2, C3, C4, C5, C6, BLOCK, BLOCK_ON, INPUT_ON, LAY, LAY_ON, SMALL_STEP = range(19)
 X, Y, Z_NEAR, Z_FAR = range(4)
 ORDERS = (
+    ((Z_NEAR, Z_FAR, X, Y), (Z_FAR, Z_NEAR, Y)),
     ((Y, X, Z_NEAR, Z_FAR), (Z_FAR, Z_NEAR, Y)),
+    ((X, Y, Z_NEAR, Z_FAR), (Z_FAR, Z_NEAR, Y)),
+    ((Y, X, Z_NEAR, Z_FAR), (Z_FAR, Z_NEAR, Y)),
+    ((X, Y, Z_NEAR, Z_FAR), (Z_FAR, Z_NEAR, Y)),
     ((Z_NEAR, Z_FAR, X, Y), (Z_FAR, Z_NEAR, Y)),
-    ((X, Y, Z_NEAR, Z_FAR), (Z_FAR, Z_NEAR, Y)),
-    ((X, Y, Z_NEAR, Z_FAR), (Z_FAR, Z_NEAR, Y)),
-    ((X, Z_NEAR, Z_FAR, Y), (Z_FAR, Z_NEAR, Y)),
-    ((Y, Z_NEAR, Z_FAR, X), (Z_FAR, Z_NEAR, Y)),
     ((Y, X, Z_NEAR, Z_FAR), (Z_FAR, Z_NEAR, Y)),
     ((Y, X, Z_NEAR, Z_FAR), (Z_FAR, Z_NEAR, Y)),
     ((Y, X, Z_NEAR, Z_FAR), (Z_FAR, Z_NEAR, Y)),
+    ((X, Y, Z_NEAR, Z_FAR), (Y, Z_FAR, Z_NEAR)),
+    ((X, Z_NEAR, Z_FAR, Y), (Z_FAR, Z_NEAR, Y)),
+    ((Y, X, Z_NEAR, Z_FAR), (Z_FAR, Z_NEAR, Y)),
     ((X, Y, Z_NEAR, Z_FAR), (Z_FAR, Z_NEAR, Y)),
-    ((Y, X, Z_NEAR, Z_FAR), (Y, Z_FAR, Z_NEAR)),
-    ((X, Z_NEAR, Z_FAR, Y), (Z_FAR, Z_NEAR, Y)),
-    ((X, Z_NEAR, Z_FAR, Y), (Z_FAR, Z_NEAR, Y)),
 )
 SCHEDULE = {
-    (START, 0): ((BLOCK, 1), (BLOCK, 3),),
+    (START, 0): ((BLOCK, 2),),
+    (FFN, 3): ((BLOCK_ON, 2),),
+    (FFN, 10): ((A0, 0), (A2, 0),),
     (FFN, 11): ((A1, 0),),
-    (NORM, 0): ((A2, 0), (BLOCK_ON, 3),),
-    (OUT, 0): ((BLOCK_ON, 1),),
-    (HEAD, 1): ((B2, 0),),
-    (HEAD, 5): ((A1, 1), (B0, 0), (A2, 1),),
-    (HEAD, 6): ((A0, 0), (B2, 1),),
-    (HEAD, 9): ((A2, 2),),
-    (HEAD, 10): ((B0, 1),),
-    (SENT, 0): ((B1, 0), (B2, 2), (A2, 3),),
-    (MERGED, 0): ((B0, 2), (B1, 1), (A0, 1),),
-    (DLAYER, 0): ((B2, 3),),
-    (DLAYER, 1): ((A1, 2), (A2, 4),),
-    (DLAYER, 3): ((BLOCK, 2), (B0, 3),),
-    (LAYOUT, 0): ((C3, 0),),
-    (TABLE, 0): ((C0, 0), (C1, 0), (C5, 0), (A0, 2), (B1, 2), (A2, 5), (B2, 4),),
-    (TABLE, 2): ((C4, 0),),
-    (TABLE, 3): ((A1, 3),),
-    (TABLE, 4): ((B0, 4),),
-    (TABLE, 5): ((C2, 0), (C6, 0),),
-    (TABLE, 6): ((B1, 3), (B2, 5),),
-    (TABLE, 7): ((C3, 1), (A0, 3),),
-    (TABLE, 8): ((A1, 4), (BLOCK_ON, 2),),
-    (TABLE, 10): ((BLOCK, 0), (C5, 1),),
-    (TABLE, 11): ((C6, 1), (B0, 5),),
-    (TABLE, 15): ((A0, 4),),
+    (HEAD, 2): ((A2, 1), (B1, 0),),
+    (HEAD, 4): ((A0, 1), (B2, 0), (B0, 0), (A1, 1),),
+    (HEAD, 5): ((BLOCK, 0),),
+    (HEAD, 7): ((A0, 2),),
+    (HEAD, 9): ((B1, 1),),
+    (HEAD, 11): ((A0, 3), (B0, 1),),
+    (SENT, 0): ((B1, 2), (B2, 1),),
+    (MERGED, 0): ((A2, 2), (A1, 2), (A0, 4), (B0, 2), (B2, 2), (B1, 3), (BLOCK_ON, 0),),
+    (LAYOUT, 0): ((C0, 0), (A2, 3),),
+    (TABLE, 0): ((C1, 0), (C4, 0), (C2, 0), (C0, 1), (A0, 5), (B0, 3), (C3, 0), (B1, 4),),
+    (TABLE, 3): ((C5, 0), (A2, 4),),
+    (TABLE, 4): ((C4, 1), (B2, 3), (C6, 0), (C0, 2),),
+    (TABLE, 5): ((BLOCK, 1), (BLOCK, 3), (B0, 4),),
+    (TABLE, 7): ((B1, 5),),
+    (TABLE, 8): ((A1, 3),),
+    (TABLE, 12): ((A2, 5),),
+    (TABLE, 13): ((C6, 1),),
+    (TABLE, 14): ((C0, 3), (B2, 4),),
+    (TABLE, 15): ((B0, 5), (A1, 4), (C3, 1), (C6, 2), (C0, 4), (B2, 5), (INPUT_ON, 0),),
     (TAIL, 0): (
-        (A1, 5), (C3, 2), (A2, 6), (B1, 4), (B2, 6), (B0, 6), (C5, 2), (SMALL_STEP, 0), (C6, 2), (INPUT_ON, 0),
-        (A0, 5), (C3, 3), (A1, 6), (C5, 3), (C0, 1), (C6, 3), (B1, 5), (C3, 4), (C1, 1), (C5, 4), (C0, 2), (C4, 1),
-        (A0, 6), (C6, 4), (C3, 5), (C1, 2), (C2, 1), (C5, 5), (C0, 3), (B1, 6), (C4, 2), (C6, 5), (BLOCK_ON, 0),
-        (C3, 6), (C1, 3), (C2, 2), (SMALL_STEP, 1), (C0, 4), (C5, 6), (C4, 3), (C1, 4), (C6, 6), (LAY, 0), (C2, 3),
-        (SMALL_STEP, 2), (C0, 5), (C4, 4), (C1, 5), (C2, 4), (SMALL_STEP, 3), (C0, 6), (LAY_ON, 0), (C2, 5),
-        (C4, 5), (C1, 6), (SMALL_STEP, 4), (C2, 6), (C4, 6),
+        (C1, 1), (B1, 6), (A2, 6), (A0, 6), (C4, 2), (A1, 5), (C3, 2), (C2, 1), (SMALL_STEP, 0), (B0, 6), (C6, 3),
+        (C0, 5), (C5, 1), (C1, 2), (C3, 3), (C2, 2), (B2, 6), (C6, 4), (C4, 3), (C5, 2), (BLOCK_ON, 1), (C1, 3),
+        (C2, 3), (C6, 5), (C4, 4), (A1, 6), (C5, 3), (BLOCK_ON, 3), (C1, 4), (SMALL_STEP, 1), (C0, 6), (C3, 4),
+        (C2, 4), (C4, 5), (C5, 4), (C6, 6), (LAY, 0), (C1, 5), (SMALL_STEP, 2), (C2, 5), (C3, 5), (C4, 6), (C5, 5),
+        (SMALL_STEP, 3), (C1, 6), (LAY_ON, 0), (C3, 6), (C2, 6), (SMALL_STEP, 4), (C5, 6),
     ),
 }
 
@@ -1275,26 +1270,34 @@
 
 
 def finish_kernel(
-    rates, small_ref, block_in, in_in, red1, red2, red3, lay_in,
-    block_out, in_out, lay_out, qkv_out, qvb_out, table_out, wo_out, ob_out, g1_out, s1_out, w1_out, b1_out, w2_out, c2_out,
-    g2_out, s2_out, in_low, low1, low2, low3, lay_low, in_wide, wide1, wide2, wide3, lay_wide, block_low, load_sem, store_sem,
+    rates, small_ref, in_in, red1, red2, red3, lay_in,
+    in_out, lay_out, qkv_out, qvb_out, table_out, wo_out, ob_out, g1_out, s1_out, w1_out, b1_out, w2_out, c2_out,
+    g2_out, s2_out, in_low, low1, low2, low3, lay_low, in_wide, wide1, wide2, wide3, lay_wide, load_sem, store_sem,
 ):
     t = lax.axis_index("tensor")
     cols_t = HEADS_T * HD
     inverse = 1.0 / small_ref[6:7, 0:1]
-    order = [
-        (in_in, in_low, in_wide, in_out, None),
-        (red2, low2, wide2, w2_out, 4),
-        (red1, low1, wide1, w1_out, 3),
-        (red3, low3, wide3, None, None),
-        (lay_in, lay_low, lay_wide, lay_out, 6),
-    ]
-    loads = [pltpu.make_async_copy(src, low, load_sem.at[k]) for k, (src, low, _, _, _) in enumerate(order)]
-    for c in loads:
+    jobs = []
+
+    def job(src, low, wide, out, rate):
+        jobs.append((src, low, wide, out, rate))
+
+    def split(src, low, wide, out, rate, step):
+        for at in range(0, low.shape[0], step):
+            sl = pl.ds(at, step)
+            job(src.at[sl], low.at[sl], None if wide is None else wide.at[sl], out.at[sl], rate)
+
+    split(in_in, in_low, in_wide, in_out, None, 256)
+    split(red2, low2, wide2, w2_out, 4, 256)
+    split(red1, low1, wide1, w1_out, 3, 256)
+    for n, at, rate in ((2, 0, 0), (None, 1, 1), (0, 2, 0), (1, 3, 0)):
+        sl = pl.ds(at * cols_t, cols_t)
+        job(red3.at[sl], low3.at[sl], wide3.at[sl], wo_out if n is None else qkv_out.at[n], rate)
+    split(lay_in, lay_low, lay_wide, lay_out, 6, 256)
+    loads = [pltpu.make_async_copy(src, low, load_sem.at[k]) for k, (src, low, _, _, _) in enumerate(jobs)]
+    ahead = len(loads)
+    for c in loads[:ahead]:
         c.start()
-    whole_in = pltpu.make_async_copy(block_in, block_low, load_sem.at[5])
-    whole_in.start()
-    whole_out = pltpu.make_async_copy(block_low, block_out, store_sem.at[9])
 
     def row(ref, index, rate):
         ref[...] = (small_ref[index : index + 1, :] * (inverse * rates[rate])).reshape(ref.shape)
@@ -1310,34 +1313,17 @@
         table_out[a : a + 1, :] = own[:, at : at + 2 * BUCKETS] * (inverse * rates[7])
 
     stores = []
-
-    def store(k, src, dst):
-        stores.append(pltpu.make_async_copy(src, dst, store_sem.at[k]))
-
-    for k, (_, low, wide, out, rate) in enumerate(order):
+    for k, (_, low, wide, out, rate) in enumerate(jobs):
         loads[k].wait()
-        step = 128
-        if out is not None:
+        if k + ahead < len(jobs):
+            loads[k + ahead].start()
+        if wide is None:
+            stores.append(pltpu.make_async_copy(low, out, store_sem.at[k]))
+        else:
             factor = inverse if rate is None else inverse * rates[rate]
-
-            @pl.loop(0, low.shape[0] // step)
-            def _(i, low=low, wide=wide, out=out, factor=factor, k=k):
-                sl = pl.ds(pl.multiple_of(i * step, step), step)
-                wide[sl, :] = low[sl, :].astype(jnp.float32) * factor
-                pltpu.make_async_copy(wide.at[sl], out.at[sl], store_sem.at[k]).start()
-
-            store(k, wide, out)
-            if k == 0:
-                whole_in.wait()
-                whole_out.start()
-            continue
-        parts = ((2, 0, 0), (None, 1, 1), (0, 2, 0), (1, 3, 0))
-        for j, (n, at, rate) in enumerate(parts):
-            sl = pl.ds(at * cols_t, cols_t)
-            wide[sl, :] = low[sl, :].astype(jnp.float32) * (inverse * rates[rate])
-            store(5 + j, wide.at[sl], wo_out if n is None else qkv_out.at[n])
-            stores[-1].start()
-    whole_out.wait()
+            wide[...] = low[...].astype(jnp.float32) * factor
+            stores.append(pltpu.make_async_copy(wide, out, store_sem.at[k]))
+        stores[-1].start()
     for c in stores:
         c.wait()
 
@@ -1350,7 +1336,6 @@
     model = in_all.shape[1]
     vector = (shape((model,), f32), here)
     outs = [
-        (shape(block_all.shape, bf16), away),
         (shape(in_all.shape, f32), away),
         (shape(lay_all.shape, f32), away),
         (shape((3, cols_t, model), f32), away),
@@ -1366,15 +1351,15 @@
     wide = [in_all, sum1, sum2, sum3, lay_all]
     return pl.pallas_call(
         finish_kernel,
-        in_specs=[pl.BlockSpec(memory_space=pltpu.SMEM), here] + [away] * 6,
+        in_specs=[pl.BlockSpec(memory_space=pltpu.SMEM), here] + [away] * 5,
         out_specs=[spec for _, spec in outs],
         out_shape=[s for s, _ in outs],
         scratch_shapes=[pltpu.VMEM(v.shape, bf16) for v in wide]
         + [pltpu.VMEM(v.shape, f32) for v in wide]
-        + [pltpu.VMEM(block_all.shape, bf16), pltpu.SemaphoreType.DMA((6,)), pltpu.SemaphoreType.DMA((10,))],
+        + [pltpu.SemaphoreType.DMA((32,)), pltpu.SemaphoreType.DMA((32,))],
         compiler_params=pltpu.CompilerParams(vmem_limit_bytes=60 * 2**20),
         name="finish",
-    )(rates, small, block_all, in_all, sum1, sum2, sum3, lay_all)
+    )(rates, small, in_all, sum1, sum2, sum3, lay_all)
 
 
 def local(
@@ -1401,7 +1386,7 @@
         layer_low, features, qkvt, context_t, probs, rel_x, rel_y, w1, w2, wo, wqkv, block_own,
     )
     sums = [v.reshape(-1, v.shape[-1]) for v in (sum1, sum2, sum3, lay_all)]
-    out = list(finish(group_rates, small, block_all, in_all, *sums, out_weight.shape[0]))
+    out = [block_all] + list(finish(group_rates, small, block_all, in_all, *sums, out_weight.shape[0]))
     out[3] = jnp.transpose(out[3], (0, 2, 1))
     out[5] = out[5].T
     return tuple(out)

time: 189 us -> 186 us (0.984)
  Pallas kernels: 187 us -> 183 us
    pallas_call x1, Pallas kernels: 12.3 us -> 9.24 us  [finish(): pl.pallas_call(finish_kernel, in_specs=[pl.BlockSpec(memory_space=pltpu.S...]
where the time goes in v7:
time: 186 us
  Pallas kernels  183 us (98%)
    pallas_call x1, Pallas kernels, backward_window(): pl.pallas_call(functools.partial(backward_kernel, n_dp), in_specs=[here]...  117 us
    pallas_call x1, Pallas kernels, forward_window(): pl.pallas_call(forward_kernel, in_specs=[here] * len(small) + [away] * le...  56.6 us
    pallas_call x1, Pallas kernels, finish(): pl.pallas_call(finish_kernel, in_specs=[pl.BlockSpec(memory_space=pltpu.S...  9.24 us

profile of v7, /device:TPU:0, one launch (start us, length us, event | category | flops | bytes accessed | tf_op | source)
XLA Modules:
  0.0 185.7 jit_solution(10135849544198454918)
XLA Ops:
  0.7 56.6 %forward_window.1 = (f32[12,512,512]{2,1,0:T(8,128)}, bf16[3,768,512]{2,1,0:T(8,128)(2,1)}, bf16[768,512]{1,0:T(8,128)(2,1)}, bf16[512,768]{1,0:T(8,128)(2,1)}, ...) custom-call(s32[4,2048]{1,0:T(4,128)} %bitcast.15, ...), custom_call_target="tpu_custom_call" | custom-call | tf_op jit(solution)/shard_map/forward_window/pallas_call | solution.py:567
  57.3 117.5 %backward_window.1 = (bf16[2048,768]{1,0:T(8,128)(2,1)}, bf16[2048,768]{1,0:T(8,128)(2,1)}, bf16[6,2,2,2,16,768]{5,4,3,2,1,0:T(8,128)(2,1)}, bf16[6,2,2,2,16,768...) custom-call(f32[512,1]{1,0:T(8,128)} %get-tuple-element.55.inv_ref, ...), custom_call_target="tpu_custom_call" | custom-call | tf_op jit(solution)/shard_map/backward_window/pallas_call | solution.py:1245
  174.7 0.0 copy-start
  174.7 9.2 %finish.1 = (f32[2048,768]{1,0:T(8,128)}, f32[512,768]{1,0:T(8,128)}, f32[3,192,768]{2,1,0:T(8,128)}, f32[2,192]{1,0:T(2,128)}, f32[3,64]{1,0:T(4,128)}, /*index...) custom-call(f32[8]{0:T(128)} %rates.1, ...), custom_call_target="tpu_custom_call" | custom-call | tf_op jit(solution)/shard_map/finish/pallas_call | solution.py:1352
  184.0 0.0 copy-done
  184.0 1.7 copy.38
Async XLA Ops:
  174.7 9.3 %copy-start = (bf16[2048,768]{1,0:T(8,128)(2,1)S(1)}, bf16[2048,768]{1,0:T(8,128)(2,1)}, u32[]{:S(2)}) copy-start(bf16[2048,768]{1,0:T(8,128)(2,1)} %get-tuple-element.110) | copy-start | bytes 9437188

commit v8 on v7

--- a/solution.py
+++ b/solution.py
@@ -366,8 +366,8 @@
 
     def project(pieces):
         for n in range(3):
-            for r in pieces:
-                sl = pl.ds(r * cols_t, cols_t)
+            sl = pl.ds(pieces[0] * cols_t, len(pieces) * cols_t)
+            if True:
                 value = nt(wqkv[n, sl, :], low[...])
                 if n != 1:
                     value = value + cols[n, sl, :]
@@ -465,16 +465,14 @@
     for src, dst in ((w1, w1_out), (w2, w2_out)):
         leave(src.at[pl.ds(0, 2)], dst.at[pl.ds(0, 2)])
     for r in range(2):
-        @pl.loop(0, win // 256)
-        def _(i, r=r):
-            sl = pl.ds(pl.multiple_of(i * 256, 256), 256)
-            value = nn(nlow[sl, :], w1[r]) + rows[r, 0:1, :]
-            pre[r, sl, :] = value
-            low_hid = gelu(value).astype(bf16)
-            hid[r, sl, :] = low_hid
-            more = nn(low_hid, w2[r])
-            acc[sl, :] = more if r == 0 else acc[sl, :] + more
-            at_loop(F_UP, i, 2, 2 * r)
+        value = nn(nlow[...], w1[r]) + rows[r, 0:1, :]
+        pre[r] = value
+        low_hid = gelu(value).astype(bf16)
+        hid[r] = low_hid
+        more = nn(low_hid, w2[r])
+        acc[...] = more if r == 0 else acc[...] + more
+        for i in range(2):
+            at_slot(F_UP, 2 * r + i)
 
         leave(pre.at[r], pre_out.at[r])
         leave(hid.at[r], hid_out.at[r])
@@ -484,8 +482,7 @@
         far_pieces((U0 + 2 * k, D0 + 2 * k))
         units = pl.ds(k * third, third)
 
-        @pl.loop(2, 4)
-        def _(r, units=units):
+        for r in range(2, 4):
             value = nn(nlow[...], w1[r, :, units]) + rows[r, 0:1, units]
             pre[r, :, units] = value
             low_hid = gelu(value).astype(bf16)

time: 186 us -> 183 us (0.984)
  Pallas kernels: 183 us -> 180 us
    pallas_call x1, Pallas kernels: 56.6 us -> 53.7 us  [forward_window(): pl.pallas_call(forward_kernel, in_specs=[here] * len(small) + [away] * le...]
where the time goes in v8:
time: 183 us; the launch traced here: 182 us
  Pallas kernels  180 us (98%)
    pallas_call x1, Pallas kernels, backward_window(): pl.pallas_call(functools.partial(backward_kernel, n_dp), in_specs=[here]...  117 us
    pallas_call x1, Pallas kernels, forward_window(): pl.pallas_call(forward_kernel, in_specs=[here] * len(small) + [away] * le...  53.7 us
    pallas_call x1, Pallas kernels, finish(): pl.pallas_call(finish_kernel, in_specs=[pl.BlockSpec(memory_space=pltpu.S...  9.24 us

profile of v8, /device:TPU:0, one launch (start us, length us, event | category | flops | bytes accessed | tf_op | source)
XLA Modules:
  0.0 182.3 jit_solution(13591924262676144819)
XLA Ops:
  0.7 53.7 %forward_window.1 = (f32[12,512,512]{2,1,0:T(8,128)}, bf16[3,768,512]{2,1,0:T(8,128)(2,1)}, bf16[768,512]{1,0:T(8,128)(2,1)}, bf16[512,768]{1,0:T(8,128)(2,1)}, ...) custom-call(s32[4,2048]{1,0:T(4,128)} %bitcast.15, ...), custom_call_target="tpu_custom_call" | custom-call | tf_op jit(solution)/shard_map/forward_window/pallas_call | solution.py:564
  54.4 116.9 %backward_window.1 = (bf16[2048,768]{1,0:T(8,128)(2,1)}, bf16[2048,768]{1,0:T(8,128)(2,1)}, bf16[6,2,2,2,16,768]{5,4,3,2,1,0:T(8,128)(2,1)}, bf16[6,2,2,2,16,768...) custom-call(f32[512,1]{1,0:T(8,128)} %get-tuple-element.55.inv_ref, ...), custom_call_target="tpu_custom_call" | custom-call | tf_op jit(solution)/shard_map/backward_window/pallas_call | solution.py:1242
  171.3 0.0 copy-start
  171.4 9.2 %finish.1 = (f32[2048,768]{1,0:T(8,128)}, f32[512,768]{1,0:T(8,128)}, f32[3,192,768]{2,1,0:T(8,128)}, f32[2,192]{1,0:T(2,128)}, f32[3,64]{1,0:T(4,128)}, /*index...) custom-call(f32[8]{0:T(128)} %rates.1, ...), custom_call_target="tpu_custom_call" | custom-call | tf_op jit(solution)/shard_map/finish/pallas_call | solution.py:1349
  180.6 0.0 copy-done
  180.6 1.7 copy.38
Async XLA Ops:
  171.3 9.3 %copy-start = (bf16[2048,768]{1,0:T(8,128)(2,1)S(1)}, bf16[2048,768]{1,0:T(8,128)(2,1)}, u32[]{:S(2)}) copy-start(bf16[2048,768]{1,0:T(8,128)(2,1)} %get-tuple-element.110) | copy-start | bytes 9437188

commit v9 on v8

--- a/solution.py
+++ b/solution.py
@@ -20,33 +20,35 @@
 AT_R, AT_Q, AT_K, AT_V, AT_O, U0, D0, U1, D1, U2, D2 = range(11)
 WAYS = {
     AT_R: (1, 0),
-    AT_Q: (2, 0),
-    AT_K: (2, 0),
-    AT_V: (2, 1),
-    AT_O: (2, 0),
+    AT_Q: (2, 1),
+    AT_K: (2, 1),
+    AT_V: (2, 0),
+    AT_O: (2, 1),
     U0: (4, 0),
     D0: (4, 0),
     U1: (4, 0),
-    D1: (2, 1),
-    U2: (2, 0),
+    D1: (4, 0),
+    U2: (4, 0),
     D2: (1, 0),
 }
-SEND_ORDER = (AT_Q, AT_V, AT_K, D0, AT_R, U0, U1, AT_O, D1, U2, D2)
+SEND_ORDER = (AT_K, AT_V, AT_Q, U1, AT_R, D0, U0, AT_O, D1, U2, D2)
 FORWARD = {
-    (F_NEAR, 0): ((AT_Q, 0),),
+    (F_NEAR, 0): ((AT_K, 0),),
     (F_HEAD, 1): ((AT_V, 0),),
-    (F_HEAD, 2): ((AT_K, 0), (AT_Q, 1),),
-    (F_HEAD, 3): ((D0, 0),),
-    (F_HEAD, 4): ((AT_V, 1), (AT_R, 0), (U0, 0), (AT_K, 1),),
-    (F_HEAD, 5): ((U1, 0), (D0, 1),),
+    (F_HEAD, 2): ((AT_Q, 0),),
+    (F_HEAD, 3): ((AT_K, 1), (U1, 0),),
+    (F_HEAD, 4): ((AT_V, 1), (AT_R, 0), (AT_Q, 1), (D0, 0),),
+    (F_HEAD, 5): ((U0, 0), (U1, 1),),
     (F_HEAD, 6): ((AT_O, 0),),
-    (F_HEAD, 7): ((U0, 1),),
-    (F_HEAD, 9): ((U1, 1), (D0, 2), (D1, 0), (AT_O, 1),),
-    (F_HEAD, 10): ((U0, 2),),
-    (F_CONTEXT, 0): ((U2, 0),),
-    (F_NORM, 1): ((U1, 2),),
-    (F_NORM, 3): ((D1, 1),),
-    (F_UP, 2): ((U2, 1), (D2, 0),),
+    (F_HEAD, 7): ((D0, 1), (U0, 1), (D1, 0), (U1, 2),),
+    (F_HEAD, 8): ((U2, 0),),
+    (F_HEAD, 9): ((AT_O, 1),),
+    (F_HEAD, 10): ((D0, 2), (U0, 2),),
+    (F_CONTEXT, 0): ((D1, 1),),
+    (F_NORM, 1): ((U2, 1),),
+    (F_NORM, 2): ((D2, 0),),
+    (F_NORM, 3): ((D1, 2),),
+    (F_UP, 0): ((U2, 2),),
 }
 
 START, FFN, NORM, OUT, HEAD, SENT, MERGED, DLAYER, LAYOUT, TABLE, TAIL = range(11)

time: 183 us -> 185 us (1.011)
  Pallas kernels: 180 us -> 183 us
where the time goes in v9:
time: 185 us
  Pallas kernels  183 us (99%)
    pallas_call x1, Pallas kernels, backward_window(): pl.pallas_call(functools.partial(backward_kernel, n_dp), in_specs=[here]...  118 us
    pallas_call x1, Pallas kernels, forward_window(): pl.pallas_call(forward_kernel, in_specs=[here] * len(small) + [away] * le...  55.1 us
    pallas_call x1, Pallas kernels, finish(): pl.pallas_call(finish_kernel, in_specs=[pl.BlockSpec(memory_space=pltpu.S...  9.24 us

profile of v9, /device:TPU:0, one launch (start us, length us, event | category | flops | bytes accessed | tf_op | source)
XLA Modules:
  0.0 184.9 jit_solution(8264296570136497986)
XLA Ops:
  0.7 55.1 %forward_window.1 = (f32[12,512,512]{2,1,0:T(8,128)}, bf16[3,768,512]{2,1,0:T(8,128)(2,1)}, bf16[768,512]{1,0:T(8,128)(2,1)}, bf16[512,768]{1,0:T(8,128)(2,1)}, ...) custom-call(s32[4,2048]{1,0:T(4,128)} %bitcast.15, ...), custom_call_target="tpu_custom_call" | custom-call | tf_op jit(solution)/shard_map/forward_window/pallas_call | solution.py:566
  55.8 118.2 %backward_window.1 = (bf16[2048,768]{1,0:T(8,128)(2,1)}, bf16[2048,768]{1,0:T(8,128)(2,1)}, bf16[6,2,2,2,16,768]{5,4,3,2,1,0:T(8,128)(2,1)}, bf16[6,2,2,2,16,768...) custom-call(f32[512,1]{1,0:T(8,128)} %get-tuple-element.55.inv_ref, ...), custom_call_target="tpu_custom_call" | custom-call | tf_op jit(solution)/shard_map/backward_window/pallas_call | solution.py:1244
  174.0 0.0 copy-start
  174.0 9.2 %finish.1 = (f32[2048,768]{1,0:T(8,128)}, f32[512,768]{1,0:T(8,128)}, f32[3,192,768]{2,1,0:T(8,128)}, f32[2,192]{1,0:T(2,128)}, f32[3,64]{1,0:T(4,128)}, /*index...) custom-call(f32[8]{0:T(128)} %rates.1, ...), custom_call_target="tpu_custom_call" | custom-call | tf_op jit(solution)/shard_map/finish/pallas_call | solution.py:1351
  183.2 0.0 copy-done
  183.3 1.7 copy.38
Async XLA Ops:
  174.0 9.3 %copy-start = (bf16[2048,768]{1,0:T(8,128)(2,1)S(1)}, bf16[2048,768]{1,0:T(8,128)(2,1)}, u32[]{:S(2)}) copy-start(bf16[2048,768]{1,0:T(8,128)(2,1)} %get-tuple-element.110) | copy-start | bytes 9437188
